TPU v7x, 32 devices: a whole 2x2x4 slice. The times are simulated.
32 devices in a mesh: rep: 4 (over x, core), dp: 4 (over z), expert: 2 (over y).
Axes of the slice: x: 2, y: 2, z: 4, core: 2. Of those that a mesh axis runs over, the one named last changes fastest.
Arguments:
- tokens: bfloat16 [8192, 768], P(('rep', 'dp', 'expert')), may hold values from -6 to 6
- doc_ids: int32 [8192], P(('rep', 'dp', 'expert')), may hold values from 0 to 255, as said below
- routes: int32 [8192, 1], P(('rep', 'dp', 'expert')), may hold values from 0 to 1; in each aligned block of 256 rows (0 to 255, 256 to 511, ...) at most 256 rows name the same one
- cotangent: bfloat16 [8192, 768], P(('rep', 'dp', 'expert')), may hold values from -6 to 6
- attn_gain: bfloat16 [768], P(('dp', 'expert')), may hold values from 0.5 to 1.5
- w_query: bfloat16 [768, 768], P(('dp', 'expert')), may hold values from -0.02734375 to 0.02734375
- w_key: bfloat16 [768, 768], P(('dp', 'expert')), may hold values from -0.02734375 to 0.02734375
- w_value: bfloat16 [768, 768], P(('dp', 'expert')), may hold values from -0.21875 to 0.21875
- w_output: bfloat16 [768, 768], P(('dp', 'expert')), may hold values from -0.75 to 0.75
- rel_table: float32 [32, 12], replicated, may hold values from -4 to 4
- ffn_gain: bfloat16 [768], P(('dp', 'expert')), may hold values from 0.5 to 1.5
- w_router: bfloat16 [768, 2], P(('dp', 'expert')), may hold values from -0.21875 to 0.21875
- w_in: bfloat16 [2, 768, 3072], P('expert'), may hold values from -0.21875 to 0.21875
- w_out: bfloat16 [2, 3072, 768], P('expert'), may hold values from -0.21875 to 0.21875
Outputs:
- mixed: bfloat16 [8192, 768], P(('rep', 'dp', 'expert'))
- grad_tokens: float32 [8192, 768], P(('rep', 'dp', 'expert'))
- grad_attn_gain: float32 [768], P(('dp', 'expert'))
- grad_query: float32 [768, 768], P(('dp', 'expert'))
- grad_key: float32 [768, 768], P(('dp', 'expert'))
- grad_value: float32 [768, 768], P(('dp', 'expert'))
- grad_output: float32 [768, 768], P(('dp', 'expert'))
- grad_rel_table: float32 [32, 12], replicated
- grad_ffn_gain: float32 [768], P(('dp', 'expert'))
- grad_router: float32 [768, 2], P(('dp', 'expert'))
- grad_w_in: float32 [2, 768, 3072], P('expert', 'dp')
- grad_w_out: float32 [2, 3072, 768], P('expert', 'dp')
Inputs may be any that keep to these rules, and one draw needn't show every extreme that they name: `doc_ids`: along each device's 256 tokens the ids start at 0 and rise by 0 or 1 from token to token; equal ids mark one document. On some device all 256 tokens form one document, and on another every token is a document of its own. `routes`: among the 256 tokens of one device at most 256 name the same expert, and in every draw some expert is named by exactly 256 of them.
All inputs are finite; a program needn't handle non-finite values.
Results may differ from a plain program's by a relative error of at most 0.012.
Values may be sent and summed in bfloat16 or wider, within the bound.
No kernel may reach another device: no remote copies, remote signals or barrier semaphores. Data moves between devices by JAX's collectives and lax.ppermute only.
A program may use at most 128 MiB of HBM per device.

v0:
```python
import functools

import jax
import jax.numpy as jnp
from jax import lax
from jax.experimental import pallas as pl
from jax.experimental.pallas import tpu as pltpu
from jax.sharding import PartitionSpec as P

EPSILON = 1e-06
BUCKET_BOUNDS = (12, 16, 23, 32, 46, 64, 91)
INV_ROOT_TWO = 0.7071067811865476
INV_ROOT_TWO_PI = 0.3989422804014327
BF16 = jnp.bfloat16
F32 = jnp.float32


def bucket_of(offsets):
    distance = jnp.abs(offsets)
    levels = jnp.minimum(distance, 8)
    for threshold in BUCKET_BOUNDS:
        levels = levels + (distance >= threshold).astype(jnp.int32)
    return levels + 16 * (offsets > 0).astype(jnp.int32)


def bucket_onehot(tok_rows, bucket_count):
    window = 2 * tok_rows
    places = jnp.arange(window, dtype=jnp.int32)
    offsets = jnp.where(places < tok_rows, places, places - window)
    return (
        bucket_of(offsets)[:, None] == jnp.arange(bucket_count, dtype=jnp.int32)[None, :]
    ).astype(F32)


def rep_swap(values, bit):
    count = lax.axis_size("rep")
    return lax.ppermute(values, "rep", [(i, i ^ bit) for i in range(count)])


def shift(values, axis, step):
    count = lax.axis_size(axis)
    return lax.ppermute(values, axis, [(i, (i + step) % count) for i in range(count)])


def pick(values, index, axis):
    return lax.dynamic_index_in_dim(values, index, axis, keepdims=False)


def add_pair(one, two):
    return (one.astype(F32) + two.astype(F32)).astype(BF16)


def sum_over(values, axis, dimension):
    total = lax.psum_scatter(values.astype(F32), axis, scatter_dimension=dimension, tiled=False)
    return total.astype(BF16)


VMEM_BYTES = 32 * 1024 * 1024
BIG = 40
NT = (((1,), (1,)), ((), ()))
TN = (((0,), (0,)), ((), ()))


def mm(one, two):
    return jnp.dot(one, two, preferred_element_type=F32)


def mm_nt(one, two):
    return lax.dot_general(one, two, NT, preferred_element_type=F32)


def mm_tn(one, two):
    return lax.dot_general(one, two, TN, preferred_element_type=F32)


def estimate(us):
    return pl.CostEstimate(flops=us * 10**9 + 1, bytes_accessed=us * 10**6 + 1, transcendentals=0)


def whole_call(kernel, outs, scalars, arrays, scratch=(), us=2):
    vmem = pl.BlockSpec(memory_space=pltpu.VMEM)
    return pl.pallas_call(
        kernel,
        out_shape=[jax.ShapeDtypeStruct(s, d) for s, d in outs],
        in_specs=[pl.BlockSpec(memory_space=pltpu.SMEM)] * len(scalars) + [vmem] * len(arrays),
        out_specs=[vmem] * len(outs),
        scratch_shapes=list(scratch),
        cost_estimate=estimate(us),
        compiler_params=pltpu.CompilerParams(vmem_limit_bytes=VMEM_BYTES),
    )(*scalars, *arrays)


def bias_kernel(diag_ref, row_ref, col_ref, bias_ref):
    heads, tok, _ = bias_ref.shape
    window = diag_ref.shape[1]
    same = row_ref[...] == col_ref[...]
    for head in range(heads):
        wide = jnp.broadcast_to(diag_ref[head : head + 1, :], (tok, window))
        rolled = pltpu.roll(wide, 0, 1, stride=1, stride_axis=0)
        bias_ref[head] = jnp.where(same, rolled[:, :tok], -1e30)


def choose(place_ref, target, pieces):
    at = jnp.bitwise_xor(2 * place_ref[0] + place_ref[1], target)
    near = jnp.where(at % 2 == 0, pieces[0][...], pieces[1][...])
    far = jnp.where(at % 2 == 0, pieces[2][...], pieces[3][...])
    return jnp.where(at < 2, near, far)


def weight_halves(place_ref, index, pieces):
    return choose(place_ref, 2 * index, pieces), choose(place_ref, 2 * index + 1, pieces)


def project(values, halves):
    return jnp.concatenate([mm(values, halves[0]), mm(values, halves[1])], axis=1)


def project_back(turned, halves):
    half = turned.shape[0] // 2
    return mm(halves[0], turned[:half]) + mm(halves[1], turned[half:])


def low_lanes(tok, head_size):
    return lax.broadcasted_iota(jnp.int32, (tok, 2 * head_size), 1) < head_size


def scores_kernel(place_ref, tokens_ref, gain_ref, *refs):
    pieces = refs[:4]
    bias_ref, normed_ref, q_ref, k_ref, probs_ref = refs[4:]
    heads, tok, _ = bias_ref.shape
    size = tokens_ref.shape[1] // heads
    values = tokens_ref[...].astype(F32)
    factor = lax.rsqrt(jnp.mean(values * values, axis=-1, keepdims=True) + EPSILON)
    normed = (values * factor * gain_ref[...]).astype(BF16)
    normed_ref[...] = normed
    q_ref[...] = project(normed, weight_halves(place_ref, 0, pieces)).astype(BF16)
    k_ref[...] = project(normed, weight_halves(place_ref, 1, pieces)).astype(BF16)
    first = low_lanes(tok, size)
    for pair in range(heads // 2):
        lanes = slice(pair * 2 * size, (pair + 1) * 2 * size)
        queries, keys = q_ref[:, lanes], k_ref[:, lanes]
        for part in range(2):
            head = 2 * pair + part
            picked = jnp.where(first if part == 0 else ~first, queries, jnp.zeros_like(queries))
            scores = mm_nt(picked, keys) + bias_ref[head]
            exponent = jnp.exp(scores - jnp.max(scores, axis=-1, keepdims=True))
            probs = exponent / jnp.sum(exponent, axis=-1, keepdims=True)
            probs_ref[head] = probs.astype(BF16)


def attend_kernel(
    experts,
    place_ref,
    tokens_ref,
    normed_ref,
    gain_ref,
    router_ref,
    routes_ref,
    *refs,
):
    pieces = refs[:4]
    probs_ref, v_ref, attended_ref, residual_ref, normed_two_ref, gate_ref = refs[4:]
    heads, tok, _ = probs_ref.shape
    size = tokens_ref.shape[1] // heads
    v_ref[...] = project(normed_ref[...], weight_halves(place_ref, 0, pieces)).astype(BF16)
    first = low_lanes(tok, size)
    for pair in range(heads // 2):
        lanes = slice(pair * 2 * size, (pair + 1) * 2 * size)
        made = [mm(probs_ref[2 * pair + part], v_ref[:, lanes]) for part in range(2)]
        attended_ref[:, lanes] = jnp.where(first, made[0], made[1]).astype(BF16)
    halves = weight_halves(place_ref, 1, pieces)
    residual = tokens_ref[...].astype(F32) + project(attended_ref[...], halves)
    residual_ref[...] = residual
    factor = lax.rsqrt(jnp.mean(residual * residual, axis=-1, keepdims=True) + EPSILON)
    normed = (residual * factor * gain_ref[...]).astype(BF16)
    normed_two_ref[...] = normed
    probs = router_softmax(normed, router_ref[...], experts)
    lane = lax.broadcasted_iota(jnp.int32, probs.shape, 1)
    gate_ref[...] = jnp.sum(jnp.where(lane == routes_ref[...], probs, 0.0), axis=-1, keepdims=True)


def router_softmax(normed, router, experts):
    logits = mm(normed, router)
    lane = lax.broadcasted_iota(jnp.int32, logits.shape, 1)
    logits = jnp.where(lane < experts, logits, -1e30)
    exponent = jnp.exp(logits - jnp.max(logits, axis=-1, keepdims=True))
    return exponent / jnp.sum(exponent, axis=-1, keepdims=True)


def expert_kernel(
    experts,
    me_ref,
    rows_ref,
    cot_ref,
    router_ref,
    first_ref,
    second_ref,
    back_ref,
    hidden_ref,
    grad_pre_ref,
    produced_ref,
    grad_rows_ref,
    rows_turned_ref,
    cot_turned_ref,
    grad_logits_ref,
    made_ref,
    grad_ref,
    probs_ref,
):
    step, steps = pl.program_id(0), pl.num_programs(0)

    @pl.when(step == 0)
    def _():
        probs_ref[...] = router_softmax(rows_ref[...], router_ref[...], experts)
        rows_turned_ref[...] = rows_ref[...].T

    probs = probs_ref[...]
    chosen = lax.broadcasted_iota(jnp.int32, probs.shape, 1) == me_ref[0]
    gate = jnp.sum(jnp.where(chosen, probs, 0.0), axis=-1, keepdims=True)
    pre_act = mm(rows_ref[...], first_ref[0])
    cdf = 0.5 + 0.5 * lax.erf(pre_act * INV_ROOT_TWO)
    hidden = (pre_act * cdf).astype(BF16)
    slope = cdf + pre_act * jnp.exp(-0.5 * pre_act * pre_act) * INV_ROOT_TWO_PI
    grad_pre = (back_ref[...].astype(F32) * gate * slope).astype(BF16)
    hidden_ref[...] = hidden
    grad_pre_ref[...] = grad_pre
    made = mm(hidden, second_ref[0])
    grad = mm_nt(grad_pre, first_ref[0])

    @pl.when(step == 0)
    def _():
        made_ref[...] = made
        grad_ref[...] = grad

    @pl.when(step > 0)
    def _():
        made_ref[...] += made
        grad_ref[...] += grad

    @pl.when(step == steps - 1)
    def _():
        produced = made_ref[...].astype(BF16)
        produced_ref[...] = produced
        cot = cot_ref[...].astype(F32)
        grad_gate = jnp.sum(cot * produced.astype(F32), axis=-1, keepdims=True)
        grad_logits = (grad_gate * gate * (chosen.astype(F32) - probs)).astype(BF16)
        grad_logits_ref[...] = grad_logits
        grad_rows_ref[...] = (grad_ref[...] + mm_nt(grad_logits, router_ref[...])).astype(BF16)
        cot_turned_ref[...] = (cot * gate).astype(BF16).T


def run_expert(experts, me, rows, cot, router, w_in, w_out, slot_back, part):
    count, width = rows.shape
    inner = w_in.shape[2]
    tile = 512
    lanes = router.shape[1]
    const = lambda shape: pl.BlockSpec(shape, lambda j, s: (0, 0))
    wide = pl.BlockSpec((count, tile), lambda j, s: (0, j))
    return pl.pallas_call(
        functools.partial(expert_kernel, experts),
        out_shape=[
            jax.ShapeDtypeStruct((count, inner), BF16),
            jax.ShapeDtypeStruct((count, inner), BF16),
            jax.ShapeDtypeStruct((count, width), BF16),
            jax.ShapeDtypeStruct((count, width), BF16),
            jax.ShapeDtypeStruct((width, count), BF16),
            jax.ShapeDtypeStruct((width, count), BF16),
            jax.ShapeDtypeStruct((count, lanes), BF16),
        ],
        grid_spec=pltpu.PrefetchScalarGridSpec(
            num_scalar_prefetch=1,
            grid=(inner // tile,),
            in_specs=[
                const((count, width)),
                const((count, width)),
                const((width, lanes)),
                pl.BlockSpec((1, width, tile), lambda j, s: (0, 0, j)),
                pl.BlockSpec((1, tile, width), lambda j, s: (0, j, 0)),
                pl.BlockSpec((count, tile), lambda j, s: (part, j)),
            ],
            out_specs=[wide, wide]
            + [const((count, width))] * 2
            + [const((width, count))] * 2
            + [const((count, lanes))],
            scratch_shapes=[
                pltpu.VMEM((count, width), F32),
                pltpu.VMEM((count, width), F32),
                pltpu.VMEM((count, lanes), F32),
            ],
        ),
        cost_estimate=estimate(9),
        compiler_params=pltpu.CompilerParams(vmem_limit_bytes=VMEM_BYTES),
    )(me, rows, cot, router, w_in, w_out, slot_back)


def outer_kernel(keep, second, place_ref, left_a, left_b, right_a, right_b, *refs):
    total = mm(left_a[...], right_a[...]) + mm(left_b[...], right_b[...])
    if not keep:
        refs[0][0] = total.astype(BF16)
        return
    got, outs = refs[0], refs[1:]
    total = (total + got[0].astype(F32)).astype(BF16)
    step = pl.program_id(0)
    if second:
        half = total.shape[0] // 2
        high = place_ref[0]
        send = jnp.where(high == 0, total[half:], total[:half])
        kept = jnp.where(high == 0, total[:half], total[half:])
        for block in range(len(outs) - 2):

            @pl.when(step == block)
            def _():
                outs[block][0] = send[: half // 2]
                outs[block][1] = kept[: half // 2]

        outs[-2][0] = send[half // 2 :]
        outs[-1][0] = kept[half // 2 :]
        return
    blocks, rows, _ = outs[0].shape
    for part in range(2):

        @pl.when(step == part)
        def _():
            for block in range(blocks):
                at = lax.rem(block - place_ref[2] + blocks, blocks)
                start = 2 * block * rows
                outs[2 * part][at] = total[start : start + rows]
                outs[2 * part + 1][at] = total[start + rows : start + 2 * rows]


def outer_grad(second, place, left, right, blocks, got=None, us=0):
    keep = got is not None
    width, count = left[0].shape
    inner = right[0].shape[1]
    core = lambda s: s[1] if keep else 1 - s[1]
    whole = pl.BlockSpec((width, count), lambda i, s: (0, 0))
    fixed = lambda shape: pl.BlockSpec(shape, lambda i, s: (0,) * len(shape))
    if second:
        steps, columns = blocks, inner // (2 * blocks)
        wide = pl.BlockSpec((count, columns), lambda i, s: (0, 2 * lax.rem(i + s[2], blocks) + core(s)))
        quarter = pl.BlockSpec((1, width // 4, columns), lambda i, s: (i, 0, 0))
        shapes = [(2, width // 4, columns)] * blocks + [(blocks, width // 4, columns)] * 2
        out_specs = [fixed(shapes[0])] * blocks + [quarter] * 2
    else:
        steps, columns = 2, inner // 4
        wide = pl.BlockSpec(
            (count, columns), lambda i, s: (0, 2 * jnp.where(i == 0, 1 - s[0], s[0]) + core(s))
        )
        shapes = [(blocks, width // (2 * blocks), columns)] * 4
        out_specs = [fixed(shapes[0])] * 4
    got_spec = pl.BlockSpec((1, width, columns), lambda i, s: (i, 0, 0))
    if not keep:
        out_specs, shapes = [got_spec], [(steps, width, columns)]
    return pl.pallas_call(
        functools.partial(outer_kernel, keep, second),
        out_shape=[jax.ShapeDtypeStruct(s, BF16) for s in shapes],
        grid_spec=pltpu.PrefetchScalarGridSpec(
            num_scalar_prefetch=1,
            grid=(steps,),
            in_specs=[whole, whole, wide, wide] + ([got_spec] if keep else []),
            out_specs=out_specs,
        ),
        cost_estimate=estimate(us),
        compiler_params=pltpu.CompilerParams(vmem_limit_bytes=VMEM_BYTES),
    )(place, *left, *right, *([got] if keep else []))


def add_kernel(count, *refs):
    ins, outs = refs[: len(refs) - count], refs[len(refs) - count :]
    for index, out in enumerate(outs):
        total = 0.0
        for ref in ins:
            total = total + (ref[index] if count > 1 else ref[...]).astype(F32)
        out[...] = total.astype(BF16)


def add_arrays(arrays, count=1, us=0):
    shape = arrays[0].shape[1:] if count > 1 else arrays[0].shape
    outs = whole_call(functools.partial(add_kernel, count), [(shape, BF16)] * count, [], arrays, us=us)
    return outs if count > 1 else outs[0]


def core_add_kernel(place_ref, keep_ref, got_ref, send_low, send_high, keep_low, keep_high):
    blocks, rows = send_low.shape[1], send_low.shape[2]
    me = place_ref[3]
    for matrix in range(2):
        for block in range(blocks):
            at = lax.rem(block - place_ref[2] + blocks, blocks)
            start = 4 * block * rows
            total = keep_ref[matrix, start : start + 4 * rows].astype(F32)
            total = (total + got_ref[matrix, start : start + 4 * rows].astype(F32)).astype(BF16)
            one, two = total[: 2 * rows], total[2 * rows :]
            mine, other = jnp.where(me == 0, one, two), jnp.where(me == 0, two, one)
            send_low[matrix, at] = other[:rows]
            send_high[matrix, at] = other[rows:]
            keep_low[matrix, at] = mine[:rows]
            keep_high[matrix, at] = mine[rows:]


def pair_add_kernel(place_ref, keep_ref, got_ref, send_ref, mine_ref):
    high = place_ref[0]
    send_ref[...] = (keep_ref[1 - high].astype(F32) + got_ref[1 - high].astype(F32)).astype(BF16)
    mine_ref[...] = (keep_ref[high].astype(F32) + got_ref[high].astype(F32)).astype(BF16)


def lay_rows_kernel(rows, place_ref, own_ref, got_ref, out_ref, *rest):
    blocks = own_ref.shape[0]
    me = place_ref[3]
    for block in range(blocks):
        at = lax.rem(place_ref[2] - block + blocks, blocks)
        own, got = own_ref[at], got_ref[at]
        both = (jnp.where(me == 0, own, got), jnp.where(me == 0, got, own))
        for index in range(2):
            start = (2 * block + index) * rows
            out_ref[start : start + rows, :] = both[index][:rows]
            for ref in rest:
                ref[2 * block + index] = both[index][rows:, : ref.shape[2]]


def attend_back_kernel(
    place_ref,
    mask_ref,
    own_ref,
    got_ref,
    residual_ref,
    cot_ref,
    gain_ref,
    attended_ref,
    *refs,
):
    pieces = refs[:4]
    q_ref, k_ref, v_ref, probs_ref, normed_ref, send_ref, keep_ref, ds_ref, gq_ref, gk_ref, gv_ref = refs[4:15]
    grad_res_ref, gain_grad_ref, ga_ref, gat_ref, qt_ref, kt_ref = refs[15:]
    heads, tok, _ = probs_ref.shape
    size = residual_ref.shape[1] // heads
    low = place_ref[1]

    def store(index, grad):
        grad = grad.astype(BF16)

        @pl.when(low == index % 2)
        def _():
            keep_ref[index // 2] = grad

        @pl.when(low != index % 2)
        def _():
            send_ref[index // 2] = grad

    grad_two = jnp.where(mask_ref[...] > 0, own_ref[...], got_ref[...]).astype(F32)
    residual = residual_ref[...]
    factor = lax.rsqrt(jnp.mean(residual * residual, axis=-1, keepdims=True) + EPSILON)
    scaled = grad_two * gain_ref[...]
    inner = jnp.mean(scaled * residual, axis=-1, keepdims=True)
    grad_res = cot_ref[...].astype(F32) + factor * scaled - residual * (factor * factor * factor) * inner
    grad_res_ref[...] = grad_res
    gain_grad_ref[...] = jnp.sum(grad_two * residual * factor, axis=0, keepdims=True)
    grad_attn = grad_res.astype(BF16)
    store(3, mm(attended_ref[...].T, grad_attn))
    left, right = weight_halves(place_ref, 1, pieces)
    half = left.shape[1]
    ga_ref[...] = (mm_nt(grad_attn[:, :half], left) + mm_nt(grad_attn[:, half:], right)).astype(BF16)
    gat_ref[...] = (mm_nt(left, grad_attn[:, :half]) + mm_nt(right, grad_attn[:, half:])).astype(BF16)
    qt_ref[...] = q_ref[...].T
    kt_ref[...] = k_ref[...].T
    first = low_lanes(tok, size)
    for head in range(heads):
        lanes = slice(head // 2 * 2 * size, (head // 2 + 1) * 2 * size)
        rows = slice(head * size, (head + 1) * size)
        grads = ga_ref[:, lanes]
        picked = jnp.where(first if head % 2 == 0 else ~first, grads, jnp.zeros_like(grads))
        grad_probs = mm_nt(picked, v_ref[:, lanes])
        probs = probs_ref[head]
        wide = probs.astype(F32)
        total = jnp.sum(wide * grad_probs, axis=-1, keepdims=True)
        ds = (wide * (grad_probs - total)).astype(BF16)
        ds_ref[head] = ds
        gq_ref[rows, :] = mm_nt(kt_ref[rows, :], ds).astype(BF16)
        gk_ref[rows, :] = mm(qt_ref[rows, :], ds).astype(BF16)
        gv_ref[rows, :] = mm(gat_ref[rows, :], probs).astype(BF16)
    turned = normed_ref[...].T
    store(0, mm_nt(turned, gq_ref[...]))
    store(1, mm_nt(turned, gk_ref[...]))
    store(2, mm_nt(turned, gv_ref[...]))


def finish_kernel(
    place_ref,
    tokens_ref,
    gain_ref,
    *refs,
):
    qk_pieces, vo_pieces = refs[:4], refs[4:8]
    gq_ref, gk_ref, gv_ref, ds_ref, grad_res_ref, grad_tokens_ref, gain_grad_ref, diag_ref = refs[8:]
    heads, tok, _ = ds_ref.shape
    window = diag_ref.shape[1]
    grad = project_back(gq_ref[...], weight_halves(place_ref, 0, qk_pieces))
    grad = grad + project_back(gk_ref[...], weight_halves(place_ref, 1, qk_pieces))
    grad = grad + project_back(gv_ref[...], weight_halves(place_ref, 0, vo_pieces))
    grad = grad.T
    values = tokens_ref[...].astype(F32)
    factor = lax.rsqrt(jnp.mean(values * values, axis=-1, keepdims=True) + EPSILON)
    scaled = grad * gain_ref[...]
    inner = jnp.mean(scaled * values, axis=-1, keepdims=True)
    grad_tokens_ref[...] = grad_res_ref[...] + factor * scaled - values * (factor * factor * factor) * inner
    gain_grad_ref[...] = jnp.sum(grad * values * factor, axis=0, keepdims=True)
    row = lax.broadcasted_iota(jnp.int32, (tok, tok), 0)
    column = lax.broadcasted_iota(jnp.int32, (tok, tok), 1)
    turned = (row + column == tok - 1).astype(BF16)
    for head in range(heads):
        flipped = mm(turned, ds_ref[head])
        wide = jnp.concatenate([flipped, jnp.zeros((tok, window - tok), F32)], axis=1)
        rolled = pltpu.roll(wide, window - tok + 1, 1, stride=1, stride_axis=0)
        diag_ref[head : head + 1, :] = jnp.sum(rolled, axis=0, keepdims=True)


def second_shared_kernel(place_ref, *refs):
    pieces, out = refs[:4], refs[4]
    rows, columns = pieces[0].shape
    for target in range(4):
        x, core = target // 2, target % 2
        out[0, core * rows : (core + 1) * rows, x * columns : (x + 1) * columns] = choose(place_ref, target, pieces).astype(F32)


def first_shared_kernel(place_ref, *refs):
    pieces, out = refs[:4], refs[4]
    columns = pieces[0].shape[1]
    for target in range(4):
        out[0, :, target * columns : (target + 1) * columns] = choose(place_ref, target, pieces).astype(F32)


def attention_shared_kernel(place_ref, *refs):
    for target in range(4):
        refs[4 + target][...] = choose(place_ref, target, refs[:4]).astype(F32)


def spread(values, *others):
    far = rep_swap(values, 2)
    if others:
        far = after(far, *others)
    return [values, rep_swap(values, 1), far, rep_swap(far, 1)]


def after(values, *others):
    return lax.optimization_barrier((values,) + others)[0]


def local(
    tokens,
    doc_ids,
    routes,
    cotangent,
    attn_gain,
    w_query,
    w_key,
    w_value,
    w_output,
    rel_table,
    ffn_gain,
    w_router,
    w_in,
    w_out,
):
    tok_rows, width = tokens.shape
    head_count = rel_table.shape[1]
    experts = w_router.shape[1]
    dp_count = lax.axis_size("dp")
    expert_axis = lax.axis_size("expert")
    capacity = 2 * tok_rows // expert_axis
    inner = w_in.shape[2]
    rep = lax.axis_index("rep")
    high, low = rep // 2, rep % 2
    me = lax.axis_index("expert")
    dp = lax.axis_index("dp")
    place = jnp.stack([high, low, dp, me]).astype(jnp.int32)
    shard_rows = w_query.shape[0]
    lanes = 128
    slots = experts * capacity

    onehot = bucket_onehot(tok_rows, rel_table.shape[0])
    diag_values = jnp.dot(onehot, rel_table, precision=lax.Precision.HIGHEST).T
    square = (head_count, tok_rows, tok_rows)
    (bias,) = whole_call(
        bias_kernel, [(square, F32)], [], [diag_values, doc_ids[None, :], doc_ids[:, None]], us=2
    )

    half = width // 2
    small = jnp.concatenate([attn_gain[None], ffn_gain[None], w_router.T], axis=0)
    small_rows = -(-(2 + experts) // 16) * 16
    small = jnp.pad(small, ((0, small_rows - 2 - experts), (0, half - shard_rows)))

    def quarter(one, two):
        return lax.dynamic_slice_in_dim(jnp.where(high == 0, one, two), low * half, half, 1)

    qk_quarter = jnp.concatenate([quarter(w_query, w_key), small], axis=0)
    vo_quarter = quarter(w_value, w_output)
    if expert_axis == 2:

        def along_dp(values):
            return jnp.stack([values] + [shift(values, "dp", step) for step in range(1, dp_count)])

        qk_own, vo_own = along_dp(qk_quarter), along_dp(vo_quarter)
        qk_own = after(qk_own, bias)
        qk_got = shift(qk_own, "expert", 1)
        vo_got = shift(vo_own, "expert", 1)
        rest_shape = (dp_count * expert_axis, small_rows, lanes)
        qk_mine, rest = whole_call(
            functools.partial(lay_rows_kernel, shard_rows),
            [((width, half), BF16), (rest_shape, BF16)],
            [place],
            [qk_own, qk_got],
            us=1,
        )
        (vo_mine,) = whole_call(
            functools.partial(lay_rows_kernel, shard_rows), [((width, half), BF16)], [place], [vo_own, vo_got], us=1
        )
    else:
        rows_all = lax.all_gather(qk_quarter, ("dp", "expert"), axis=0)
        qk_mine, rest = rows_all[:, :shard_rows].reshape(width, half), rows_all[:, shard_rows:]
        vo_mine = lax.all_gather(vo_quarter, ("dp", "expert"), axis=0, tiled=True)
    rest = jnp.moveaxis(rest[:, : 2 + experts, :shard_rows], 1, 0).reshape(2 + experts, width)
    gain_one = rest[0:1].astype(F32)
    gain_two = rest[1:2].astype(F32)
    router = jnp.pad(rest[2:].T, ((0, 0), (0, lanes - experts)))
    qk_pieces = spread(qk_mine)

    route_ids = routes[:, 0]
    direct = expert_axis == 2 and capacity == tok_rows
    if direct:
        own_mask = (routes == me).astype(F32)

        def send(values):
            return values, shift(values, "expert", 1)

        def back(one, two):
            return one, shift(two, "expert", 1)

        zero = jnp.zeros_like(cotangent)
        cot_a = jnp.where(routes == me, cotangent, zero)
        cot_b = shift(after(jnp.where(routes == me, zero, cotangent), vo_got), "expert", 1)
    else:
        own_mask = jnp.ones((tok_rows, 1), F32)
        chosen = (route_ids[:, None] == jnp.arange(experts, dtype=jnp.int32)[None, :]).astype(jnp.int32)
        slot_rank = jnp.sum(jnp.cumsum(chosen, axis=0) * chosen, axis=-1) - 1
        slot_index = route_ids * capacity + slot_rank
        place_of = (jnp.arange(slots, dtype=jnp.int32)[:, None] == slot_index[None, :]).astype(BF16)

        def send(values):
            filled = mm(place_of, values).astype(BF16)
            filled = lax.all_to_all(filled, "expert", split_axis=0, concat_axis=0, tiled=True)
            return filled[: slots // 2], filled[slots // 2 :]

        def back(one, two):
            rows = jnp.concatenate([one, two], axis=0)
            rows = lax.all_to_all(rows, "expert", split_axis=0, concat_axis=0, tiled=True)
            rows = mm_tn(place_of, rows).astype(BF16)
            return rows, rows

        cot_a, cot_b = send(cotangent)

    slot_back = mm_nt(jnp.concatenate([cot_a, cot_b], axis=0), w_out[0]).astype(BF16)

    flat = (tok_rows, width)
    normed_one, queries, keys, probs = whole_call(
        scores_kernel,
        [(flat, BF16)] * 3 + [(square, BF16)],
        [place],
        [tokens, gain_one, *qk_pieces, bias],
        us=4,
    )
    vo_pieces = spread(vo_mine, slot_back, normed_one)
    values, attended, residual, normed_two, gate = whole_call(
        functools.partial(attend_kernel, experts),
        [(flat, BF16), (flat, BF16), (flat, F32), (flat, BF16), ((tok_rows, 1), F32)],
        [place],
        [tokens, normed_one, gain_two, router, routes, *vo_pieces, probs],
        us=4,
    )

    rows_a, rows_b = send(normed_two)
    where_me = me[None].astype(jnp.int32)
    run = functools.partial(run_expert, experts, where_me)
    hid_a, pre_a, made_a, grad_a, turn_a, cot_turn_a, logits_a = run(
        rows_a, cot_a, router, w_in, w_out, slot_back, 0
    )
    hid_b, pre_b, made_b, grad_b, turn_b, cot_turn_b, logits_b = run(
        rows_b, cot_b, router, w_in, w_out, slot_back, 1
    )
    grad_own, grad_got = back(grad_a, grad_b)

    hid, pre, rows, cots = (hid_a, hid_b), (pre_a, pre_b), (turn_a, turn_b), (cot_turn_a, cot_turn_b)
    (second_out,) = outer_grad(True, place, cots, hid, dp_count, us=BIG)
    second_in = rep_swap(second_out, 1)
    (first_out,) = outer_grad(False, place, rows, pre, dp_count)
    first_in = rep_swap(first_out, 1)
    *early, second_send, second_keep = outer_grad(True, place, cots, hid, dp_count, second_in)
    first_in = after(first_in, grad_got, second_send)
    first_send, first_late, first_keep, first_last = outer_grad(False, place, rows, pre, dp_count, first_in, us=BIG)
    grad_got = after(grad_got, second_send, first_send)

    def z_sent(blocks):
        return [blocks[0]] + [shift(blocks[step], "dp", step) for step in range(1, dp_count)]

    early = z_sent(early)
    second_got = rep_swap(second_send, 2)

    square_weight = (2, width, width)
    send_part, keep_part, grad_scores, grad_q, grad_k, grad_v, grad_res, grad_gain_two = whole_call(
        attend_back_kernel,
        [(square_weight, BF16)] * 2
        + [(square, BF16)]
        + [((width, tok_rows), BF16)] * 3
        + [(flat, F32), ((1, width), F32)],
        [place],
        [own_mask, grad_own, grad_got, residual, cotangent, gain_two, attended]
        + [*vo_pieces, queries, keys, values, probs, normed_one],
        scratch=[pltpu.VMEM(flat, BF16)] + [pltpu.VMEM((width, tok_rows), BF16)] * 3,
        us=0,
    )
    core_got = rep_swap(send_part, 1)

    second_blocks = list(add_arrays([after(second_keep, grad_res), second_got], dp_count))
    first_got = rep_swap(after(first_send, second_got), 2)

    grad_tokens, grad_gain_one, diag_grads = whole_call(
        finish_kernel,
        [(flat, F32), ((1, width), F32), ((head_count, 2 * tok_rows), F32)],
        [place],
        [tokens, gain_one, *qk_pieces, *vo_pieces, grad_q, grad_k, grad_v, grad_scores]
        + [after(grad_res, second_blocks[0])],
        us=0,
    )

    early_sum = add_arrays([after(early[0], grad_tokens)] + early[1:], us=BIG)
    early_got = rep_swap(early_sum[0], 2)
    second_blocks[0] = after(second_blocks[0], early_sum)
    second_z = z_sent([second_blocks[0]] + [after(block, early_sum) for block in second_blocks[1:]])

    keep_part = after(keep_part, early_sum)
    if expert_axis == 2:
        rows_half = shard_rows // 2
        chunk_shape = (2, dp_count, rows_half, width)
        send_low, send_high, keep_low, keep_high = whole_call(
            core_add_kernel, [(chunk_shape, BF16)] * 4, [place], [keep_part, core_got], us=2
        )
        low_got = shift(send_low, "expert", 1)
        token = send_low
    else:
        part = add_pair(keep_part, core_got).reshape(2, dp_count, expert_axis, shard_rows, width)
        part = sum_over(part, "expert", 2)
        token = part

    first_blocks = add_arrays([after(first_keep, token), first_got], dp_count)
    first_z = z_sent(first_blocks)
    late_got = rep_swap(after(first_late, first_got), 2)

    if expert_axis == 2:
        pair_shape = [(chunk_shape[1:], BF16)] * 2
        x_send, x_low = whole_call(
            pair_add_kernel, pair_shape, [place], [after(keep_low, first_blocks[0]), low_got], us=1
        )
        high_got = shift(after(send_high, low_got), "expert", 1)
        x_low_got = rep_swap(x_send, 2)
        token = x_low

    late_blocks = add_arrays([after(first_last, token), late_got], dp_count)
    late_z = z_sent(late_blocks)

    second_low = add_arrays([after(second_z[0], late_blocks[0])] + second_z[1:])
    second_high = add_arrays([after(early_sum[1], second_low), early_got])
    second_pieces = spread(jnp.concatenate([second_high, second_low], axis=0).T)

    if expert_axis == 2:
        low_blocks = add_arrays([after(x_low, second_pieces[0]), x_low_got], dp_count)
        low_z = z_sent(low_blocks)
        x_send, x_high = whole_call(
            pair_add_kernel, pair_shape, [place], [after(keep_high, low_blocks[0]), high_got], us=1
        )
        x_high_got = rep_swap(x_send, 2)
        first_low = add_arrays([after(first_z[0], x_high)] + first_z[1:])
        high_blocks = add_arrays([after(x_high, first_low), x_high_got], dp_count)
        high_z = z_sent(high_blocks)
        token = x_high
        first_high = add_arrays([after(late_z[0], high_blocks[0])] + late_z[1:])
        first_pieces = spread(jnp.concatenate([first_low, first_high], axis=0))
        attn_low = add_arrays([after(low_z[0], first_pieces[0])] + low_z[1:])
        attn_high = add_arrays([after(high_z[0], attn_low)] + high_z[1:])
        attn_pieces = spread(jnp.concatenate([attn_low, attn_high], axis=0))
    else:
        first_low = add_arrays([first_z[0]] + first_z[1:])
        first_high = add_arrays([late_z[0]] + late_z[1:])
        first_pieces = spread(jnp.concatenate([first_low, first_high], axis=0))
        x_part = add_pair(pick(part, high, 0), rep_swap(pick(part, 1 - high, 0), 2))
        attn_pieces = spread(sum_over(x_part, "dp", 0))
        token = x_part
    (grad_w_out,) = whole_call(
        second_shared_kernel, [((1, inner // dp_count, width), F32)], [place], second_pieces
    )
    (grad_w_in,) = whole_call(first_shared_kernel, [((1, width // dp_count, inner), F32)], [place], first_pieces)
    owned = whole_call(attention_shared_kernel, [((shard_rows, width), F32)] * 4, [place], attn_pieces)

    made_own, made_got = back(made_a, after(made_b, token))
    expert_rows = jnp.where(own_mask > 0, made_own, made_got).astype(F32)
    mixed = (residual + gate * expert_rows).astype(BF16)
    grad_router = mm(turn_a, logits_a) + mm(turn_b, logits_b)
    grad_router = grad_router[:, :experts]
    grad_table = jnp.dot(onehot.T, diag_grads.T, precision=lax.Precision.HIGHEST)
    small = jnp.concatenate([grad_gain_one, grad_gain_two, grad_router.T], axis=0)
    packed = jnp.concatenate([small.reshape(-1), grad_table.reshape(-1)])
    packed = all_sum(packed, (early_sum, first_blocks[0], late_blocks[0]))
    row_start = (dp * expert_axis + me) * shard_rows
    small = packed[: (2 + experts) * width].reshape(2 + experts, width)
    small = lax.dynamic_slice_in_dim(small, row_start, shard_rows, 1)
    table_total = packed[(2 + experts) * width :].reshape(rel_table.shape)
    return (
        mixed,
        grad_tokens,
        small[0],
        owned[0],
        owned[1],
        owned[2],
        owned[3],
        table_total,
        small[1],
        small[2:].T,
        grad_w_in,
        grad_w_out,
    )


def all_sum(values, tokens):
    for axis, token in zip(("rep", "expert", "dp"), tokens, strict=True):
        count = lax.axis_size(axis)
        if count > 4:
            values = lax.psum(values, axis)
            continue
        total = values = after(values, token)
        for step in range(1, count):
            total = total + shift(values, axis, step)
        values = total
    return values


def solution(mesh):
    rows = P(("rep", "dp", "expert"), None)
    split = P(("dp", "expert"), None)
    vector = P(("dp", "expert"))
    return jax.shard_map(
        local,
        mesh=mesh,
        in_specs=(
            rows,
            P(("rep", "dp", "expert")),
            rows,
            rows,
            vector,
            split,
            split,
            split,
            split,
            P(),
            vector,
            split,
            P("expert", None, None),
            P("expert", None, None),
        ),
        out_specs=(
            rows,
            rows,
            vector,
            split,
            split,
            split,
            split,
            P(),
            vector,
            split,
            P("expert", "dp", None),
            P("expert", "dp", None),
        ),
        check_vma=False,
    )
```

profile of v0, /device:TPU:0, one launch (start us, length us, event | category | flops | bytes accessed | tf_op | source)
XLA Modules:
  0.0 260.8 jit_solution(12435044170716965463)
XLA Ops:
  2.4 5.1 %collective-permute-start.2 = (bf16[112,384]{1,0:T(8,128)(2,1)S(1)}, bf16[112,384]{1,0:T(8,128)(2,1)S(1)}, u32[]{:S(2)}, u32[]{:S(2)}) collective-permute-start(bf16[112,384]{1,0:T(8,128)(2,1)S(1)} %get-tuple-element.255), channel_id=1, source_target_pairs={{0,6},{2,0},{4,2},{6,4},{1,7},{3,1},{5,3},{7,5},{8,14},{10,8},{12,... | collective-permute-start | bytes 258056 | tf_op jit(solution)/shard_map/ppermute | solution.py:42
  9.4 2.9 %collective-permute-start.9 = (bf16[96,384]{1,0:T(8,128)(2,1)S(1)}, bf16[96,384]{1,0:T(8,128)(2,1)S(1)}, u32[]{:S(2)}, u32[]{:S(2)}) collective-permute-start(bf16[96,384]{1,0:T(8,128)(2,1)S(1)} %dynamic-slice_select_fusion), channel_id=1, source_target_pairs={{0,6},{2,0},{4,2},{6,4},{1,7},{3,1},{5,3},{7,5},{8,14},{10,8},{12,... | collective-permute-start | bytes 221192 | tf_op jit(solution)/shard_map/ppermute | solution.py:42
  17.7 1.7 copy-done.60
  19.5 1.6 collective-permute-start.3
  21.8 3.7 %collective-permute-done.7 = bf16[96,384]{1,0:T(8,128)(2,1)S(1)} collective-permute-done((bf16[96,384]{1,0:T(8,128)(2,1)S(1)}, bf16[96,384]{1,0:T(8,128)(2,1)S(1)}, u32[]{:S(2)}, u32[]{:S(2)}) %collective-permute-start.7) | collective-permute-done | bytes 73760 | tf_op jit(solution)/shard_map/ppermute | solution.py:42
  25.6 1.6 collective-permute-start.10
  27.2 3.1 %collective-permute-done.3.got_ref = bf16[4,112,384]{2,1,0:T(8,128)(2,1)S(1)} collective-permute-done((bf16[4,112,384]{2,1,0:T(8,128)(2,1)S(1)}, bf16[4,112,384]{2,1,0:T(8,128)(2,1)S(1)}, u32[]{:S(2)}, u32[]{:S(2)}) %collective-permute-start.3) | collective-permute-done | bytes 344096 | tf_op jit(solution)/shard_map/ppermute | solution.py:42
  38.3 4.8 %collective-permute-done.5.refs_2_ = bf16[768,384]{1,0:T(8,128)(2,1)S(1)} collective-permute-done((bf16[768,384]{1,0:T(8,128)(2,1)S(1)}, bf16[768,384]{1,0:T(8,128)(2,1)S(1)}, u32[]{:S(2)}, u32[]{:S(2)}) %collective-permute-start.5) | collective-permute-done | bytes 589856 | tf_op jit(solution)/shard_map/ppermute | solution.py:37
  43.4 7.0 %fusion.2.back_ref = bf16[512,3072]{1,0:T(8,128)(2,1)} fusion(bf16[1,3072,768]{2,1,0:T(8,128)(2,1)} %second_ref.3, bf16[256,768]{1,0:T(8,128)(2,1)} %collective-permute-done.13.cot_ref, bf16[256,768]{1,0:T(8,128)(2,1)} %get-tuple-element.250.cot_ref), kind=kOutput, calls=%fused_computation.2 | convolution fusion | flops 2419064832 | bytes 8650752 | tf_op jit(solution)/shard_map/dot_general | solution.py:69
  50.5 3.7 %shard_map.231 = (bf16[256,768]{1,0:T(8,128)(2,1)S(1)}, bf16[256,768]{1,0:T(8,128)(2,1)S(1)}, bf16[256,768]{1,0:T(8,128)(2,1)S(1)}, bf16[12,256,256]{2,1,0:T(8,128)(2,1)S(1)}) custom-call(s32[4]{0:T(128)S(1)} %pad_add_fusion.place_ref, bf16[256,768]{1,0:T(8,128)(2,1)S(1)} %copy-done.29, f32[1,768]{1,0:T(1,128)S(1)} %reshape.111.gain_ref, ...), custom_call_target="tpu_custom_call" | custom-call | flops 4000000000 | bytes 4000001 | tf_op jit(solution)/shard_map/pallas_call | solution.py:82
  64.0 2.8 %shard_map.233 = (bf16[256,768]{1,0:T(8,128)(2,1)S(1)}, bf16[256,768]{1,0:T(8,128)(2,1)S(1)}, f32[256,768]{1,0:T(8,128)S(1)}, bf16[256,768]{1,0:T(8,128)(2,1)S(1)}, f32[256,1]{1,0:T(8,128)S(1)}) custom-call(s32[4]{0:T(128)S(1)} %pad_add_fusion.place_ref, bf16[256,768]{1,0:T(8,128)(2,1)S(1)} %copy-done.30, bf16[256,768]{1,0:T(8,128)(2,1)S(1)} %copy-done.20, ...), custom_call_target="tpu_custom_call" | custom-call | flops 4000000000 | bytes 4000001 | tf_op jit(solution)/shard_map/pallas_call | solution.py:82
  66.7 2.5 collective-permute-start.15
  69.2 2.3 copy-done.42
  71.6 2.3 copy-done.44
  73.9 8.8 %shard_map.234 = (bf16[256,3072]{1,0:T(8,128)(2,1)S(1)}, bf16[256,3072]{1,0:T(8,128)(2,1)S(1)}, bf16[256,768]{1,0:T(8,128)(2,1)S(1)}, bf16[256,768]{1,0:T(8,128)...) custom-call(s32[1]{0:T(128)} %bitcast.3.me_ref, ...), custom_call_target="tpu_custom_call" | custom-call | flops 9000000512 | bytes 9000001 | tf_op jit(solution)/shard_map/pallas_call | solution.py:259
  83.5 2.3 copy-done.43
  85.8 2.3 copy-done.45
  88.1 9.7 %shard_map.235 = (bf16[256,3072]{1,0:T(8,128)(2,1)S(1)}, bf16[256,3072]{1,0:T(8,128)(2,1)S(1)}, bf16[256,768]{1,0:T(8,128)(2,1)S(1)}, bf16[256,768]{1,0:T(8,128)...) custom-call(s32[1]{0:T(128)} %bitcast.3.me_ref, ...), custom_call_target="tpu_custom_call" | custom-call | flops 9000000512 | bytes 9000001 | tf_op jit(solution)/shard_map/pallas_call | solution.py:259
  97.9 3.2 %shard_map.236 = bf16[4,768,384]{2,1,0:T(8,128)(2,1)S(1)} custom-call(s32[4]{0:T(128)S(1)} %pad_add_fusion.place_ref, bf16[768,256]{1,0:T(8,128)(2,1)S(1)} %get-tuple-element.136.left_a, bf16[768,256]{1,0:T(8,128)(2,1)S(1)} %get-tuple-element.137.left_b, bf16[256,3072]{1,0:T(8,128)(2,1)S(1)} %get-tuple-element.138.right_a, ...), custom_call_target="tpu_custom_call" | custom-call | flops 40000000000 | bytes 40000000 | tf_op jit(solution)/shard_map/pallas_call | solution.py:354
  101.2 2.3 shard_map.238
  105.7 3.5 %shard_map.237 = (bf16[2,192,384]{2,1,0:T(8,128)(2,1)S(1)}, bf16[2,192,384]{2,1,0:T(8,128)(2,1)S(1)}, bf16[2,192,384]{2,1,0:T(8,128)(2,1)S(1)}, bf16[2,192,384]{...) custom-call(s32[4]{0:T(128)S(1)} %pad_add_fusion.place_ref, ...), custom_call_target="tpu_custom_call" | custom-call | flops 1 | bytes 1 | tf_op jit(solution)/shard_map/pallas_call | solution.py:354
  109.1 1.6 collective-permute-start.19
  110.7 4.8 %collective-permute-done.16.got_ref = bf16[256,768]{1,0:T(8,128)(2,1)S(1)} collective-permute-done((bf16[256,768]{1,0:T(8,128)(2,1)S(1)}, bf16[256,768]{1,0:T(8,128)(2,1)S(1)}, u32[]{:S(2)}, u32[]{:S(2)}) %collective-permute-start.16) | collective-permute-done | bytes 393248 | tf_op jit(solution)/shard_map/ppermute | solution.py:42
  115.5 2.4 collective-permute-start.20
  117.8 1.8 collective-permute-start.21
  120.8 3.4 %shard_map.239 = (bf16[4,96,768]{2,1,0:T(8,128)(2,1)S(1)}, bf16[4,96,768]{2,1,0:T(8,128)(2,1)}, bf16[4,96,768]{2,1,0:T(8,128)(2,1)S(1)}, bf16[4,96,768]{2,1,0:T(8,128)(2,1)S(1)}) custom-call(s32[4]{0:T(128)S(1)} %pad_add_fusion.place_ref, bf16[768,256]{1,0:T(8,128)(2,1)S(1)} %get-tuple-element.141.left_a, bf16[768,256]{1,0:T(8,128)(2,1)S(1)} %get-tuple-element.142.left_b, ...), custom_call_target="tpu_custom_call" | custom-call | flops 40000000000 | bytes 40000000 | tf_op jit(solution)/shard_map/pallas_call | solution.py:354
  125.9 9.0 %shard_map.240 = (bf16[2,768,768]{2,1,0:T(8,128)(2,1)S(1)}, bf16[2,768,768]{2,1,0:T(8,128)(2,1)S(1)}, bf16[12,256,256]{2,1,0:T(8,128)(2,1)S(1)}, bf16[768,256]{1...) custom-call(s32[4]{0:T(128)S(1)} %pad_add_fusion.place_ref, ...), custom_call_target="tpu_custom_call" | custom-call | flops 1 | bytes 1 | tf_op jit(solution)/shard_map/pallas_call | solution.py:82
  136.5 4.9 %shard_map.242 = (f32[256,768]{1,0:T(8,128)}, f32[1,768]{1,0:T(1,128)S(1)}, f32[12,512]{1,0:T(8,128)S(1)}) custom-call(s32[4]{0:T(128)S(1)} %pad_add_fusion.place_ref, bf16[256,768]{1,0:T(8,128)(2,1)S(1)} %copy-done.31, f32[1,768]{1,0:T(1,128)S(1)} %copy-done.38, bf16[768,384]{1,0:T(8,128)(2,1)S(1)} %copy-done.11, ...), custom_call_target="tpu_custom_call" | custom-call | flops 1 | bytes 1 | tf_op jit(solution)/shard_map/pallas_call | solution.py:82
  143.1 14.1 %collective-permute-done.24.refs_1_ = bf16[4,96,768]{2,1,0:T(8,128)(2,1)S(1)} collective-permute-done((bf16[4,96,768]{2,1,0:T(8,128)(2,1)S(1)}, bf16[4,96,768]{2,1,0:T(8,128)(2,1)S(1)}, u32[]{:S(2)}, u32[]{:S(2)}) %collective-permute-start.24) | collective-permute-done | bytes 589856 | tf_op jit(solution)/shard_map/ppermute | solution.py:37
  158.8 2.0 shard_map.244
  164.9 7.0 %collective-permute-done.36 = f32[3456]{0:T(1024)S(1)} collective-permute-done((f32[3456]{0:T(1024)S(1)}, f32[3456]{0:T(1024)S(1)}, u32[]{:S(2)}, u32[]{:S(2)}) %collective-permute-start.36) | collective-permute-done | bytes 13856 | tf_op jit(solution)/shard_map/ppermute | solution.py:42
  174.0 2.4 collective-permute-start.29
  179.9 1.9 shard_map.246
  182.5 1.7 collective-permute-start.37
  186.4 8.1 %collective-permute-done.37 = f32[3456]{0:T(1024)S(1)} collective-permute-done((f32[3456]{0:T(1024)S(1)}, f32[3456]{0:T(1024)S(1)}, u32[]{:S(2)}, u32[]{:S(2)}) %collective-permute-start.37) | collective-permute-done | bytes 13856 | tf_op jit(solution)/shard_map/ppermute | solution.py:42
  202.7 2.3 collective-permute-start.40
  205.1 1.9 collective-permute-start.39
  210.0 1.9 shard_map.251
  211.8 3.8 %collective-permute-start.43 = (bf16[96,768]{1,0:T(8,128)(2,1)S(1)}, bf16[96,768]{1,0:T(8,128)(2,1)S(1)}, u32[]{:S(2)}, u32[]{:S(2)}) collective-permute-start(bf16[96,768]{1,0:T(8,128)(2,1)S(1)} %copy-done.50), channel_id=1, source_target_pairs={{0,6},{2,0},{4,2},{6,4},{1,7},{3,1},{5,3},{7,5},{8,14},{10,8},{12,... | collective-permute-start | bytes 442376 | tf_op jit(solution)/shard_map/ppermute | solution.py:42
  219.8 4.3 %collective-permute-start.47 = (bf16[96,768]{1,0:T(8,128)(2,1)}, bf16[96,768]{1,0:T(8,128)(2,1)S(1)}, u32[]{:S(2)}, u32[]{:S(2)}) collective-permute-start(bf16[96,768]{1,0:T(8,128)(2,1)} %copy-done.53), channel_id=1, source_target_pairs={{0,6},{2,0},{4,2},{6,4},{1,7},{3,1},{5,3},{7,5},{8,14},{10,8},{12,... | collective-permute-start | bytes 442376 | tf_op jit(solution)/shard_map/ppermute | solution.py:42
  224.1 4.1 %collective-permute-done.44.refs_1_ = bf16[4,48,768]{2,1,0:T(8,128)(2,1)S(1)} collective-permute-done((bf16[4,48,768]{2,1,0:T(8,128)(2,1)}, bf16[4,48,768]{2,1,0:T(8,128)(2,1)S(1)}, u32[]{:S(2)}, u32[]{:S(2)}) %collective-permute-start.44) | collective-permute-done | bytes 294944 | tf_op jit(solution)/shard_map/ppermute | solution.py:37
  231.9 3.5 %collective-permute-start.50 = (bf16[48,768]{1,0:T(8,128)(2,1)}, bf16[48,768]{1,0:T(8,128)(2,1)S(1)}, u32[]{:S(2)}, u32[]{:S(2)}) collective-permute-start(bf16[48,768]{1,0:T(8,128)(2,1)} %copy-done.58), channel_id=1, source_target_pairs={{0,6},{2,0},{4,2},{6,4},{1,7},{3,1},{5,3},{7,5},{8,14},{10,8},{12,... | collective-permute-start | bytes 221192 | tf_op jit(solution)/shard_map/ppermute | solution.py:42
  240.0 1.9 collective-permute-done.51.refs_1_
  243.4 2.4 collective-permute-done.52.refs_2_
  248.0 2.8 %shard_map.259 = f32[1,768,768]{2,1,0:T(8,128)} custom-call(s32[4]{0:T(128)S(1)} %pad_add_fusion.place_ref, bf16[384,384]{1,0:T(8,128)(2,1)S(1)} %maximum_bitcast_fusion.refs_0_, bf16[384,384]{1,0:T(8,128)(2,1)S(1)} %collective-permute-done.60.refs_1_, bf16[384,384]{1,0:T(8,128)(2,1)} %collective-permute-done.61.refs_2_, ...), custom_call_target="tpu_custom_call" | custom-call | flops 2000000000 | bytes 2000001 | tf_op jit(solution)/shard_map/pallas_call | solution.py:82
  251.3 4.1 %collective-permute-done.55.refs_2_ = bf16[96,768]{1,0:T(8,128)(2,1)S(1)} collective-permute-done((bf16[96,768]{1,0:T(8,128)(2,1)S(1)}, bf16[96,768]{1,0:T(8,128)(2,1)S(1)}, u32[]{:S(2)}, u32[]{:S(2)}) %collective-permute-start.55) | collective-permute-done | bytes 147488 | tf_op jit(solution)/shard_map/ppermute | solution.py:37
  256.9 1.6 shard_map.257
  258.5 2.3 shard_map.258
  (302 shorter events, 80.4 us)
Async XLA Ops:
  2.4 17.0 %collective-permute-start.2 = (bf16[112,384]{1,0:T(8,128)(2,1)S(1)}, bf16[112,384]{1,0:T(8,128)(2,1)S(1)}, u32[]{:S(2)}, u32[]{:S(2)}) collective-permute-start(bf16[112,384]{1,0:T(8,128)(2,1)S(1)} %get-tuple-element.255), channel_id=1, source_target_pairs={{0,6},{2,0},{4,2},{6,4},{1,7},{3,1},{5,3},{7,5},{8,14},{10,8},{12,... | collective-permute-start | bytes 258056 | tf_op jit(solution)/shard_map/ppermute | solution.py:42
  7.5 11.9 %collective-permute-start.1 = (bf16[112,384]{1,0:T(8,128)(2,1)S(1)}, bf16[112,384]{1,0:T(8,128)(2,1)S(1)}, u32[]{:S(2)}, u32[]{:S(2)}) collective-permute-start(bf16[112,384]{1,0:T(8,128)(2,1)S(1)} %get-tuple-element.255), channel_id=1, source_target_pairs={{0,4},{2,6},{4,0},{6,2},{1,5},{3,7},{5,1},{7,3},{8,12},{10,14},{12... | collective-permute-start | bytes 258056 | tf_op jit(solution)/shard_map/ppermute | solution.py:42
  7.5 11.9 %collective-permute-start = (bf16[112,384]{1,0:T(8,128)(2,1)S(1)}, bf16[112,384]{1,0:T(8,128)(2,1)S(1)}, u32[]{:S(2)}, u32[]{:S(2)}) collective-permute-start(bf16[112,384]{1,0:T(8,128)(2,1)S(1)} %get-tuple-element.255), channel_id=1, source_target_pairs={{0,2},{2,4},{4,6},{6,0},{1,3},{3,5},{5,7},{7,1},{8,10},{10,12},{12... | collective-permute-start | bytes 258056 | tf_op jit(solution)/shard_map/ppermute | solution.py:42
  9.4 12.4 %collective-permute-start.9 = (bf16[96,384]{1,0:T(8,128)(2,1)S(1)}, bf16[96,384]{1,0:T(8,128)(2,1)S(1)}, u32[]{:S(2)}, u32[]{:S(2)}) collective-permute-start(bf16[96,384]{1,0:T(8,128)(2,1)S(1)} %dynamic-slice_select_fusion), channel_id=1, source_target_pairs={{0,6},{2,0},{4,2},{6,4},{1,7},{3,1},{5,3},{7,5},{8,14},{10,8},{12,... | collective-permute-start | bytes 221192 | tf_op jit(solution)/shard_map/ppermute | solution.py:42
  12.3 9.5 %collective-permute-start.8 = (bf16[96,384]{1,0:T(8,128)(2,1)S(1)}, bf16[96,384]{1,0:T(8,128)(2,1)S(1)}, u32[]{:S(2)}, u32[]{:S(2)}) collective-permute-start(bf16[96,384]{1,0:T(8,128)(2,1)S(1)} %dynamic-slice_select_fusion), channel_id=1, source_target_pairs={{0,4},{2,6},{4,0},{6,2},{1,5},{3,7},{5,1},{7,3},{8,12},{10,14},{12... | collective-permute-start | bytes 221192 | tf_op jit(solution)/shard_map/ppermute | solution.py:42
  19.5 10.8 %collective-permute-start.3 = (bf16[4,112,384]{2,1,0:T(8,128)(2,1)S(1)}, bf16[4,112,384]{2,1,0:T(8,128)(2,1)S(1)}, u32[]{:S(2)}, u32[]{:S(2)}) collective-permute-start(bf16[4,112,384]{2,1,0:T(8,128)(2,1)S(1)} %pad_maximum_fusion.own_ref), channel_id=1, source_target_pairs={{0,1},{1,0},{2,3},{3,2},{4,5},{5,4},{6,7},{7,6},{8,9},{9,8},{10,11... | collective-permute-start | bytes 1032200 | tf_op jit(solution)/shard_map/ppermute | solution.py:42
  25.6 8.7 %collective-permute-start.10 = (bf16[4,96,384]{2,1,0:T(8,128)(2,1)S(1)}, bf16[4,96,384]{2,1,0:T(8,128)(2,1)S(1)}, u32[]{:S(2)}, u32[]{:S(2)}) collective-permute-start(bf16[4,96,384]{2,1,0:T(8,128)(2,1)S(1)} %pad_maximum_fusion.1.own_ref), channel_id=1, source_target_pairs={{0,1},{1,0},{2,3},{3,2},{4,5},{5,4},{6,7},{7,6},{8,9},{9,8},{10,11... | collective-permute-start | bytes 884744 | tf_op jit(solution)/shard_map/ppermute | solution.py:42
  30.9 12.2 %collective-permute-start.5 = (bf16[768,384]{1,0:T(8,128)(2,1)S(1)}, bf16[768,384]{1,0:T(8,128)(2,1)S(1)}, u32[]{:S(2)}, u32[]{:S(2)}) collective-permute-start(bf16[768,384]{1,0:T(8,128)(2,1)S(1)} %get-tuple-element.124.refs_0_), channel_id=1, source_target_pairs={{0,16},{8,24},{16,0},{24,8},{1,17},{9,25},{17,1},{25,9},{2,18},{10... | collective-permute-start | bytes 1769480 | tf_op jit(solution)/shard_map/ppermute | solution.py:37
  34.3 9.1 %collective-permute-start.13 = (bf16[256,768]{1,0:T(8,128)(2,1)}, bf16[256,768]{1,0:T(8,128)(2,1)}, u32[]{:S(2)}, u32[]{:S(2)}) collective-permute-start(bf16[256,768]{1,0:T(8,128)(2,1)} %get-tuple-element.126), channel_id=1, source_target_pairs={{0,1},{1,0},{2,3},{3,2},{4,5},{5,4},{6,7},{7,6},{8,9},{9,8},{10,11... | collective-permute-start | bytes 1179656 | tf_op jit(solution)/shard_map/ppermute | solution.py:42
  36.4 21.8 %collective-permute-start.11 = (bf16[768,384]{1,0:T(8,128)(2,1)S(1)}, bf16[768,384]{1,0:T(8,128)(2,1)S(1)}, u32[]{:S(2)}, u32[]{:S(2)}) collective-permute-start(bf16[768,384]{1,0:T(8,128)(2,1)S(1)} %shard_map.232.refs_0_.refs_4_), channel_id=1, source_target_pairs={{0,8},{8,0},{16,24},{24,16},{1,9},{9,1},{17,25},{25,17},{2,10},{10... | collective-permute-start | bytes 1769480 | tf_op jit(solution)/shard_map/ppermute | solution.py:37
  36.5 21.2 %collective-permute-start.12 = (bf16[768,384]{1,0:T(8,128)(2,1)S(1)}, bf16[768,384]{1,0:T(8,128)(2,1)S(1)}, u32[]{:S(2)}, u32[]{:S(2)}) collective-permute-start(bf16[768,384]{1,0:T(8,128)(2,1)S(1)} %shard_map.232.refs_0_.refs_4_), channel_id=1, source_target_pairs={{0,16},{8,24},{16,0},{24,8},{1,17},{9,25},{17,1},{25,9},{2,18},{10... | collective-permute-start | bytes 1769480 | tf_op jit(solution)/shard_map/ppermute | solution.py:37
  38.0 12.4 %collective-permute-start.4 = (bf16[768,384]{1,0:T(8,128)(2,1)S(1)}, bf16[768,384]{1,0:T(8,128)(2,1)}, u32[]{:S(2)}, u32[]{:S(2)}) collective-permute-start(bf16[768,384]{1,0:T(8,128)(2,1)S(1)} %get-tuple-element.124.refs_0_), channel_id=1, source_target_pairs={{0,8},{8,0},{16,24},{24,16},{1,9},{9,1},{17,25},{25,17},{2,10},{10... | collective-permute-start | bytes 1769480 | tf_op jit(solution)/shard_map/ppermute | solution.py:37
  66.7 16.7 %collective-permute-start.15 = (bf16[256,768]{1,0:T(8,128)(2,1)S(1)}, bf16[256,768]{1,0:T(8,128)(2,1)S(1)}, u32[]{:S(2)}, u32[]{:S(2)}) collective-permute-start(bf16[256,768]{1,0:T(8,128)(2,1)S(1)} %get-tuple-element.131.rows_ref), channel_id=1, source_target_pairs={{0,1},{1,0},{2,3},{3,2},{4,5},{5,4},{6,7},{7,6},{8,9},{9,8},{10,11... | collective-permute-start | bytes 1179656 | tf_op jit(solution)/shard_map/ppermute | solution.py:42
  103.5 11.9 %collective-permute-start.18 = (bf16[2,768,768]{2,1,0:T(8,128)(2,1)S(1)}, bf16[2,768,768]{2,1,0:T(8,128)(2,1)S(1)}, u32[]{:S(2)}, u32[]{:S(2)}) collective-permute-start(bf16[2,768,768]{2,1,0:T(8,128)(2,1)S(1)} %shard_map.238), channel_id=1, source_target_pairs={{0,8},{8,0},{16,24},{24,16},{1,9},{9,1},{17,25},{25,17},{2,10},{10... | collective-permute-start | bytes 7077896 | tf_op jit(solution)/shard_map/ppermute | solution.py:37
  104.3 11.2 %collective-permute-start.16 = (bf16[256,768]{1,0:T(8,128)(2,1)S(1)}, bf16[256,768]{1,0:T(8,128)(2,1)S(1)}, u32[]{:S(2)}, u32[]{:S(2)}) collective-permute-start(bf16[256,768]{1,0:T(8,128)(2,1)S(1)} %get-tuple-element.135), channel_id=1, source_target_pairs={{0,1},{1,0},{2,3},{3,2},{4,5},{5,4},{6,7},{7,6},{8,9},{9,8},{10,11... | collective-permute-start | bytes 1179656 | tf_op jit(solution)/shard_map/ppermute | solution.py:42
  109.1 25.9 %collective-permute-start.19 = (bf16[4,192,384]{2,1,0:T(8,128)(2,1)S(1)}, bf16[4,192,384]{2,1,0:T(8,128)(2,1)S(1)}, u32[]{:S(2)}, u32[]{:S(2)}) collective-permute-start(bf16[4,192,384]{2,1,0:T(8,128)(2,1)S(1)} %get-tuple-element.140), channel_id=1, source_target_pairs={{0,16},{8,24},{16,0},{24,8},{1,17},{9,25},{17,1},{25,9},{2,18},{10... | collective-permute-start | bytes 1769480 | tf_op jit(solution)/shard_map/ppermute | solution.py:37
  115.5 27.5 %collective-permute-start.20 = (bf16[2,192,384]{2,1,0:T(8,128)(2,1)S(1)}, bf16[2,192,384]{2,1,0:T(8,128)(2,1)S(1)}, u32[]{:S(2)}, u32[]{:S(2)}) collective-permute-start(bf16[2,192,384]{2,1,0:T(8,128)(2,1)S(1)} %get-tuple-element.165), channel_id=1, source_target_pairs={{0,2},{2,4},{4,6},{6,0},{1,3},{3,5},{5,7},{7,1},{8,10},{10,12},{12... | collective-permute-start | bytes 884744 | tf_op jit(solution)/shard_map/ppermute | solution.py:42
  117.8 25.1 %collective-permute-start.21 = (bf16[2,192,384]{2,1,0:T(8,128)(2,1)S(1)}, bf16[2,192,384]{2,1,0:T(8,128)(2,1)S(1)}, u32[]{:S(2)}, u32[]{:S(2)}) collective-permute-start(bf16[2,192,384]{2,1,0:T(8,128)(2,1)S(1)} %get-tuple-element.166), channel_id=1, source_target_pairs={{0,4},{2,6},{4,0},{6,2},{1,5},{3,7},{5,1},{7,3},{8,12},{10,14},{12... | collective-permute-start | bytes 884744 | tf_op jit(solution)/shard_map/ppermute | solution.py:42
  119.7 23.3 %collective-permute-start.22 = (bf16[2,192,384]{2,1,0:T(8,128)(2,1)S(1)}, bf16[2,192,384]{2,1,0:T(8,128)(2,1)S(1)}, u32[]{:S(2)}, u32[]{:S(2)}) collective-permute-start(bf16[2,192,384]{2,1,0:T(8,128)(2,1)S(1)} %get-tuple-element.167), channel_id=1, source_target_pairs={{0,6},{2,0},{4,2},{6,4},{1,7},{3,1},{5,3},{7,5},{8,14},{10,8},{12,... | collective-permute-start | bytes 884744 | tf_op jit(solution)/shard_map/ppermute | solution.py:42
  135.0 23.8 %collective-permute-start.23 = (bf16[2,768,768]{2,1,0:T(8,128)(2,1)S(1)}, bf16[2,768,768]{2,1,0:T(8,128)(2,1)S(1)}, u32[]{:S(2)}, u32[]{:S(2)}) collective-permute-start(bf16[2,768,768]{2,1,0:T(8,128)(2,1)S(1)} %get-tuple-element.169), channel_id=1, source_target_pairs={{0,8},{8,0},{16,24},{24,16},{1,9},{9,1},{17,25},{25,17},{2,10},{10... | collective-permute-start | bytes 7077896 | tf_op jit(solution)/shard_map/ppermute | solution.py:37
  141.4 15.7 %collective-permute-start.24 = (bf16[4,96,768]{2,1,0:T(8,128)(2,1)S(1)}, bf16[4,96,768]{2,1,0:T(8,128)(2,1)S(1)}, u32[]{:S(2)}, u32[]{:S(2)}) collective-permute-start(bf16[4,96,768]{2,1,0:T(8,128)(2,1)S(1)} %get-tuple-element.175), channel_id=1, source_target_pairs={{0,16},{8,24},{16,0},{24,8},{1,17},{9,25},{17,1},{25,9},{2,18},{10... | collective-permute-start | bytes 1769480 | tf_op jit(solution)/shard_map/ppermute | solution.py:37
  157.2 27.0 %collective-permute-start.26 = (bf16[4,96,768]{2,1,0:T(8,128)(2,1)}, bf16[4,96,768]{2,1,0:T(8,128)(2,1)S(1)}, u32[]{:S(2)}, u32[]{:S(2)}) collective-permute-start(bf16[4,96,768]{2,1,0:T(8,128)(2,1)} %get-tuple-element.183), channel_id=1, source_target_pairs={{0,16},{8,24},{16,0},{24,8},{1,17},{9,25},{17,1},{25,9},{2,18},{10... | collective-permute-start | bytes 1769480 | tf_op jit(solution)/shard_map/ppermute | solution.py:37
  163.2 15.3 %collective-permute-start.25 = (bf16[2,4,48,768]{3,2,1,0:T(8,128)(2,1)}, bf16[2,4,48,768]{3,2,1,0:T(8,128)(2,1)}, u32[]{:S(2)}, u32[]{:S(2)}) collective-permute-start(bf16[2,4,48,768]{3,2,1,0:T(8,128)(2,1)} %get-tuple-element.173), channel_id=1, source_target_pairs={{0,1},{1,0},{2,3},{3,2},{4,5},{5,4},{6,7},{7,6},{8,9},{9,8},{10,11... | collective-permute-start | bytes 1769480 | tf_op jit(solution)/shard_map/ppermute | solution.py:42
  164.1 7.9 %collective-permute-start.36 = (f32[3456]{0:T(1024)S(1)}, f32[3456]{0:T(1024)S(1)}, u32[]{:S(2)}, u32[]{:S(2)}) collective-permute-start(f32[3456]{0:T(1024)S(1)} %pad_maximum_fusion.5), channel_id=1, source_target_pairs={{0,24},{8,0},{16,8},{24,16},{1,25},{9,1},{17,9},{25,17},{2,26},{10... | collective-permute-start | bytes 41480 | tf_op jit(solution)/shard_map/ppermute | solution.py:42
  164.1 9.0 %collective-permute-start.35 = (f32[3456]{0:T(1024)S(1)}, f32[3456]{0:T(1024)S(1)}, u32[]{:S(2)}, u32[]{:S(2)}) collective-permute-start(f32[3456]{0:T(1024)S(1)} %pad_maximum_fusion.5), channel_id=1, source_target_pairs={{0,16},{8,24},{16,0},{24,8},{1,17},{9,25},{17,1},{25,9},{2,18},{10... | collective-permute-start | bytes 41480 | tf_op jit(solution)/shard_map/ppermute | solution.py:42
  164.9 9.1 %collective-permute-start.34 = (f32[3456]{0:T(1024)S(1)}, f32[3456]{0:T(1024)S(1)}, u32[]{:S(2)}, u32[]{:S(2)}) collective-permute-start(f32[3456]{0:T(1024)S(1)} %pad_maximum_fusion.5), channel_id=1, source_target_pairs={{0,8},{8,16},{16,24},{24,0},{1,9},{9,17},{17,25},{25,1},{2,10},{10... | collective-permute-start | bytes 41480 | tf_op jit(solution)/shard_map/ppermute | solution.py:42
  172.0 9.8 %collective-permute-start.27 = (bf16[192,384]{1,0:T(8,128)(2,1)S(1)}, bf16[192,384]{1,0:T(8,128)(2,1)S(1)}, u32[]{:S(2)}, u32[]{:S(2)}) collective-permute-start(bf16[192,384]{1,0:T(8,128)(2,1)S(1)} %copy-done.57), channel_id=1, source_target_pairs={{0,2},{2,4},{4,6},{6,0},{1,3},{3,5},{5,7},{7,1},{8,10},{10,12},{12... | collective-permute-start | bytes 442376 | tf_op jit(solution)/shard_map/ppermute | solution.py:42
  173.1 25.3 %collective-permute-start.28 = (bf16[192,384]{1,0:T(8,128)(2,1)}, bf16[192,384]{1,0:T(8,128)(2,1)}, u32[]{:S(2)}, u32[]{:S(2)}) collective-permute-start(bf16[192,384]{1,0:T(8,128)(2,1)} %get-tuple-element.189), channel_id=1, source_target_pairs={{0,4},{2,6},{4,0},{6,2},{1,5},{3,7},{5,1},{7,3},{8,12},{10,14},{12... | collective-permute-start | bytes 442376 | tf_op jit(solution)/shard_map/ppermute | solution.py:42
  174.0 24.9 %collective-permute-start.29 = (bf16[192,384]{1,0:T(8,128)(2,1)}, bf16[192,384]{1,0:T(8,128)(2,1)}, u32[]{:S(2)}, u32[]{:S(2)}) collective-permute-start(bf16[192,384]{1,0:T(8,128)(2,1)} %get-tuple-element.191), channel_id=1, source_target_pairs={{0,6},{2,0},{4,2},{6,4},{1,7},{3,1},{5,3},{7,5},{8,14},{10,8},{12,... | collective-permute-start | bytes 442376 | tf_op jit(solution)/shard_map/ppermute | solution.py:42
  178.6 30.3 %collective-permute-start.32 = (bf16[2,4,48,768]{3,2,1,0:T(8,128)(2,1)}, bf16[2,4,48,768]{3,2,1,0:T(8,128)(2,1)}, u32[]{:S(2)}, u32[]{:S(2)}) collective-permute-start(bf16[2,4,48,768]{3,2,1,0:T(8,128)(2,1)} %copy-done.46), channel_id=1, source_target_pairs={{0,1},{1,0},{2,3},{3,2},{4,5},{5,4},{6,7},{7,6},{8,9},{9,8},{10,11... | collective-permute-start | bytes 1769480 | tf_op jit(solution)/shard_map/ppermute | solution.py:42
  182.5 12.0 %collective-permute-start.37 = (f32[3456]{0:T(1024)S(1)}, f32[3456]{0:T(1024)S(1)}, u32[]{:S(2)}, u32[]{:S(2)}) collective-permute-start(f32[3456]{0:T(1024)S(1)} %add_add_fusion.1), channel_id=1, source_target_pairs={{0,1},{1,0},{2,3},{3,2},{4,5},{5,4},{6,7},{7,6},{8,9},{9,8},{10,11... | collective-permute-start | bytes 41480 | tf_op jit(solution)/shard_map/ppermute | solution.py:42
  184.2 20.9 %collective-permute-start.31 = (bf16[4,48,768]{2,1,0:T(8,128)(2,1)}, bf16[4,48,768]{2,1,0:T(8,128)(2,1)S(1)}, u32[]{:S(2)}, u32[]{:S(2)}) collective-permute-start(bf16[4,48,768]{2,1,0:T(8,128)(2,1)} %get-tuple-element.194), channel_id=1, source_target_pairs={{0,16},{8,24},{16,0},{24,8},{1,17},{9,25},{17,1},{25,9},{2,18},{10... | collective-permute-start | bytes 884744 | tf_op jit(solution)/shard_map/ppermute | solution.py:37
  198.4 20.1 %collective-permute-start.41 = (bf16[96,768]{1,0:T(8,128)(2,1)}, bf16[96,768]{1,0:T(8,128)(2,1)S(1)}, u32[]{:S(2)}, u32[]{:S(2)}) collective-permute-start(bf16[96,768]{1,0:T(8,128)(2,1)} %copy-done.52), channel_id=1, source_target_pairs={{0,2},{2,4},{4,6},{6,0},{1,3},{3,5},{5,7},{7,1},{8,10},{10,12},{12... | collective-permute-start | bytes 442376 | tf_op jit(solution)/shard_map/ppermute | solution.py:42
  199.0 19.5 %collective-permute-start.42 = (bf16[96,768]{1,0:T(8,128)(2,1)}, bf16[96,768]{1,0:T(8,128)(2,1)S(1)}, u32[]{:S(2)}, u32[]{:S(2)}) collective-permute-start(bf16[96,768]{1,0:T(8,128)(2,1)} %copy-done.51), channel_id=1, source_target_pairs={{0,4},{2,6},{4,0},{6,2},{1,5},{3,7},{5,1},{7,3},{8,12},{10,14},{12... | collective-permute-start | bytes 442376 | tf_op jit(solution)/shard_map/ppermute | solution.py:42
  202.7 9.1 %collective-permute-start.40 = (f32[3456]{0:T(1024)}, f32[3456]{0:T(1024)S(1)}, u32[]{:S(2)}, u32[]{:S(2)}) collective-permute-start(f32[3456]{0:T(1024)} %add.138), channel_id=1, source_target_pairs={{0,6},{2,0},{4,2},{6,4},{1,7},{3,1},{5,3},{7,5},{8,14},{10,8},{12,... | collective-permute-start | bytes 41480 | tf_op jit(solution)/shard_map/ppermute | solution.py:42
  205.1 10.5 %collective-permute-start.39 = (f32[3456]{0:T(1024)}, f32[3456]{0:T(1024)S(1)}, u32[]{:S(2)}, u32[]{:S(2)}) collective-permute-start(f32[3456]{0:T(1024)} %add.138), channel_id=1, source_target_pairs={{0,4},{2,6},{4,0},{6,2},{1,5},{3,7},{5,1},{7,3},{8,12},{10,14},{12... | collective-permute-start | bytes 41480 | tf_op jit(solution)/shard_map/ppermute | solution.py:42
  211.8 8.0 %collective-permute-start.43 = (bf16[96,768]{1,0:T(8,128)(2,1)S(1)}, bf16[96,768]{1,0:T(8,128)(2,1)S(1)}, u32[]{:S(2)}, u32[]{:S(2)}) collective-permute-start(bf16[96,768]{1,0:T(8,128)(2,1)S(1)} %copy-done.50), channel_id=1, source_target_pairs={{0,6},{2,0},{4,2},{6,4},{1,7},{3,1},{5,3},{7,5},{8,14},{10,8},{12,... | collective-permute-start | bytes 442376 | tf_op jit(solution)/shard_map/ppermute | solution.py:42
  215.6 19.8 %collective-permute-start.61 = (bf16[384,384]{1,0:T(8,128)(2,1)S(1)}, bf16[384,384]{1,0:T(8,128)(2,1)}, u32[]{:S(2)}, u32[]{:S(2)}) collective-permute-start(bf16[384,384]{1,0:T(8,128)(2,1)S(1)} %maximum_bitcast_fusion.refs_0_), channel_id=1, source_target_pairs={{0,16},{8,24},{16,0},{24,8},{1,17},{9,25},{17,1},{25,9},{2,18},{10... | collective-permute-start | bytes 884744 | tf_op jit(solution)/shard_map/ppermute | solution.py:37
  216.1 12.1 %collective-permute-start.44 = (bf16[4,48,768]{2,1,0:T(8,128)(2,1)}, bf16[4,48,768]{2,1,0:T(8,128)(2,1)S(1)}, u32[]{:S(2)}, u32[]{:S(2)}) collective-permute-start(bf16[4,48,768]{2,1,0:T(8,128)(2,1)} %get-tuple-element.214), channel_id=1, source_target_pairs={{0,16},{8,24},{16,0},{24,8},{1,17},{9,25},{17,1},{25,9},{2,18},{10... | collective-permute-start | bytes 884744 | tf_op jit(solution)/shard_map/ppermute | solution.py:37
  218.5 11.2 %collective-permute-start.45 = (bf16[96,768]{1,0:T(8,128)(2,1)}, bf16[96,768]{1,0:T(8,128)(2,1)S(1)}, u32[]{:S(2)}, u32[]{:S(2)}) collective-permute-start(bf16[96,768]{1,0:T(8,128)(2,1)} %copy-done.55), channel_id=1, source_target_pairs={{0,2},{2,4},{4,6},{6,0},{1,3},{3,5},{5,7},{7,1},{8,10},{10,12},{12... | collective-permute-start | bytes 442376 | tf_op jit(solution)/shard_map/ppermute | solution.py:42
  218.5 11.9 %collective-permute-start.46 = (bf16[96,768]{1,0:T(8,128)(2,1)}, bf16[96,768]{1,0:T(8,128)(2,1)S(1)}, u32[]{:S(2)}, u32[]{:S(2)}) collective-permute-start(bf16[96,768]{1,0:T(8,128)(2,1)} %copy-done.54), channel_id=1, source_target_pairs={{0,4},{2,6},{4,0},{6,2},{1,5},{3,7},{5,1},{7,3},{8,12},{10,14},{12... | collective-permute-start | bytes 442376 | tf_op jit(solution)/shard_map/ppermute | solution.py:42
  219.8 12.1 %collective-permute-start.47 = (bf16[96,768]{1,0:T(8,128)(2,1)}, bf16[96,768]{1,0:T(8,128)(2,1)S(1)}, u32[]{:S(2)}, u32[]{:S(2)}) collective-permute-start(bf16[96,768]{1,0:T(8,128)(2,1)} %copy-done.53), channel_id=1, source_target_pairs={{0,6},{2,0},{4,2},{6,4},{1,7},{3,1},{5,3},{7,5},{8,14},{10,8},{12,... | collective-permute-start | bytes 442376 | tf_op jit(solution)/shard_map/ppermute | solution.py:42
  229.7 18.3 %collective-permute-start.60 = (bf16[384,384]{1,0:T(8,128)(2,1)S(1)}, bf16[384,384]{1,0:T(8,128)(2,1)S(1)}, u32[]{:S(2)}, u32[]{:S(2)}) collective-permute-start(bf16[384,384]{1,0:T(8,128)(2,1)S(1)} %maximum_bitcast_fusion.refs_0_), channel_id=1, source_target_pairs={{0,8},{8,0},{16,24},{24,16},{1,9},{9,1},{17,25},{25,17},{2,10},{10... | collective-permute-start | bytes 884744 | tf_op jit(solution)/shard_map/ppermute | solution.py:37
  230.4 7.8 %collective-permute-start.49 = (bf16[48,768]{1,0:T(8,128)(2,1)}, bf16[48,768]{1,0:T(8,128)(2,1)S(1)}, u32[]{:S(2)}, u32[]{:S(2)}) collective-permute-start(bf16[48,768]{1,0:T(8,128)(2,1)} %copy-done.59), channel_id=1, source_target_pairs={{0,4},{2,6},{4,0},{6,2},{1,5},{3,7},{5,1},{7,3},{8,12},{10,14},{12... | collective-permute-start | bytes 221192 | tf_op jit(solution)/shard_map/ppermute | solution.py:42
  235.4 12.6 %collective-permute-start.62 = (bf16[384,384]{1,0:T(8,128)(2,1)}, bf16[384,384]{1,0:T(8,128)(2,1)}, u32[]{:S(2)}, u32[]{:S(2)}) collective-permute-start(bf16[384,384]{1,0:T(8,128)(2,1)} %collective-permute-done.61.refs_2_), channel_id=1, source_target_pairs={{0,8},{8,0},{16,24},{24,16},{1,9},{9,1},{17,25},{25,17},{2,10},{10... | collective-permute-start | bytes 884744 | tf_op jit(solution)/shard_map/ppermute | solution.py:37
  238.2 17.7 %collective-permute-start.33 = (bf16[256,768]{1,0:T(8,128)(2,1)S(1)}, bf16[256,768]{1,0:T(8,128)(2,1)S(1)}, u32[]{:S(2)}, u32[]{:S(2)}) collective-permute-start(bf16[256,768]{1,0:T(8,128)(2,1)S(1)} %copy-done.48), channel_id=1, source_target_pairs={{0,1},{1,0},{2,3},{3,2},{4,5},{5,4},{6,7},{7,6},{8,9},{9,8},{10,11... | collective-permute-start | bytes 1179656 | tf_op jit(solution)/shard_map/ppermute | solution.py:42
  245.8 9.6 %collective-permute-start.58 = (bf16[192,768]{1,0:T(8,128)(2,1)S(1)}, bf16[192,768]{1,0:T(8,128)(2,1)S(1)}, u32[]{:S(2)}, u32[]{:S(2)}) collective-permute-start(bf16[192,768]{1,0:T(8,128)(2,1)S(1)} %pad_maximum_fusion.2.refs_0_), channel_id=1, source_target_pairs={{0,16},{8,24},{16,0},{24,8},{1,17},{9,25},{17,1},{25,9},{2,18},{10... | collective-permute-start | bytes 884744 | tf_op jit(solution)/shard_map/ppermute | solution.py:37
  246.5 8.8 %collective-permute-start.55 = (bf16[96,768]{1,0:T(8,128)(2,1)S(1)}, bf16[96,768]{1,0:T(8,128)(2,1)S(1)}, u32[]{:S(2)}, u32[]{:S(2)}) collective-permute-start(bf16[96,768]{1,0:T(8,128)(2,1)S(1)} %pad_maximum_fusion.3.refs_0_), channel_id=1, source_target_pairs={{0,16},{8,24},{16,0},{24,8},{1,17},{9,25},{17,1},{25,9},{2,18},{10... | collective-permute-start | bytes 442376 | tf_op jit(solution)/shard_map/ppermute | solution.py:37
  (87 other events, 500.2 us)
where the time goes:
time: 263 us; the launch traced here: 261 us
  starting transfers between devices  70.9 us (27%)
  Pallas kernels  69.6 us (26%)
  waiting for transfers between devices  62.8 us (24%)
  local copies, waits for them, and re-layouts  38.5 us (15%)
  other arithmetic  9.31 us (4%)
  matrix products  8.27 us (3%)
    ppermute x39, starting transfers between devices, shift(): lax.ppermute(values, axis, [(i, (i + step) % count) for i in range(count)])  54 us
    pallas_call x25, Pallas kernels, whole_call(): pl.pallas_call(kernel, out_shape=[jax.ShapeDtypeStruct(s, d) for s, d in...  38.8 us
    unnamed x146, local copies, waits for them, and re-layouts  34.2 us
    ppermute x39, waiting for transfers between devices, shift(): lax.ppermute(values, axis, [(i, (i + step) % count) for i in range(count)])  33.9 us
    ppermute x24, waiting for transfers between devices, rep_swap(): return lax.ppermute(values, 'rep', [(i, i ^ bit) for i in range(count)])  28.8 us
    pallas_call x2, Pallas kernels, run_expert(): pl.pallas_call(functools.partial(expert_kernel, experts), out_shape=[jax....  18.5 us
    ppermute x24, starting transfers between devices, rep_swap(): return lax.ppermute(values, 'rep', [(i, i ^ bit) for i in range(count)])  16.9 us
    pallas_call x4, Pallas kernels, outer_grad(): pl.pallas_call(functools.partial(outer_kernel, keep, second), out_shape=[...  12.3 us
  transfers between devices with their start and end apart: 63, of which 19 were waited for; matrix products, arithmetic and copies ran while one was open for 8% of the time, Pallas kernels for 20%

commit v1 on v0

--- a/solution.py
+++ b/solution.py
@@ -55,8 +55,9 @@
     return total.astype(BF16)
 
 
-VMEM_BYTES = 32 * 1024 * 1024
-BIG = 40
+VMEM_BYTES = 26 * 1024 * 1024
+EXPERT_VMEM = 18 * 1024 * 1024
+BIG = 30
 NT = (((1,), (1,)), ((), ()))
 TN = (((0,), (0,)), ((), ()))
 
@@ -77,7 +78,7 @@
     return pl.CostEstimate(flops=us * 10**9 + 1, bytes_accessed=us * 10**6 + 1, transcendentals=0)
 
 
-def whole_call(kernel, outs, scalars, arrays, scratch=(), us=2):
+def whole_call(kernel, outs, scalars, arrays, scratch=(), us=2, vmem_bytes=VMEM_BYTES):
     vmem = pl.BlockSpec(memory_space=pltpu.VMEM)
     return pl.pallas_call(
         kernel,
@@ -86,7 +87,7 @@
         out_specs=[vmem] * len(outs),
         scratch_shapes=list(scratch),
         cost_estimate=estimate(us),
-        compiler_params=pltpu.CompilerParams(vmem_limit_bytes=VMEM_BYTES),
+        compiler_params=pltpu.CompilerParams(vmem_limit_bytes=vmem_bytes),
     )(*scalars, *arrays)
 
 
@@ -252,7 +253,7 @@
 def run_expert(experts, me, rows, cot, router, w_in, w_out, slot_back, part):
     count, width = rows.shape
     inner = w_in.shape[2]
-    tile = 512
+    tile = 1024
     lanes = router.shape[1]
     const = lambda shape: pl.BlockSpec(shape, lambda j, s: (0, 0))
     wide = pl.BlockSpec((count, tile), lambda j, s: (0, j))
@@ -289,80 +290,46 @@
             ],
         ),
         cost_estimate=estimate(9),
-        compiler_params=pltpu.CompilerParams(vmem_limit_bytes=VMEM_BYTES),
+        compiler_params=pltpu.CompilerParams(vmem_limit_bytes=EXPERT_VMEM),
     )(me, rows, cot, router, w_in, w_out, slot_back)
 
 
-def outer_kernel(keep, second, place_ref, left_a, left_b, right_a, right_b, *refs):
-    total = mm(left_a[...], right_a[...]) + mm(left_b[...], right_b[...])
-    if not keep:
-        refs[0][0] = total.astype(BF16)
-        return
-    got, outs = refs[0], refs[1:]
-    total = (total + got[0].astype(F32)).astype(BF16)
-    step = pl.program_id(0)
-    if second:
-        half = total.shape[0] // 2
-        high = place_ref[0]
+def outer_kernel(place_ref, *refs):
+    cots, hidden, rows, grad_pre = refs[0:2], refs[2:4], refs[4:6], refs[6:8]
+    second_send, second_own, first_send, first_own = refs[8:]
+    high, low, dp = place_ref[0], place_ref[1], place_ref[2]
+    blocks, _, columns = second_send.shape
+    for block in range(blocks):
+        for core, out in ((1 - low, second_send), (low, second_own)):
+            start = (2 * lax.rem(block + dp, blocks) + core) * columns
+            lanes = pl.ds(pl.multiple_of(start, 128), columns)
+            out[block] = (mm(cots[0][...], hidden[0][:, lanes]) + mm(cots[1][...], hidden[1][:, lanes])).astype(BF16)
+    columns = first_send.shape[2]
+    for index, x in enumerate((1 - high, high)):
+        for core, out in ((1 - low, first_send), (low, first_own)):
+            lanes = pl.ds(pl.multiple_of((2 * x + core) * columns, 128), columns)
+            out[index] = (mm(rows[0][...], grad_pre[0][:, lanes]) + mm(rows[1][...], grad_pre[1][:, lanes])).astype(BF16)
+
+
+def core_sum_kernel(place_ref, second_own, second_got, first_own, first_got, *outs):
+    high, dp = place_ref[0], place_ref[2]
+    blocks, width, _ = second_own.shape
+    half, rows = width // 2, width // 4
+    for block in range(blocks):
+        total = (second_own[block].astype(F32) + second_got[block].astype(F32)).astype(BF16)
         send = jnp.where(high == 0, total[half:], total[:half])
         kept = jnp.where(high == 0, total[:half], total[half:])
-        for block in range(len(outs) - 2):
-
-            @pl.when(step == block)
-            def _():
-                outs[block][0] = send[: half // 2]
-                outs[block][1] = kept[: half // 2]
-
-        outs[-2][0] = send[half // 2 :]
-        outs[-1][0] = kept[half // 2 :]
-        return
-    blocks, rows, _ = outs[0].shape
-    for part in range(2):
-
-        @pl.when(step == part)
-        def _():
-            for block in range(blocks):
-                at = lax.rem(block - place_ref[2] + blocks, blocks)
-                start = 2 * block * rows
-                outs[2 * part][at] = total[start : start + rows]
-                outs[2 * part + 1][at] = total[start + rows : start + 2 * rows]
-
-
-def outer_grad(second, place, left, right, blocks, got=None, us=0):
-    keep = got is not None
-    width, count = left[0].shape
-    inner = right[0].shape[1]
-    core = lambda s: s[1] if keep else 1 - s[1]
-    whole = pl.BlockSpec((width, count), lambda i, s: (0, 0))
-    fixed = lambda shape: pl.BlockSpec(shape, lambda i, s: (0,) * len(shape))
-    if second:
-        steps, columns = blocks, inner // (2 * blocks)
-        wide = pl.BlockSpec((count, columns), lambda i, s: (0, 2 * lax.rem(i + s[2], blocks) + core(s)))
-        quarter = pl.BlockSpec((1, width // 4, columns), lambda i, s: (i, 0, 0))
-        shapes = [(2, width // 4, columns)] * blocks + [(blocks, width // 4, columns)] * 2
-        out_specs = [fixed(shapes[0])] * blocks + [quarter] * 2
-    else:
-        steps, columns = 2, inner // 4
-        wide = pl.BlockSpec(
-            (count, columns), lambda i, s: (0, 2 * jnp.where(i == 0, 1 - s[0], s[0]) + core(s))
-        )
-        shapes = [(blocks, width // (2 * blocks), columns)] * 4
-        out_specs = [fixed(shapes[0])] * 4
-    got_spec = pl.BlockSpec((1, width, columns), lambda i, s: (i, 0, 0))
-    if not keep:
-        out_specs, shapes = [got_spec], [(steps, width, columns)]
-    return pl.pallas_call(
-        functools.partial(outer_kernel, keep, second),
-        out_shape=[jax.ShapeDtypeStruct(s, BF16) for s in shapes],
-        grid_spec=pltpu.PrefetchScalarGridSpec(
-            num_scalar_prefetch=1,
-            grid=(steps,),
-            in_specs=[whole, whole, wide, wide] + ([got_spec] if keep else []),
-            out_specs=out_specs,
-        ),
-        cost_estimate=estimate(us),
-        compiler_params=pltpu.CompilerParams(vmem_limit_bytes=VMEM_BYTES),
-    )(place, *left, *right, *([got] if keep else []))
+        outs[block][0] = send[:rows]
+        outs[block][1] = kept[:rows]
+        at = lax.rem(block + dp, blocks)
+        outs[blocks][at] = send[rows:]
+        outs[blocks + 1][at] = kept[rows:]
+    rows = width // blocks
+    for index in range(2):
+        for block in range(blocks):
+            lines = slice(block * rows, (block + 1) * rows)
+            total = first_own[index, lines].astype(F32) + first_got[index, lines].astype(F32)
+            outs[blocks + 2 + index][lax.rem(block - dp + blocks, blocks)] = total.astype(BF16)
 
 
 def add_kernel(count, *refs):
@@ -374,33 +341,55 @@
         out[...] = total.astype(BF16)
 
 
-def add_arrays(arrays, count=1, us=0):
+def add_arrays(arrays, count=1, us=BIG):
     shape = arrays[0].shape[1:] if count > 1 else arrays[0].shape
     outs = whole_call(functools.partial(add_kernel, count), [(shape, BF16)] * count, [], arrays, us=us)
     return outs if count > 1 else outs[0]
 
 
-def core_add_kernel(place_ref, keep_ref, got_ref, send_low, send_high, keep_low, keep_high):
-    blocks, rows = send_low.shape[1], send_low.shape[2]
+def core_add_kernel(place_ref, keep_ref, got_ref, small_ref, small_got_ref, send_ref, mine_ref):
+    blocks = send_ref.shape[1]
+    rows = keep_ref.shape[1] // (2 * blocks)
     me = place_ref[3]
-    for matrix in range(2):
-        for block in range(blocks):
-            at = lax.rem(block - place_ref[2] + blocks, blocks)
-            start = 4 * block * rows
-            total = keep_ref[matrix, start : start + 4 * rows].astype(F32)
-            total = (total + got_ref[matrix, start : start + 4 * rows].astype(F32)).astype(BF16)
-            one, two = total[: 2 * rows], total[2 * rows :]
-            mine, other = jnp.where(me == 0, one, two), jnp.where(me == 0, two, one)
-            send_low[matrix, at] = other[:rows]
-            send_high[matrix, at] = other[rows:]
-            keep_low[matrix, at] = mine[:rows]
-            keep_high[matrix, at] = mine[rows:]
+    for block in range(blocks):
+        small = [
+            (small_ref[2 * block + at].astype(F32) + small_got_ref[2 * block + at].astype(F32)).astype(BF16)
+            for at in range(2)
+        ]
+        for matrix in range(2):
+            start = 2 * block * rows
+            total = keep_ref[matrix, start : start + 2 * rows].astype(F32)
+            total = (total + got_ref[matrix, start : start + 2 * rows].astype(F32)).astype(BF16)
+            one, two = total[:rows], total[rows:]
+            mine_ref[matrix, block, :rows] = jnp.where(me == 0, one, two)
+            send_ref[matrix, block, :rows] = jnp.where(me == 0, two, one)
+            mine_ref[matrix, block, rows:] = jnp.where(me == 0, small[0], small[1])
+            send_ref[matrix, block, rows:] = jnp.where(me == 0, small[1], small[0])
 
 
 def pair_add_kernel(place_ref, keep_ref, got_ref, send_ref, mine_ref):
     high = place_ref[0]
     send_ref[...] = (keep_ref[1 - high].astype(F32) + got_ref[1 - high].astype(F32)).astype(BF16)
     mine_ref[...] = (keep_ref[high].astype(F32) + got_ref[high].astype(F32)).astype(BF16)
+
+
+def plain_add_kernel(one, two, out):
+    out[...] = (one[...].astype(F32) + two[...].astype(F32)).astype(BF16)
+
+
+def sum_kernel(blocks, out):
+    total = blocks[0].astype(F32)
+    for block in range(1, blocks.shape[0]):
+        total = total + blocks[block].astype(F32)
+    out[...] = total.astype(BF16)
+
+
+def second_sum_kernel(early_keep, early_got, blocks, out):
+    low = blocks[0].astype(F32)
+    for block in range(1, blocks.shape[0]):
+        low = low + blocks[block].astype(F32)
+    high = early_keep[1].astype(F32) + early_got[...].astype(F32)
+    out[...] = jnp.concatenate([high, low], axis=0).T.astype(BF16)
 
 
 def lay_rows_kernel(rows, place_ref, own_ref, got_ref, out_ref, *rest):
@@ -429,8 +418,8 @@
     *refs,
 ):
     pieces = refs[:4]
-    q_ref, k_ref, v_ref, probs_ref, normed_ref, send_ref, keep_ref, ds_ref, gq_ref, gk_ref, gv_ref = refs[4:15]
-    grad_res_ref, gain_grad_ref, ga_ref, gat_ref, qt_ref, kt_ref = refs[15:]
+    q_ref, k_ref, v_ref, probs_ref, normed_ref, keep_ref, ds_ref, gq_ref, gk_ref, gv_ref = refs[4:14]
+    grad_res_ref, gain_grad_ref, send_ref, ga_ref, gat_ref, qt_ref, kt_ref = refs[14:]
     heads, tok, _ = probs_ref.shape
     size = residual_ref.shape[1] // heads
     low = place_ref[1]
@@ -490,9 +479,10 @@
     *refs,
 ):
     qk_pieces, vo_pieces = refs[:4], refs[4:8]
-    gq_ref, gk_ref, gv_ref, ds_ref, grad_res_ref, grad_tokens_ref, gain_grad_ref, diag_ref = refs[8:]
+    gq_ref, gk_ref, gv_ref, ds_ref, grad_res_ref, gain_two_ref, onehot_ref = refs[8:15]
+    turn_a_ref, turn_b_ref, logits_a_ref, logits_b_ref, grad_tokens_ref, small_ref = refs[15:]
     heads, tok, _ = ds_ref.shape
-    window = diag_ref.shape[1]
+    window, lanes = onehot_ref.shape
     grad = project_back(gq_ref[...], weight_halves(place_ref, 0, qk_pieces))
     grad = grad + project_back(gk_ref[...], weight_halves(place_ref, 1, qk_pieces))
     grad = grad + project_back(gv_ref[...], weight_halves(place_ref, 0, vo_pieces))
@@ -502,7 +492,12 @@
     scaled = grad * gain_ref[...]
     inner = jnp.mean(scaled * values, axis=-1, keepdims=True)
     grad_tokens_ref[...] = grad_res_ref[...] + factor * scaled - values * (factor * factor * factor) * inner
-    gain_grad_ref[...] = jnp.sum(grad * values * factor, axis=0, keepdims=True)
+    experts = small_ref.shape[0] - 2 - heads
+    small_ref[0:1, :] = jnp.sum(grad * values * factor, axis=0, keepdims=True)
+    small_ref[1:2, :] = gain_two_ref[...]
+    router = mm(turn_a_ref[...], logits_a_ref[...]) + mm(turn_b_ref[...], logits_b_ref[...])
+    small_ref[2 : 2 + experts, :] = router.T[:experts]
+    small_ref[2 + experts :, :] = jnp.zeros((heads, small_ref.shape[1]), F32)
     row = lax.broadcasted_iota(jnp.int32, (tok, tok), 0)
     column = lax.broadcasted_iota(jnp.int32, (tok, tok), 1)
     turned = (row + column == tok - 1).astype(BF16)
@@ -510,7 +505,9 @@
         flipped = mm(turned, ds_ref[head])
         wide = jnp.concatenate([flipped, jnp.zeros((tok, window - tok), F32)], axis=1)
         rolled = pltpu.roll(wide, window - tok + 1, 1, stride=1, stride_axis=0)
-        diag_ref[head : head + 1, :] = jnp.sum(rolled, axis=0, keepdims=True)
+        diagonal = jnp.broadcast_to(jnp.sum(rolled, axis=0, keepdims=True), (8, window))
+        table = jnp.dot(diagonal, onehot_ref[...], precision=lax.Precision.HIGHEST, preferred_element_type=F32)
+        small_ref[2 + experts + head : 3 + experts + head, 0:lanes] = table[0:1]
 
 
 def second_shared_kernel(place_ref, *refs):
@@ -657,7 +654,8 @@
 
         cot_a, cot_b = send(cotangent)
 
-    slot_back = mm_nt(jnp.concatenate([cot_a, cot_b], axis=0), w_out[0]).astype(BF16)
+    slot_cot = jnp.concatenate([cot_a, cot_b], axis=0)
+    slot_back = mm_nt(slot_cot, w_out[0]).astype(BF16)
 
     flat = (tok_rows, width)
     normed_one, queries, keys, probs = whole_call(
@@ -667,7 +665,7 @@
         [tokens, gain_one, *qk_pieces, bias],
         us=4,
     )
-    vo_pieces = spread(vo_mine, slot_back, normed_one)
+    vo_pieces = spread(after(vo_mine, qk_pieces[2]), slot_back, normed_one)
     values, attended, residual, normed_two, gate = whole_call(
         functools.partial(attend_kernel, experts),
         [(flat, BF16), (flat, BF16), (flat, F32), (flat, BF16), ((tok_rows, 1), F32)],
@@ -687,29 +685,24 @@
     )
     grad_own, grad_got = back(grad_a, grad_b)
 
-    hid, pre, rows, cots = (hid_a, hid_b), (pre_a, pre_b), (turn_a, turn_b), (cot_turn_a, cot_turn_b)
-    (second_out,) = outer_grad(True, place, cots, hid, dp_count, us=BIG)
-    second_in = rep_swap(second_out, 1)
-    (first_out,) = outer_grad(False, place, rows, pre, dp_count)
-    first_in = rep_swap(first_out, 1)
-    *early, second_send, second_keep = outer_grad(True, place, cots, hid, dp_count, second_in)
-    first_in = after(first_in, grad_got, second_send)
-    first_send, first_late, first_keep, first_last = outer_grad(False, place, rows, pre, dp_count, first_in, us=BIG)
-    grad_got = after(grad_got, second_send, first_send)
-
-    def z_sent(blocks):
-        return [blocks[0]] + [shift(blocks[step], "dp", step) for step in range(1, dp_count)]
-
-    early = z_sent(early)
-    second_got = rep_swap(second_send, 2)
-
-    square_weight = (2, width, width)
-    send_part, keep_part, grad_scores, grad_q, grad_k, grad_v, grad_res, grad_gain_two = whole_call(
+    quarter_columns = inner // 4
+    second_shape, first_shape = (dp_count, width, width // 2), (2, width, quarter_columns)
+    second_send, second_own, first_send, first_own = whole_call(
+        outer_kernel,
+        [(second_shape, BF16)] * 2 + [(first_shape, BF16)] * 2,
+        [place],
+        [cot_turn_a, cot_turn_b, hid_a, hid_b, turn_a, turn_b, pre_a, pre_b],
+        us=BIG,
+    )
+    second_in = rep_swap(after(second_send, grad_got), 1)
+    first_in = rep_swap(after(first_send, grad_got), 1)
+
+    keep_part, grad_scores, grad_q, grad_k, grad_v, grad_res, grad_gain_two, send_part = whole_call(
         attend_back_kernel,
-        [(square_weight, BF16)] * 2
-        + [(square, BF16)]
+        [((2, width, width), BF16), (square, BF16)]
         + [((width, tok_rows), BF16)] * 3
-        + [(flat, F32), ((1, width), F32)],
+        + [(flat, F32), ((1, width), F32)]
+        + [((2, width, width), BF16)],
         [place],
         [own_mask, grad_own, grad_got, residual, cotangent, gain_two, attended]
         + [*vo_pieces, queries, keys, values, probs, normed_one],
@@ -718,99 +711,110 @@
     )
     core_got = rep_swap(send_part, 1)
 
-    second_blocks = list(add_arrays([after(second_keep, grad_res), second_got], dp_count))
+    *early, second_send, second_keep, first_send, first_keep = whole_call(
+        core_sum_kernel,
+        [((2, width // 4, width // 2), BF16)] * dp_count
+        + [((dp_count, width // 4, width // 2), BF16)] * 2
+        + [((dp_count, width // dp_count, quarter_columns), BF16)] * 2,
+        [place],
+        [after(second_own, grad_res), second_in, first_own, first_in],
+        us=0,
+    )
+
+    def z_sent(blocks):
+        return [blocks[0]] + [shift(blocks[step], "dp", step) for step in range(1, dp_count)]
+
+    second_got = rep_swap(second_send, 2)
     first_got = rep_swap(after(first_send, second_got), 2)
-
-    grad_tokens, grad_gain_one, diag_grads = whole_call(
+    early_z = z_sent(early)
+
+    wide_onehot = jnp.pad(onehot, ((0, 0), (0, lanes - onehot.shape[1])))
+    grad_tokens, small = whole_call(
         finish_kernel,
-        [(flat, F32), ((1, width), F32), ((head_count, 2 * tok_rows), F32)],
+        [(flat, F32), ((2 + experts + head_count, width), F32)],
         [place],
         [tokens, gain_one, *qk_pieces, *vo_pieces, grad_q, grad_k, grad_v, grad_scores]
-        + [after(grad_res, second_blocks[0])],
-        us=0,
-    )
-
-    early_sum = add_arrays([after(early[0], grad_tokens)] + early[1:], us=BIG)
-    early_got = rep_swap(early_sum[0], 2)
-    second_blocks[0] = after(second_blocks[0], early_sum)
-    second_z = z_sent([second_blocks[0]] + [after(block, early_sum) for block in second_blocks[1:]])
-
-    keep_part = after(keep_part, early_sum)
+        + [after(grad_res, early[0]), grad_gain_two, wide_onehot, turn_a, turn_b, logits_a, logits_b],
+        us=BIG,
+    )
+
     if expert_axis == 2:
-        rows_half = shard_rows // 2
-        chunk_shape = (2, dp_count, rows_half, width)
-        send_low, send_high, keep_low, keep_high = whole_call(
-            core_add_kernel, [(chunk_shape, BF16)] * 4, [place], [keep_part, core_got], us=2
+        shards = dp_count * expert_axis
+        count = 2 + experts
+        small_rows = -(-(count + head_count) // 16) * 16
+        split = jnp.swapaxes(small[:count].reshape(count, shards, shard_rows), 0, 1).astype(BF16)
+        split = jnp.pad(split, ((0, 0), (0, 0), (0, width - shard_rows)))
+        table = jnp.broadcast_to(small[count:].astype(BF16)[None], (shards, head_count, width))
+        small = jnp.concatenate([split, table], axis=1)
+        small = jnp.pad(small, ((0, 0), (0, small_rows - count - head_count), (0, 0)))
+        cross = (2, dp_count, shard_rows + small_rows, width)
+        y_send, y_keep = whole_call(
+            core_add_kernel, [(cross, BF16)] * 2, [place], [keep_part, core_got, small, rep_swap(small, 1)], us=0
         )
-        low_got = shift(send_low, "expert", 1)
-        token = send_low
+        y_got = shift(y_send, "expert", 1)
+        token = y_send
     else:
-        part = add_pair(keep_part, core_got).reshape(2, dp_count, expert_axis, shard_rows, width)
+        part = add_pair(after(keep_part, grad_tokens), core_got)
+        part = part.reshape(2, dp_count, expert_axis, shard_rows, width)
         part = sum_over(part, "expert", 2)
         token = part
 
-    first_blocks = add_arrays([after(first_keep, token), first_got], dp_count)
-    first_z = z_sent(first_blocks)
-    late_got = rep_swap(after(first_late, first_got), 2)
-
+    (second_blocks,) = whole_call(
+        plain_add_kernel, [(second_keep.shape, BF16)], [], [after(second_keep, token), second_got], us=0
+    )
+    early_sum = add_arrays([after(early_z[0], second_blocks)] + early_z[1:], us=BIG)
+    early_got = rep_swap(early_sum[0], 2)
+    second_z = lax.all_to_all(after(second_blocks, early_sum), "dp", split_axis=0, concat_axis=0, tiled=True)
+    first_z = z_sent(add_arrays([after(first_keep, early_sum), first_got], dp_count, us=BIG))
     if expert_axis == 2:
-        pair_shape = [(chunk_shape[1:], BF16)] * 2
-        x_send, x_low = whole_call(
-            pair_add_kernel, pair_shape, [place], [after(keep_low, first_blocks[0]), low_got], us=1
+        x_send, x_keep = whole_call(
+            pair_add_kernel, [(cross[1:], BF16)] * 2, [place], [after(y_keep, first_z[0]), y_got], us=0
         )
-        high_got = shift(after(send_high, low_got), "expert", 1)
-        x_low_got = rep_swap(x_send, 2)
-        token = x_low
-
-    late_blocks = add_arrays([after(first_last, token), late_got], dp_count)
-    late_z = z_sent(late_blocks)
-
-    second_low = add_arrays([after(second_z[0], late_blocks[0])] + second_z[1:])
-    second_high = add_arrays([after(early_sum[1], second_low), early_got])
-    second_pieces = spread(jnp.concatenate([second_high, second_low], axis=0).T)
-
+        x_got = rep_swap(x_send, 2)
+        token = x_keep
+    else:
+        x_part = add_pair(pick(part, high, 0), rep_swap(pick(part, 1 - high, 0), 2))
+        token = x_part
+    made_own, made_got = back(made_a, after(made_b, token))
+    half_rows, half_columns = second_z.shape[1:]
+    (second_sum,) = whole_call(
+        second_sum_kernel,
+        [((half_columns, 2 * half_rows), BF16)],
+        [],
+        [after(early_sum, token), early_got, second_z],
+        us=0,
+    )
+    second_pieces = spread(second_sum)
     if expert_axis == 2:
-        low_blocks = add_arrays([after(x_low, second_pieces[0]), x_low_got], dp_count)
-        low_z = z_sent(low_blocks)
-        x_send, x_high = whole_call(
-            pair_add_kernel, pair_shape, [place], [after(keep_high, low_blocks[0]), high_got], us=1
+        (x_sum,) = whole_call(
+            plain_add_kernel, [(cross[1:], BF16)], [], [after(x_keep, second_sum), x_got], us=0
         )
-        x_high_got = rep_swap(x_send, 2)
-        first_low = add_arrays([after(first_z[0], x_high)] + first_z[1:])
-        high_blocks = add_arrays([after(x_high, first_low), x_high_got], dp_count)
-        high_z = z_sent(high_blocks)
-        token = x_high
-        first_high = add_arrays([after(late_z[0], high_blocks[0])] + late_z[1:])
-        first_pieces = spread(jnp.concatenate([first_low, first_high], axis=0))
-        attn_low = add_arrays([after(low_z[0], first_pieces[0])] + low_z[1:])
-        attn_high = add_arrays([after(high_z[0], attn_low)] + high_z[1:])
-        attn_pieces = spread(jnp.concatenate([attn_low, attn_high], axis=0))
-    else:
-        first_low = add_arrays([first_z[0]] + first_z[1:])
-        first_high = add_arrays([late_z[0]] + late_z[1:])
-        first_pieces = spread(jnp.concatenate([first_low, first_high], axis=0))
-        x_part = add_pair(pick(part, high, 0), rep_swap(pick(part, 1 - high, 0), 2))
-        attn_pieces = spread(sum_over(x_part, "dp", 0))
-        token = x_part
+        attn_z = lax.all_to_all(x_sum, "dp", split_axis=0, concat_axis=0, tiled=True)
+        token = x_sum
     (grad_w_out,) = whole_call(
         second_shared_kernel, [((1, inner // dp_count, width), F32)], [place], second_pieces
     )
+    first_sum = add_arrays([after(first_z[0], token, made_got)] + first_z[1:], us=0)
+    first_pieces = spread(first_sum)
+    if expert_axis == 2:
+        (attn_sum,) = whole_call(
+            sum_kernel, [(cross[2:], BF16)], [], [after(attn_z, first_sum)], us=0
+        )
+        attn_pieces = spread(attn_sum[:shard_rows])
+        small = attn_sum[shard_rows:].astype(F32)
+        table_total = small[2 + experts : 2 + experts + head_count, : rel_table.shape[0]].T
+        small = small[: 2 + experts, :shard_rows]
+    else:
+        attn_pieces = spread(sum_over(x_part, "dp", 0))
+        small = lax.psum(small, ("rep", "dp", "expert"))
+        table_total = small[2 + experts :, : rel_table.shape[0]].T
+        row_start = (dp * expert_axis + me) * shard_rows
+        small = lax.dynamic_slice_in_dim(small[: 2 + experts], row_start, shard_rows, 1)
     (grad_w_in,) = whole_call(first_shared_kernel, [((1, width // dp_count, inner), F32)], [place], first_pieces)
     owned = whole_call(attention_shared_kernel, [((shard_rows, width), F32)] * 4, [place], attn_pieces)
 
-    made_own, made_got = back(made_a, after(made_b, token))
     expert_rows = jnp.where(own_mask > 0, made_own, made_got).astype(F32)
     mixed = (residual + gate * expert_rows).astype(BF16)
-    grad_router = mm(turn_a, logits_a) + mm(turn_b, logits_b)
-    grad_router = grad_router[:, :experts]
-    grad_table = jnp.dot(onehot.T, diag_grads.T, precision=lax.Precision.HIGHEST)
-    small = jnp.concatenate([grad_gain_one, grad_gain_two, grad_router.T], axis=0)
-    packed = jnp.concatenate([small.reshape(-1), grad_table.reshape(-1)])
-    packed = all_sum(packed, (early_sum, first_blocks[0], late_blocks[0]))
-    row_start = (dp * expert_axis + me) * shard_rows
-    small = packed[: (2 + experts) * width].reshape(2 + experts, width)
-    small = lax.dynamic_slice_in_dim(small, row_start, shard_rows, 1)
-    table_total = packed[(2 + experts) * width :].reshape(rel_table.shape)
     return (
         mixed,
         grad_tokens,
@@ -827,19 +831,6 @@
     )
 
 
-def all_sum(values, tokens):
-    for axis, token in zip(("rep", "expert", "dp"), tokens, strict=True):
-        count = lax.axis_size(axis)
-        if count > 4:
-            values = lax.psum(values, axis)
-            continue
-        total = values = after(values, token)
-        for step in range(1, count):
-            total = total + shift(values, axis, step)
-        values = total
-    return values
-
-
 def solution(mesh):
     rows = P(("rep", "dp", "expert"), None)
     split = P(("dp", "expert"), None)

time: 263 us -> 241 us (0.916)
  starting transfers between devices: 70.9 us -> 52.2 us
  local copies, waits for them, and re-layouts: 38.5 us -> 29.6 us
  Pallas kernels: 69.6 us -> 72.7 us
  waiting for transfers between devices: 62.8 us -> 65.5 us
    ppermute x39 -> x19, starting transfers between devices: 54 us -> 27.4 us  [shift(): lax.ppermute(values, axis, [(i, (i + step) % count) for i in range(count)])]
    pallas_call x25 -> x21, Pallas kernels: 38.8 us -> 58.4 us  [whole_call(): pl.pallas_call(kernel, out_shape=[jax.ShapeDtypeStruct(s, d) for s, d in...]
    ppermute x24 -> x23, waiting for transfers between devices: 28.8 us -> 41.7 us  [rep_swap(): return lax.ppermute(values, 'rep', [(i, i ^ bit) for i in range(count)])]
    pallas_call x4 -> x0, Pallas kernels: 12.3 us -> none  [outer_grad(): pl.pallas_call(functools.partial(outer_kernel, keep, second), out_shape=[...]
    all_to_all x0 -> x2, starting transfers between devices: none -> 12 us  [the longest x1 7.79 us: local(): lax.all_to_all(after(second_blocks, early_sum), 'dp', split_axis=0, conca...]
    ppermute x39 -> x19, waiting for transfers between devices: 33.9 us -> 23.8 us  [shift(): lax.ppermute(values, axis, [(i, (i + step) % count) for i in range(count)])]
    unnamed x146 -> x125, local copies, waits for them, and re-layouts: 34.2 us -> 26.5 us
    pallas_call x2, Pallas kernels: 18.5 us -> 14.3 us  [run_expert(): pl.pallas_call(functools.partial(expert_kernel, experts), out_shape=[jax....]
  transfers between devices with their start and end apart: 63 -> 44, of which waited for: 19 -> 14; matrix products, arithmetic and copies ran while one was open for 8% -> 8% of each run, Pallas kernels for 20% -> 25%
where the time goes in v1:
time: 241 us; the launch traced here: 237 us
  Pallas kernels  72.7 us (30%)
  waiting for transfers between devices  65.5 us (27%)
  starting transfers between devices  52.2 us (22%)
  local copies, waits for them, and re-layouts  29.6 us (12%)
  other arithmetic  8.32 us (3%)
  matrix products  7.44 us (3%)
    pallas_call x21, Pallas kernels, whole_call(): pl.pallas_call(kernel, out_shape=[jax.ShapeDtypeStruct(s, d) for s, d in...  58.4 us
    ppermute x23, waiting for transfers between devices, rep_swap(): return lax.ppermute(values, 'rep', [(i, i ^ bit) for i in range(count)])  41.7 us
    ppermute x19, starting transfers between devices, shift(): lax.ppermute(values, axis, [(i, (i + step) % count) for i in range(count)])  27.4 us
    unnamed x125, local copies, waits for them, and re-layouts  26.5 us
    ppermute x19, waiting for transfers between devices, shift(): lax.ppermute(values, axis, [(i, (i + step) % count) for i in range(count)])  23.8 us
    pallas_call x2, Pallas kernels, run_expert(): pl.pallas_call(functools.partial(expert_kernel, experts), out_shape=[jax....  14.3 us
    ppermute x23, starting transfers between devices, rep_swap(): return lax.ppermute(values, 'rep', [(i, i ^ bit) for i in range(count)])  12.8 us
    all_to_all x1, starting transfers between devices, local(): lax.all_to_all(after(second_blocks, early_sum), 'dp', split_axis=0, conca...  7.79 us
  transfers between devices with their start and end apart: 44, of which 14 were waited for; matrix products, arithmetic and copies ran while one was open for 8% of the time, Pallas kernels for 25%

profile of v1, /device:TPU:0, one launch (start us, length us, event | category | flops | bytes accessed | tf_op | source)
XLA Modules:
  0.0 237.2 jit_solution(1349008003075563552)
XLA Ops:
  2.4 5.1 %collective-permute-start.2 = (bf16[112,384]{1,0:T(8,128)(2,1)S(1)}, bf16[112,384]{1,0:T(8,128)(2,1)S(1)}, u32[]{:S(2)}, u32[]{:S(2)}) collective-permute-start(bf16[112,384]{1,0:T(8,128)(2,1)S(1)} %get-tuple-element.177), channel_id=1, source_target_pairs={{0,6},{2,0},{4,2},{6,4},{1,7},{3,1},{5,3},{7,5},{8,14},{10,8},{12,... | collective-permute-start | bytes 258056 | tf_op jit(solution)/shard_map/ppermute | solution.py:42
  9.4 3.4 %collective-permute-start.7 = (bf16[96,384]{1,0:T(8,128)(2,1)S(1)}, bf16[96,384]{1,0:T(8,128)(2,1)S(1)}, u32[]{:S(2)}, u32[]{:S(2)}) collective-permute-start(bf16[96,384]{1,0:T(8,128)(2,1)S(1)} %dynamic-slice_select_fusion), channel_id=1, source_target_pairs={{0,2},{2,4},{4,6},{6,0},{1,3},{3,5},{5,7},{7,1},{8,10},{10,12},{12... | collective-permute-start | bytes 221192 | tf_op jit(solution)/shard_map/ppermute | solution.py:42
  17.1 1.6 copy-done.56
  18.8 2.4 %collective-permute-start.9 = (bf16[96,384]{1,0:T(8,128)(2,1)S(1)}, bf16[96,384]{1,0:T(8,128)(2,1)S(1)}, u32[]{:S(2)}, u32[]{:S(2)}) collective-permute-start(bf16[96,384]{1,0:T(8,128)(2,1)S(1)} %dynamic-slice_select_fusion), channel_id=1, source_target_pairs={{0,6},{2,0},{4,2},{6,4},{1,7},{3,1},{5,3},{7,5},{8,14},{10,8},{12,... | collective-permute-start | bytes 221192 | tf_op jit(solution)/shard_map/ppermute | solution.py:42
  21.3 1.6 collective-permute-start.3
  24.8 7.5 %collective-permute-done.3.got_ref = bf16[4,112,384]{2,1,0:T(8,128)(2,1)S(1)} collective-permute-done((bf16[4,112,384]{2,1,0:T(8,128)(2,1)S(1)}, bf16[4,112,384]{2,1,0:T(8,128)(2,1)S(1)}, u32[]{:S(2)}, u32[]{:S(2)}) %collective-permute-start.3) | collective-permute-done | bytes 344096 | tf_op jit(solution)/shard_map/ppermute | solution.py:42
  33.0 1.6 collective-permute-start.5
  36.1 1.5 collective-permute-start.13
  38.5 6.4 %collective-permute-done.5.refs_2_ = bf16[768,384]{1,0:T(8,128)(2,1)} collective-permute-done((bf16[768,384]{1,0:T(8,128)(2,1)S(1)}, bf16[768,384]{1,0:T(8,128)(2,1)}, u32[]{:S(2)}, u32[]{:S(2)}) %collective-permute-start.5) | collective-permute-done | bytes 589856 | tf_op jit(solution)/shard_map/ppermute | solution.py:37
  44.8 1.5 collective-permute-start.12
  46.4 7.1 %fusion.2.back_ref = bf16[512,3072]{1,0:T(8,128)(2,1)} fusion(bf16[1,3072,768]{2,1,0:T(8,128)(2,1)} %second_ref.3, bf16[256,768]{1,0:T(8,128)(2,1)S(1)} %collective-permute-done.13.cot_ref, bf16[256,768]{1,0:T(8,128)(2,1)S(1)} %get-tuple-element.174.cot_ref), kind=kOutput, calls=%fused_computation.2 | convolution fusion | flops 2419064832 | bytes 8650752 | tf_op jit(solution)/shard_map/dot_general | solution.py:70
  54.0 4.0 %shard_map.231 = (bf16[256,768]{1,0:T(8,128)(2,1)S(1)}, bf16[256,768]{1,0:T(8,128)(2,1)S(1)}, bf16[256,768]{1,0:T(8,128)(2,1)S(1)}, bf16[12,256,256]{2,1,0:T(8,128)(2,1)S(1)}) custom-call(s32[4]{0:T(128)S(1)} %pad_add_fusion.place_ref, bf16[256,768]{1,0:T(8,128)(2,1)S(1)} %copy-done.48, f32[1,768]{1,0:T(1,128)S(1)} %reshape.93.gain_ref, ...), custom_call_target="tpu_custom_call" | custom-call | flops 4000000000 | bytes 4000001 | tf_op jit(solution)/shard_map/pallas_call | solution.py:83
  65.5 3.7 %shard_map.233 = (bf16[256,768]{1,0:T(8,128)(2,1)S(1)}, bf16[256,768]{1,0:T(8,128)(2,1)S(1)}, f32[256,768]{1,0:T(8,128)S(1)}, bf16[256,768]{1,0:T(8,128)(2,1)S(1)}, f32[256,1]{1,0:T(8,128)S(1)}) custom-call(s32[4]{0:T(128)S(1)} %pad_add_fusion.place_ref, bf16[256,768]{1,0:T(8,128)(2,1)S(1)} %copy-done.49, bf16[256,768]{1,0:T(8,128)(2,1)S(1)} %copy-done.19, ...), custom_call_target="tpu_custom_call" | custom-call | flops 4000000000 | bytes 4000001 | tf_op jit(solution)/shard_map/pallas_call | solution.py:83
  69.9 2.5 %collective-permute-start.15 = (bf16[256,768]{1,0:T(8,128)(2,1)S(1)}, bf16[256,768]{1,0:T(8,128)(2,1)S(1)}, u32[]{:S(2)}, u32[]{:S(2)}) collective-permute-start(bf16[256,768]{1,0:T(8,128)(2,1)S(1)} %get-tuple-element.100.rows_ref), channel_id=1, source_target_pairs={{0,1},{1,0},{2,3},{3,2},{4,5},{5,4},{6,7},{7,6},{8,9},{9,8},{10,11... | collective-permute-start | bytes 1179656 | tf_op jit(solution)/shard_map/ppermute | solution.py:42
  72.4 2.3 copy-done.37
  74.8 2.3 copy-done.39
  77.1 6.7 %shard_map.234 = (bf16[256,3072]{1,0:T(8,128)(2,1)S(1)}, bf16[256,3072]{1,0:T(8,128)(2,1)S(1)}, bf16[256,768]{1,0:T(8,128)(2,1)S(1)}, bf16[256,768]{1,0:T(8,128)...) custom-call(s32[1]{0:T(128)} %bitcast.3.me_ref, ...), custom_call_target="tpu_custom_call" | custom-call | flops 9000000512 | bytes 9000001 | tf_op jit(solution)/shard_map/pallas_call | solution.py:260
  84.6 2.3 copy-done.38
  86.9 2.3 copy-done.40
  89.2 7.6 %shard_map.235 = (bf16[256,3072]{1,0:T(8,128)(2,1)S(1)}, bf16[256,3072]{1,0:T(8,128)(2,1)S(1)}, bf16[256,768]{1,0:T(8,128)(2,1)}, bf16[256,768]{1,0:T(8,128)(2,1...) custom-call(s32[1]{0:T(128)} %bitcast.3.me_ref, ...), custom_call_target="tpu_custom_call" | custom-call | flops 9000000512 | bytes 9000001 | tf_op jit(solution)/shard_map/pallas_call | solution.py:260
  97.0 6.5 %shard_map.237 = (bf16[4,768,384]{2,1,0:T(8,128)(2,1)S(1)}, bf16[4,768,384]{2,1,0:T(8,128)(2,1)S(1)}, bf16[2,768,768]{2,1,0:T(8,128)(2,1)S(1)}, bf16[2,768,768]{2,1,0:T(8,128)(2,1)S(1)}) custom-call(s32[4]{0:T(128)S(1)} %pad_add_fusion.place_ref, bf16[768,256]{1,0:T(8,128)(2,1)S(1)} %get-tuple-element.116.refs_0_, ...), custom_call_target="tpu_custom_call" | custom-call | flops 30000001024 | bytes 30000000 | tf_op jit(solution)/shard_map/pallas_call | solution.py:83
  103.5 4.3 %collective-permute-done.16.got_ref = bf16[256,768]{1,0:T(8,128)(2,1)S(1)} collective-permute-done((bf16[256,768]{1,0:T(8,128)(2,1)S(1)}, bf16[256,768]{1,0:T(8,128)(2,1)S(1)}, u32[]{:S(2)}, u32[]{:S(2)}) %collective-permute-start.16) | collective-permute-done | bytes 393248 | tf_op jit(solution)/shard_map/ppermute | solution.py:42
  108.5 11.3 %shard_map.236 = (bf16[2,768,768]{2,1,0:T(8,128)(2,1)S(1)}, bf16[12,256,256]{2,1,0:T(8,128)(2,1)S(1)}, bf16[768,256]{1,0:T(8,128)(2,1)S(1)}, bf16[768,256]{1,0:T...) custom-call(s32[4]{0:T(128)S(1)} %pad_add_fusion.place_ref, ...), custom_call_target="tpu_custom_call" | custom-call | flops 1 | bytes 1 | tf_op jit(solution)/shard_map/pallas_call | solution.py:83
  119.9 2.9 %shard_map.238 = (bf16[2,192,384]{2,1,0:T(8,128)(2,1)S(1)}, bf16[2,192,384]{2,1,0:T(8,128)(2,1)S(1)}, bf16[2,192,384]{2,1,0:T(8,128)(2,1)S(1)}, bf16[2,192,384]{...) custom-call(s32[4]{0:T(128)S(1)} %pad_add_fusion.place_ref, ...), custom_call_target="tpu_custom_call" | custom-call | flops 1 | bytes 1 | tf_op jit(solution)/shard_map/pallas_call | solution.py:83
  123.5 9.2 %shard_map.239 = (f32[256,768]{1,0:T(8,128)}, f32[16,768]{1,0:T(8,128)S(1)}) custom-call(s32[4]{0:T(128)S(1)} %pad_add_fusion.place_ref, bf16[256,768]{1,0:T(8,128)(2,1)S(1)} %copy-done.50, f32[1,768]{1,0:T(1,128)S(1)} %reshape.93.gain_ref, bf16[768,384]{1,0:T(8,128)(2,1)S(1)} %copy-done.45, bf16[768,384]{1,0:T(8,128)(2,1)} %collective-permute-done.4.refs_1_, ...), custom_call_target="tpu_custom_call" | custom-call | flops 30000001024 | bytes 30000000 | tf_op jit(solution)/shard_map/pallas_call | solution.py:83
  132.9 2.3 collective-permute-start.23
  135.2 1.6 collective-permute-start.24
  136.9 1.4 collective-permute-done.20.small_got_ref
  138.3 3.5 %shard_map.240 = (bf16[2,4,112,768]{3,2,1,0:T(8,128)(2,1)}, bf16[2,4,112,768]{3,2,1,0:T(8,128)(2,1)S(1)}) custom-call(s32[4]{0:T(128)S(1)} %pad_add_fusion.place_ref, bf16[2,768,768]{2,1,0:T(8,128)(2,1)S(1)} %get-tuple-element.109.keep_ref, bf16[2,768,768]{2,1,0:T(8,128)(2,1)} %collective-permute-done.17.got_ref, bf16[8,16,768]{2,1,0:T(8,128)(2,1)S(1)} %fusion.9.small_ref, ...), custom_call_target="tpu_custom_call" | custom-call | flops 1 | bytes 1 | tf_op jit(solution)/shard_map/pallas_call | solution.py:83
  143.2 2.0 shard_map.241
  146.5 10.1 %collective-permute-done.23.refs_2_ = bf16[2,192,384]{2,1,0:T(8,128)(2,1)S(1)} collective-permute-done((bf16[2,192,384]{2,1,0:T(8,128)(2,1)}, bf16[2,192,384]{2,1,0:T(8,128)(2,1)S(1)}, u32[]{:S(2)}, u32[]{:S(2)}) %collective-permute-start.23) | collective-permute-done | bytes 294944 | tf_op jit(solution)/shard_map/ppermute | solution.py:42
  157.4 7.8 %all-to-all-start = ((bf16[4,192,384]{2,1,0:T(8,128)(2,1)}), bf16[4,192,384]{2,1,0:T(8,128)(2,1)S(1)}, u32[]{:S(2)}, u32[]{:S(2)}) async-start(bf16[4,192,384]{2,1,0:T(8,128)(2,1)} %shard_map.241), calls=%async_computation | async-start | bytes 1179648 | tf_op jit(solution)/shard_map/all_to_all | solution.py:767
  165.2 8.0 %collective-permute-done.25.refs_1_ = bf16[4,192,768]{2,1,0:T(8,128)(2,1)} collective-permute-done((bf16[4,192,768]{2,1,0:T(8,128)(2,1)}, bf16[4,192,768]{2,1,0:T(8,128)(2,1)}, u32[]{:S(2)}, u32[]{:S(2)}) %collective-permute-start.25) | collective-permute-done | bytes 1179680 | tf_op jit(solution)/shard_map/ppermute | solution.py:37
  174.5 2.2 shard_map.243
  176.8 1.6 shard_map.244
  180.6 1.7 collective-permute-start.27
  182.9 1.5 collective-permute-start.31
  184.3 13.8 %collective-permute-done.28.early_got = bf16[192,384]{1,0:T(8,128)(2,1)S(1)} collective-permute-done((bf16[192,384]{1,0:T(8,128)(2,1)S(1)}, bf16[192,384]{1,0:T(8,128)(2,1)S(1)}, u32[]{:S(2)}, u32[]{:S(2)}) %collective-permute-start.28) | collective-permute-done | bytes 147488 | tf_op jit(solution)/shard_map/ppermute | solution.py:37
  203.2 4.2 %all-to-all-start.1 = ((bf16[4,112,768]{2,1,0:T(8,128)(2,1)}), bf16[4,112,768]{2,1,0:T(8,128)(2,1)S(1)}, u32[]{:S(2)}, u32[]{:S(2)}) async-start(bf16[4,112,768]{2,1,0:T(8,128)(2,1)} %shard_map.246), calls=%async_computation.1 | async-start | bytes 1376256 | tf_op jit(solution)/shard_map/all_to_all | solution.py:792
  211.2 1.3 collective-permute-start.37
  212.5 2.5 %collective-permute-done.40.refs_2_ = bf16[384,384]{1,0:T(8,128)(2,1)S(1)} collective-permute-done((bf16[384,384]{1,0:T(8,128)(2,1)}, bf16[384,384]{1,0:T(8,128)(2,1)S(1)}, u32[]{:S(2)}, u32[]{:S(2)}) %collective-permute-start.40) | collective-permute-done | bytes 294944 | tf_op jit(solution)/shard_map/ppermute | solution.py:37
  216.6 4.2 %collective-permute-done.37.refs_2_ = bf16[192,768]{1,0:T(8,128)(2,1)S(1)} collective-permute-done((bf16[192,768]{1,0:T(8,128)(2,1)S(1)}, bf16[192,768]{1,0:T(8,128)(2,1)S(1)}, u32[]{:S(2)}, u32[]{:S(2)}) %collective-permute-start.37) | collective-permute-done | bytes 294944 | tf_op jit(solution)/shard_map/ppermute | solution.py:37
  220.8 2.0 add_convert_fusion
  222.7 2.7 %shard_map.251 = f32[1,768,768]{2,1,0:T(8,128)} custom-call(s32[4]{0:T(128)S(1)} %pad_add_fusion.place_ref, bf16[384,384]{1,0:T(8,128)(2,1)S(1)} %copy-done.32, bf16[384,384]{1,0:T(8,128)(2,1)S(1)} %collective-permute-done.39.refs_1_, bf16[384,384]{1,0:T(8,128)(2,1)S(1)} %collective-permute-done.40.refs_2_, bf16[384,384]{1,0:T(8,128)(2,1)} %collective-permute-done.41.refs_3_), custom_call_target="tpu_custom_call" | custom-call | flops 2000000000 | bytes 2000001 | tf_op jit(solution)/shard_map/pallas_call | solution.py:83
  225.4 2.2 shard_map.250
  227.8 1.3 collective-permute-start.34
  230.4 3.7 %collective-permute-done.34.refs_2_ = bf16[96,768]{1,0:T(8,128)(2,1)S(1)} collective-permute-done((bf16[96,768]{1,0:T(8,128)(2,1)S(1)}, bf16[96,768]{1,0:T(8,128)(2,1)S(1)}, u32[]{:S(2)}, u32[]{:S(2)}) %collective-permute-start.34) | collective-permute-done | bytes 147488 | tf_op jit(solution)/shard_map/ppermute | solution.py:37
  235.5 1.6 shard_map.249
  (226 shorter events, 44.6 us)
Async XLA Ops:
  2.4 16.4 %collective-permute-start.2 = (bf16[112,384]{1,0:T(8,128)(2,1)S(1)}, bf16[112,384]{1,0:T(8,128)(2,1)S(1)}, u32[]{:S(2)}, u32[]{:S(2)}) collective-permute-start(bf16[112,384]{1,0:T(8,128)(2,1)S(1)} %get-tuple-element.177), channel_id=1, source_target_pairs={{0,6},{2,0},{4,2},{6,4},{1,7},{3,1},{5,3},{7,5},{8,14},{10,8},{12,... | collective-permute-start | bytes 258056 | tf_op jit(solution)/shard_map/ppermute | solution.py:42
  7.5 13.7 %collective-permute-start = (bf16[112,384]{1,0:T(8,128)(2,1)S(1)}, bf16[112,384]{1,0:T(8,128)(2,1)S(1)}, u32[]{:S(2)}, u32[]{:S(2)}) collective-permute-start(bf16[112,384]{1,0:T(8,128)(2,1)S(1)} %get-tuple-element.177), channel_id=1, source_target_pairs={{0,2},{2,4},{4,6},{6,0},{1,3},{3,5},{5,7},{7,1},{8,10},{10,12},{12... | collective-permute-start | bytes 258056 | tf_op jit(solution)/shard_map/ppermute | solution.py:42
  7.5 13.7 %collective-permute-start.1 = (bf16[112,384]{1,0:T(8,128)(2,1)S(1)}, bf16[112,384]{1,0:T(8,128)(2,1)S(1)}, u32[]{:S(2)}, u32[]{:S(2)}) collective-permute-start(bf16[112,384]{1,0:T(8,128)(2,1)S(1)} %get-tuple-element.177), channel_id=1, source_target_pairs={{0,4},{2,6},{4,0},{6,2},{1,5},{3,7},{5,1},{7,3},{8,12},{10,14},{12... | collective-permute-start | bytes 258056 | tf_op jit(solution)/shard_map/ppermute | solution.py:42
  9.4 14.2 %collective-permute-start.7 = (bf16[96,384]{1,0:T(8,128)(2,1)S(1)}, bf16[96,384]{1,0:T(8,128)(2,1)S(1)}, u32[]{:S(2)}, u32[]{:S(2)}) collective-permute-start(bf16[96,384]{1,0:T(8,128)(2,1)S(1)} %dynamic-slice_select_fusion), channel_id=1, source_target_pairs={{0,2},{2,4},{4,6},{6,0},{1,3},{3,5},{5,7},{7,1},{8,10},{10,12},{12... | collective-permute-start | bytes 221192 | tf_op jit(solution)/shard_map/ppermute | solution.py:42
  12.9 10.8 %collective-permute-start.8 = (bf16[96,384]{1,0:T(8,128)(2,1)S(1)}, bf16[96,384]{1,0:T(8,128)(2,1)S(1)}, u32[]{:S(2)}, u32[]{:S(2)}) collective-permute-start(bf16[96,384]{1,0:T(8,128)(2,1)S(1)} %dynamic-slice_select_fusion), channel_id=1, source_target_pairs={{0,4},{2,6},{4,0},{6,2},{1,5},{3,7},{5,1},{7,3},{8,12},{10,14},{12... | collective-permute-start | bytes 221192 | tf_op jit(solution)/shard_map/ppermute | solution.py:42
  18.8 4.9 %collective-permute-start.9 = (bf16[96,384]{1,0:T(8,128)(2,1)S(1)}, bf16[96,384]{1,0:T(8,128)(2,1)S(1)}, u32[]{:S(2)}, u32[]{:S(2)}) collective-permute-start(bf16[96,384]{1,0:T(8,128)(2,1)S(1)} %dynamic-slice_select_fusion), channel_id=1, source_target_pairs={{0,6},{2,0},{4,2},{6,4},{1,7},{3,1},{5,3},{7,5},{8,14},{10,8},{12,... | collective-permute-start | bytes 221192 | tf_op jit(solution)/shard_map/ppermute | solution.py:42
  21.3 11.1 %collective-permute-start.3 = (bf16[4,112,384]{2,1,0:T(8,128)(2,1)S(1)}, bf16[4,112,384]{2,1,0:T(8,128)(2,1)S(1)}, u32[]{:S(2)}, u32[]{:S(2)}) collective-permute-start(bf16[4,112,384]{2,1,0:T(8,128)(2,1)S(1)} %pad_maximum_fusion.own_ref), channel_id=1, source_target_pairs={{0,1},{1,0},{2,3},{3,2},{4,5},{5,4},{6,7},{7,6},{8,9},{9,8},{10,11... | collective-permute-start | bytes 1032200 | tf_op jit(solution)/shard_map/ppermute | solution.py:42
  23.7 12.4 %collective-permute-start.10 = (bf16[4,96,384]{2,1,0:T(8,128)(2,1)S(1)}, bf16[4,96,384]{2,1,0:T(8,128)(2,1)S(1)}, u32[]{:S(2)}, u32[]{:S(2)}) collective-permute-start(bf16[4,96,384]{2,1,0:T(8,128)(2,1)S(1)} %pad_maximum_fusion.1.own_ref), channel_id=1, source_target_pairs={{0,1},{1,0},{2,3},{3,2},{4,5},{5,4},{6,7},{7,6},{8,9},{9,8},{10,11... | collective-permute-start | bytes 884744 | tf_op jit(solution)/shard_map/ppermute | solution.py:42
  33.0 11.8 %collective-permute-start.5 = (bf16[768,384]{1,0:T(8,128)(2,1)S(1)}, bf16[768,384]{1,0:T(8,128)(2,1)}, u32[]{:S(2)}, u32[]{:S(2)}) collective-permute-start(bf16[768,384]{1,0:T(8,128)(2,1)S(1)} %get-tuple-element.92.refs_0_), channel_id=1, source_target_pairs={{0,16},{8,24},{16,0},{24,8},{1,17},{9,25},{17,1},{25,9},{2,18},{10... | collective-permute-start | bytes 1769480 | tf_op jit(solution)/shard_map/ppermute | solution.py:37
  36.1 10.2 %collective-permute-start.13 = (bf16[256,768]{1,0:T(8,128)(2,1)}, bf16[256,768]{1,0:T(8,128)(2,1)S(1)}, u32[]{:S(2)}, u32[]{:S(2)}) collective-permute-start(bf16[256,768]{1,0:T(8,128)(2,1)} %get-tuple-element.95), channel_id=1, source_target_pairs={{0,1},{1,0},{2,3},{3,2},{4,5},{5,4},{6,7},{7,6},{8,9},{9,8},{10,11... | collective-permute-start | bytes 1179656 | tf_op jit(solution)/shard_map/ppermute | solution.py:42
  38.2 24.2 %copy-start.10 = (bf16[768,384]{1,0:T(8,128)(2,1)}, bf16[768,384]{1,0:T(8,128)(2,1)S(1)}, u32[]{:S(2)}) copy-start(bf16[768,384]{1,0:T(8,128)(2,1)S(1)} %shard_map.232.refs_0_.refs_4_) | copy-start | bytes 1769476
  38.2 15.7 %collective-permute-start.4 = (bf16[768,384]{1,0:T(8,128)(2,1)S(1)}, bf16[768,384]{1,0:T(8,128)(2,1)}, u32[]{:S(2)}, u32[]{:S(2)}) collective-permute-start(bf16[768,384]{1,0:T(8,128)(2,1)S(1)} %get-tuple-element.92.refs_0_), channel_id=1, source_target_pairs={{0,8},{8,0},{16,24},{24,16},{1,9},{9,1},{17,25},{25,17},{2,10},{10... | collective-permute-start | bytes 1769480 | tf_op jit(solution)/shard_map/ppermute | solution.py:37
  44.8 15.5 %collective-permute-start.12 = (bf16[768,384]{1,0:T(8,128)(2,1)S(1)}, bf16[768,384]{1,0:T(8,128)(2,1)S(1)}, u32[]{:S(2)}, u32[]{:S(2)}) collective-permute-start(bf16[768,384]{1,0:T(8,128)(2,1)S(1)} %shard_map.232.refs_0_.refs_4_), channel_id=1, source_target_pairs={{0,16},{8,24},{16,0},{24,8},{1,17},{9,25},{17,1},{25,9},{2,18},{10... | collective-permute-start | bytes 1769480 | tf_op jit(solution)/shard_map/ppermute | solution.py:37
  46.3 7.7 %collective-permute-start.6 = (bf16[768,384]{1,0:T(8,128)(2,1)}, bf16[768,384]{1,0:T(8,128)(2,1)S(1)}, u32[]{:S(2)}, u32[]{:S(2)}) collective-permute-start(bf16[768,384]{1,0:T(8,128)(2,1)} %collective-permute-done.5.refs_2_), channel_id=1, source_target_pairs={{0,8},{8,0},{16,24},{24,16},{1,9},{9,1},{17,25},{25,17},{2,10},{10... | collective-permute-start | bytes 1769480 | tf_op jit(solution)/shard_map/ppermute | solution.py:37
  53.5 8.0 %collective-permute-start.11 = (bf16[768,384]{1,0:T(8,128)(2,1)S(1)}, bf16[768,384]{1,0:T(8,128)(2,1)}, u32[]{:S(2)}, u32[]{:S(2)}) collective-permute-start(bf16[768,384]{1,0:T(8,128)(2,1)S(1)} %shard_map.232.refs_0_.refs_4_), channel_id=1, source_target_pairs={{0,8},{8,0},{16,24},{24,16},{1,9},{9,1},{17,25},{25,17},{2,10},{10... | collective-permute-start | bytes 1769480 | tf_op jit(solution)/shard_map/ppermute | solution.py:37
  60.3 2.1 collective-permute-start.14
  69.9 14.7 %collective-permute-start.15 = (bf16[256,768]{1,0:T(8,128)(2,1)S(1)}, bf16[256,768]{1,0:T(8,128)(2,1)S(1)}, u32[]{:S(2)}, u32[]{:S(2)}) collective-permute-start(bf16[256,768]{1,0:T(8,128)(2,1)S(1)} %get-tuple-element.100.rows_ref), channel_id=1, source_target_pairs={{0,1},{1,0},{2,3},{3,2},{4,5},{5,4},{6,7},{7,6},{8,9},{9,8},{10,11... | collective-permute-start | bytes 1179656 | tf_op jit(solution)/shard_map/ppermute | solution.py:42
  96.9 10.9 %collective-permute-start.16 = (bf16[256,768]{1,0:T(8,128)(2,1)S(1)}, bf16[256,768]{1,0:T(8,128)(2,1)S(1)}, u32[]{:S(2)}, u32[]{:S(2)}) collective-permute-start(bf16[256,768]{1,0:T(8,128)(2,1)S(1)} %get-tuple-element.104), channel_id=1, source_target_pairs={{0,1},{1,0},{2,3},{3,2},{4,5},{5,4},{6,7},{7,6},{8,9},{9,8},{10,11... | collective-permute-start | bytes 1179656 | tf_op jit(solution)/shard_map/ppermute | solution.py:42
  107.8 12.1 %collective-permute-start.19 = (bf16[2,768,768]{2,1,0:T(8,128)(2,1)S(1)}, bf16[2,768,768]{2,1,0:T(8,128)(2,1)S(1)}, u32[]{:S(2)}, u32[]{:S(2)}) collective-permute-start(bf16[2,768,768]{2,1,0:T(8,128)(2,1)S(1)} %get-tuple-element.130), channel_id=1, source_target_pairs={{0,8},{8,0},{16,24},{24,16},{1,9},{9,1},{17,25},{25,17},{2,10},{10... | collective-permute-start | bytes 7077896 | tf_op jit(solution)/shard_map/ppermute | solution.py:37
  107.8 12.1 %collective-permute-start.18 = (bf16[4,768,384]{2,1,0:T(8,128)(2,1)S(1)}, bf16[4,768,384]{2,1,0:T(8,128)(2,1)S(1)}, u32[]{:S(2)}, u32[]{:S(2)}) collective-permute-start(bf16[4,768,384]{2,1,0:T(8,128)(2,1)S(1)} %get-tuple-element.127), channel_id=1, source_target_pairs={{0,8},{8,0},{16,24},{24,16},{1,9},{9,1},{17,25},{25,17},{2,10},{10... | collective-permute-start | bytes 7077896 | tf_op jit(solution)/shard_map/ppermute | solution.py:37
  119.8 17.0 %collective-permute-start.17 = (bf16[2,768,768]{2,1,0:T(8,128)(2,1)}, bf16[2,768,768]{2,1,0:T(8,128)(2,1)}, u32[]{:S(2)}, u32[]{:S(2)}) collective-permute-start(bf16[2,768,768]{2,1,0:T(8,128)(2,1)} %get-tuple-element.110), channel_id=1, source_target_pairs={{0,8},{8,0},{16,24},{24,16},{1,9},{9,1},{17,25},{25,17},{2,10},{10... | collective-permute-start | bytes 7077896 | tf_op jit(solution)/shard_map/ppermute | solution.py:37
  122.9 20.3 %collective-permute-start.21 = (bf16[4,192,384]{2,1,0:T(8,128)(2,1)}, bf16[4,192,384]{2,1,0:T(8,128)(2,1)}, u32[]{:S(2)}, u32[]{:S(2)}) collective-permute-start(bf16[4,192,384]{2,1,0:T(8,128)(2,1)} %get-tuple-element.142), channel_id=1, source_target_pairs={{0,16},{8,24},{16,0},{24,8},{1,17},{9,25},{17,1},{25,9},{2,18},{10... | collective-permute-start | bytes 1769480 | tf_op jit(solution)/shard_map/ppermute | solution.py:37
  132.8 13.6 %collective-permute-start.22 = (bf16[2,192,384]{2,1,0:T(8,128)(2,1)}, bf16[2,192,384]{2,1,0:T(8,128)(2,1)S(1)}, u32[]{:S(2)}, u32[]{:S(2)}) collective-permute-start(bf16[2,192,384]{2,1,0:T(8,128)(2,1)} %copy-done.55), channel_id=1, source_target_pairs={{0,2},{2,4},{4,6},{6,0},{1,3},{3,5},{5,7},{7,1},{8,10},{10,12},{12... | collective-permute-start | bytes 884744 | tf_op jit(solution)/shard_map/ppermute | solution.py:42
  132.9 23.7 %collective-permute-start.23 = (bf16[2,192,384]{2,1,0:T(8,128)(2,1)}, bf16[2,192,384]{2,1,0:T(8,128)(2,1)S(1)}, u32[]{:S(2)}, u32[]{:S(2)}) collective-permute-start(bf16[2,192,384]{2,1,0:T(8,128)(2,1)} %copy-done.54), channel_id=1, source_target_pairs={{0,4},{2,6},{4,0},{6,2},{1,5},{3,7},{5,1},{7,3},{8,12},{10,14},{12... | collective-permute-start | bytes 884744 | tf_op jit(solution)/shard_map/ppermute | solution.py:42
  135.2 21.4 %collective-permute-start.24 = (bf16[2,192,384]{2,1,0:T(8,128)(2,1)}, bf16[2,192,384]{2,1,0:T(8,128)(2,1)S(1)}, u32[]{:S(2)}, u32[]{:S(2)}) collective-permute-start(bf16[2,192,384]{2,1,0:T(8,128)(2,1)} %copy-done.53), channel_id=1, source_target_pairs={{0,6},{2,0},{4,2},{6,4},{1,7},{3,1},{5,3},{7,5},{8,14},{10,8},{12,... | collective-permute-start | bytes 884744 | tf_op jit(solution)/shard_map/ppermute | solution.py:42
  136.8 1.5 collective-permute-start.20
  142.9 33.9 %collective-permute-start.26 = (bf16[2,4,112,768]{3,2,1,0:T(8,128)(2,1)}, bf16[2,4,112,768]{3,2,1,0:T(8,128)(2,1)S(1)}, u32[]{:S(2)}, u32[]{:S(2)}) collective-permute-start(bf16[2,4,112,768]{3,2,1,0:T(8,128)(2,1)} %get-tuple-element.140), channel_id=1, source_target_pairs={{0,1},{1,0},{2,3},{3,2},{4,5},{5,4},{6,7},{7,6},{8,9},{9,8},{10,11... | collective-permute-start | bytes 4128776 | tf_op jit(solution)/shard_map/ppermute | solution.py:42
  145.2 28.0 %collective-permute-start.25 = (bf16[4,192,768]{2,1,0:T(8,128)(2,1)}, bf16[4,192,768]{2,1,0:T(8,128)(2,1)}, u32[]{:S(2)}, u32[]{:S(2)}) collective-permute-start(bf16[4,192,768]{2,1,0:T(8,128)(2,1)} %get-tuple-element.149), channel_id=1, source_target_pairs={{0,16},{8,24},{16,0},{24,8},{1,17},{9,25},{17,1},{25,9},{2,18},{10... | collective-permute-start | bytes 3538952 | tf_op jit(solution)/shard_map/ppermute | solution.py:37
  157.4 42.0 %all-to-all-start = ((bf16[4,192,384]{2,1,0:T(8,128)(2,1)}), bf16[4,192,384]{2,1,0:T(8,128)(2,1)S(1)}, u32[]{:S(2)}, u32[]{:S(2)}) async-start(bf16[4,192,384]{2,1,0:T(8,128)(2,1)} %shard_map.241), calls=%async_computation | async-start | bytes 1179648 | tf_op jit(solution)/shard_map/all_to_all | solution.py:767
  176.8 22.0 %copy-start.29 = (bf16[192,768]{1,0:T(8,128)(2,1)}, bf16[192,768]{1,0:T(8,128)(2,1)S(1)}, u32[]{:S(2)}) copy-start(bf16[192,768]{1,0:T(8,128)(2,1)S(1)} %get-tuple-element.159.refs_0_) | copy-start | bytes 884740
  178.5 23.8 %collective-permute-start.29 = (bf16[4,112,768]{2,1,0:T(8,128)(2,1)}, bf16[4,112,768]{2,1,0:T(8,128)(2,1)S(1)}, u32[]{:S(2)}, u32[]{:S(2)}) collective-permute-start(bf16[4,112,768]{2,1,0:T(8,128)(2,1)} %get-tuple-element.158), channel_id=1, source_target_pairs={{0,16},{8,24},{16,0},{24,8},{1,17},{9,25},{17,1},{25,9},{2,18},{10... | collective-permute-start | bytes 2064392 | tf_op jit(solution)/shard_map/ppermute | solution.py:37
  179.7 18.4 %collective-permute-start.28 = (bf16[192,384]{1,0:T(8,128)(2,1)S(1)}, bf16[192,384]{1,0:T(8,128)(2,1)S(1)}, u32[]{:S(2)}, u32[]{:S(2)}) collective-permute-start(bf16[192,384]{1,0:T(8,128)(2,1)S(1)} %slice_bitcast_fusion), channel_id=1, source_target_pairs={{0,16},{8,24},{16,0},{24,8},{1,17},{9,25},{17,1},{25,9},{2,18},{10... | collective-permute-start | bytes 442376 | tf_op jit(solution)/shard_map/ppermute | solution.py:37
  180.6 28.2 %collective-permute-start.27 = (bf16[256,768]{1,0:T(8,128)(2,1)}, bf16[256,768]{1,0:T(8,128)(2,1)}, u32[]{:S(2)}, u32[]{:S(2)}) collective-permute-start(bf16[256,768]{1,0:T(8,128)(2,1)} %get-tuple-element.153), channel_id=1, source_target_pairs={{0,1},{1,0},{2,3},{3,2},{4,5},{5,4},{6,7},{7,6},{8,9},{9,8},{10,11... | collective-permute-start | bytes 1179656 | tf_op jit(solution)/shard_map/ppermute | solution.py:42
  182.3 26.4 %collective-permute-start.30 = (bf16[192,768]{1,0:T(8,128)(2,1)}, bf16[192,768]{1,0:T(8,128)(2,1)}, u32[]{:S(2)}, u32[]{:S(2)}) collective-permute-start(bf16[192,768]{1,0:T(8,128)(2,1)} %get-tuple-element.160), channel_id=1, source_target_pairs={{0,2},{2,4},{4,6},{6,0},{1,3},{3,5},{5,7},{7,1},{8,10},{10,12},{12... | collective-permute-start | bytes 884744 | tf_op jit(solution)/shard_map/ppermute | solution.py:42
  182.9 25.9 %collective-permute-start.31 = (bf16[192,768]{1,0:T(8,128)(2,1)}, bf16[192,768]{1,0:T(8,128)(2,1)}, u32[]{:S(2)}, u32[]{:S(2)}) collective-permute-start(bf16[192,768]{1,0:T(8,128)(2,1)} %get-tuple-element.161), channel_id=1, source_target_pairs={{0,4},{2,6},{4,0},{6,2},{1,5},{3,7},{5,1},{7,3},{8,12},{10,14},{12... | collective-permute-start | bytes 884744 | tf_op jit(solution)/shard_map/ppermute | solution.py:42
  198.8 11.1 %collective-permute-start.32 = (bf16[192,768]{1,0:T(8,128)(2,1)}, bf16[192,768]{1,0:T(8,128)(2,1)}, u32[]{:S(2)}, u32[]{:S(2)}) collective-permute-start(bf16[192,768]{1,0:T(8,128)(2,1)} %get-tuple-element.162), channel_id=1, source_target_pairs={{0,6},{2,0},{4,2},{6,4},{1,7},{3,1},{5,3},{7,5},{8,14},{10,8},{12,... | collective-permute-start | bytes 884744 | tf_op jit(solution)/shard_map/ppermute | solution.py:42
  202.2 18.5 %copy-start.28 = (bf16[256,768]{1,0:T(8,128)(2,1)S(1)}, bf16[256,768]{1,0:T(8,128)(2,1)}, u32[]{:S(2)}) copy-start(bf16[256,768]{1,0:T(8,128)(2,1)} %copy-done.27) | copy-start | bytes 1179652
  202.2 18.5 %copy-start.61 = (pred[256]{0:T(512)(128)(4,1)S(1)}, pred[256]{0:T(512)(128)(4,1)}, u32[]{:S(2)}) copy-start(pred[256]{0:T(512)(128)(4,1)} %get-tuple-element.168) | copy-start | bytes 772
  203.2 24.4 %all-to-all-start.1 = ((bf16[4,112,768]{2,1,0:T(8,128)(2,1)}), bf16[4,112,768]{2,1,0:T(8,128)(2,1)S(1)}, u32[]{:S(2)}, u32[]{:S(2)}) async-start(bf16[4,112,768]{2,1,0:T(8,128)(2,1)} %shard_map.246), calls=%async_computation.1 | async-start | bytes 1376256 | tf_op jit(solution)/shard_map/all_to_all | solution.py:792
  207.5 7.5 %collective-permute-start.40 = (bf16[384,384]{1,0:T(8,128)(2,1)}, bf16[384,384]{1,0:T(8,128)(2,1)S(1)}, u32[]{:S(2)}, u32[]{:S(2)}) collective-permute-start(bf16[384,384]{1,0:T(8,128)(2,1)} %copy-done.31), channel_id=1, source_target_pairs={{0,16},{8,24},{16,0},{24,8},{1,17},{9,25},{17,1},{25,9},{2,18},{10... | collective-permute-start | bytes 884744 | tf_op jit(solution)/shard_map/ppermute | solution.py:37
  211.2 9.5 %collective-permute-start.37 = (bf16[192,768]{1,0:T(8,128)(2,1)S(1)}, bf16[192,768]{1,0:T(8,128)(2,1)S(1)}, u32[]{:S(2)}, u32[]{:S(2)}) collective-permute-start(bf16[192,768]{1,0:T(8,128)(2,1)S(1)} %shard_map.247.refs_0_), channel_id=1, source_target_pairs={{0,16},{8,24},{16,0},{24,8},{1,17},{9,25},{17,1},{25,9},{2,18},{10... | collective-permute-start | bytes 884744 | tf_op jit(solution)/shard_map/ppermute | solution.py:37
  212.5 10.2 %collective-permute-start.39 = (bf16[384,384]{1,0:T(8,128)(2,1)S(1)}, bf16[384,384]{1,0:T(8,128)(2,1)S(1)}, u32[]{:S(2)}, u32[]{:S(2)}) collective-permute-start(bf16[384,384]{1,0:T(8,128)(2,1)S(1)} %copy-done.32), channel_id=1, source_target_pairs={{0,8},{8,0},{16,24},{24,16},{1,9},{9,1},{17,25},{25,17},{2,10},{10... | collective-permute-start | bytes 884744 | tf_op jit(solution)/shard_map/ppermute | solution.py:37
  215.0 7.7 %collective-permute-start.41 = (bf16[384,384]{1,0:T(8,128)(2,1)S(1)}, bf16[384,384]{1,0:T(8,128)(2,1)}, u32[]{:S(2)}, u32[]{:S(2)}) collective-permute-start(bf16[384,384]{1,0:T(8,128)(2,1)S(1)} %collective-permute-done.40.refs_2_), channel_id=1, source_target_pairs={{0,8},{8,0},{16,24},{24,16},{1,9},{9,1},{17,25},{25,17},{2,10},{10... | collective-permute-start | bytes 884744 | tf_op jit(solution)/shard_map/ppermute | solution.py:37
  216.0 9.4 %collective-permute-start.36 = (bf16[192,768]{1,0:T(8,128)(2,1)S(1)}, bf16[192,768]{1,0:T(8,128)(2,1)S(1)}, u32[]{:S(2)}, u32[]{:S(2)}) collective-permute-start(bf16[192,768]{1,0:T(8,128)(2,1)S(1)} %shard_map.247.refs_0_), channel_id=1, source_target_pairs={{0,8},{8,0},{16,24},{24,16},{1,9},{9,1},{17,25},{25,17},{2,10},{10... | collective-permute-start | bytes 884744 | tf_op jit(solution)/shard_map/ppermute | solution.py:37
  220.8 4.7 %collective-permute-start.38 = (bf16[192,768]{1,0:T(8,128)(2,1)S(1)}, bf16[192,768]{1,0:T(8,128)(2,1)S(1)}, u32[]{:S(2)}, u32[]{:S(2)}) collective-permute-start(bf16[192,768]{1,0:T(8,128)(2,1)S(1)} %collective-permute-done.37.refs_2_), channel_id=1, source_target_pairs={{0,8},{8,0},{16,24},{24,16},{1,9},{9,1},{17,25},{25,17},{2,10},{10... | collective-permute-start | bytes 884744 | tf_op jit(solution)/shard_map/ppermute | solution.py:37
  227.8 6.3 %collective-permute-start.34 = (bf16[96,768]{1,0:T(8,128)(2,1)S(1)}, bf16[96,768]{1,0:T(8,128)(2,1)S(1)}, u32[]{:S(2)}, u32[]{:S(2)}) collective-permute-start(bf16[96,768]{1,0:T(8,128)(2,1)S(1)} %slice.72.refs_0_), channel_id=1, source_target_pairs={{0,16},{8,24},{16,0},{24,8},{1,17},{9,25},{17,1},{25,9},{2,18},{10... | collective-permute-start | bytes 442376 | tf_op jit(solution)/shard_map/ppermute | solution.py:37
  229.1 5.6 %collective-permute-start.33 = (bf16[96,768]{1,0:T(8,128)(2,1)S(1)}, bf16[96,768]{1,0:T(8,128)(2,1)S(1)}, u32[]{:S(2)}, u32[]{:S(2)}) collective-permute-start(bf16[96,768]{1,0:T(8,128)(2,1)S(1)} %slice.72.refs_0_), channel_id=1, source_target_pairs={{0,8},{8,0},{16,24},{24,16},{1,9},{9,1},{17,25},{25,17},{2,10},{10... | collective-permute-start | bytes 442376 | tf_op jit(solution)/shard_map/ppermute | solution.py:37
  234.1 1.4 collective-permute-start.35
  (58 other events, 331.7 us)

commit v2 on v1

--- a/solution.py
+++ b/solution.py
@@ -347,30 +347,27 @@
     return outs if count > 1 else outs[0]
 
 
-def core_add_kernel(place_ref, keep_ref, got_ref, small_ref, small_got_ref, send_ref, mine_ref):
-    blocks = send_ref.shape[1]
-    rows = keep_ref.shape[1] // (2 * blocks)
+def core_add_kernel(place_ref, keep_ref, got_ref, send_ref, mine_ref):
+    blocks, rows = send_ref.shape[1], send_ref.shape[2]
     me = place_ref[3]
-    for block in range(blocks):
-        small = [
-            (small_ref[2 * block + at].astype(F32) + small_got_ref[2 * block + at].astype(F32)).astype(BF16)
-            for at in range(2)
-        ]
-        for matrix in range(2):
+    for matrix in range(2):
+        for block in range(blocks):
             start = 2 * block * rows
             total = keep_ref[matrix, start : start + 2 * rows].astype(F32)
             total = (total + got_ref[matrix, start : start + 2 * rows].astype(F32)).astype(BF16)
             one, two = total[:rows], total[rows:]
-            mine_ref[matrix, block, :rows] = jnp.where(me == 0, one, two)
-            send_ref[matrix, block, :rows] = jnp.where(me == 0, two, one)
-            mine_ref[matrix, block, rows:] = jnp.where(me == 0, small[0], small[1])
-            send_ref[matrix, block, rows:] = jnp.where(me == 0, small[1], small[0])
-
-
-def pair_add_kernel(place_ref, keep_ref, got_ref, send_ref, mine_ref):
+            mine_ref[matrix, block] = jnp.where(me == 0, one, two)
+            send_ref[matrix, block] = jnp.where(me == 0, two, one)
+
+
+def pair_add_kernel(place_ref, keep_ref, got_ref, small_keep_ref, small_got_ref, send_ref, mine_ref):
     high = place_ref[0]
-    send_ref[...] = (keep_ref[1 - high].astype(F32) + got_ref[1 - high].astype(F32)).astype(BF16)
-    mine_ref[...] = (keep_ref[high].astype(F32) + got_ref[high].astype(F32)).astype(BF16)
+    rows = keep_ref.shape[2]
+    send_ref[:, :rows] = (keep_ref[1 - high].astype(F32) + got_ref[1 - high].astype(F32)).astype(BF16)
+    mine_ref[:, :rows] = (keep_ref[high].astype(F32) + got_ref[high].astype(F32)).astype(BF16)
+    small = (small_keep_ref[...].astype(F32) + small_got_ref[...].astype(F32)).astype(BF16)
+    send_ref[:, rows:] = small
+    mine_ref[:, rows:] = small
 
 
 def plain_add_kernel(one, two, out):
@@ -728,16 +725,34 @@
     first_got = rep_swap(after(first_send, second_got), 2)
     early_z = z_sent(early)
 
+    if expert_axis == 2:
+        cross = (2, dp_count, shard_rows, width)
+        y_send, y_keep = whole_call(
+            core_add_kernel, [(cross, BF16)] * 2, [place], [after(keep_part, early[0]), core_got], us=BIG
+        )
+        y_got = shift(y_send, "expert", 1)
+        token = y_send
+    else:
+        part = add_pair(after(keep_part, early[0]), core_got)
+        part = part.reshape(2, dp_count, expert_axis, shard_rows, width)
+        part = sum_over(part, "expert", 2)
+        token = part
+
     wide_onehot = jnp.pad(onehot, ((0, 0), (0, lanes - onehot.shape[1])))
     grad_tokens, small = whole_call(
         finish_kernel,
         [(flat, F32), ((2 + experts + head_count, width), F32)],
         [place],
         [tokens, gain_one, *qk_pieces, *vo_pieces, grad_q, grad_k, grad_v, grad_scores]
-        + [after(grad_res, early[0]), grad_gain_two, wide_onehot, turn_a, turn_b, logits_a, logits_b],
+        + [after(grad_res, token), grad_gain_two, wide_onehot, turn_a, turn_b, logits_a, logits_b],
         us=BIG,
     )
-
+    (second_blocks,) = whole_call(
+        plain_add_kernel, [(second_keep.shape, BF16)], [], [after(second_keep, grad_tokens), second_got], us=0
+    )
+    early_sum = add_arrays([after(early_z[0], second_blocks)] + early_z[1:], us=0)
+    early_got = rep_swap(early_sum[0], 2)
+    second_z = lax.all_to_all(after(second_blocks, early_sum), "dp", split_axis=0, concat_axis=0, tiled=True)
     if expert_axis == 2:
         shards = dp_count * expert_axis
         count = 2 + experts
@@ -747,35 +762,24 @@
         table = jnp.broadcast_to(small[count:].astype(BF16)[None], (shards, head_count, width))
         small = jnp.concatenate([split, table], axis=1)
         small = jnp.pad(small, ((0, 0), (0, small_rows - count - head_count), (0, 0)))
-        cross = (2, dp_count, shard_rows + small_rows, width)
-        y_send, y_keep = whole_call(
-            core_add_kernel, [(cross, BF16)] * 2, [place], [keep_part, core_got, small, rep_swap(small, 1)], us=0
-        )
-        y_got = shift(y_send, "expert", 1)
-        token = y_send
-    else:
-        part = add_pair(after(keep_part, grad_tokens), core_got)
-        part = part.reshape(2, dp_count, expert_axis, shard_rows, width)
-        part = sum_over(part, "expert", 2)
-        token = part
-
-    (second_blocks,) = whole_call(
-        plain_add_kernel, [(second_keep.shape, BF16)], [], [after(second_keep, token), second_got], us=0
-    )
-    early_sum = add_arrays([after(early_z[0], second_blocks)] + early_z[1:], us=BIG)
-    early_got = rep_swap(early_sum[0], 2)
-    second_z = lax.all_to_all(after(second_blocks, early_sum), "dp", split_axis=0, concat_axis=0, tiled=True)
-    first_z = z_sent(add_arrays([after(first_keep, early_sum), first_got], dp_count, us=BIG))
+        small = after(small, early_sum)
+        small = add_pair(small, rep_swap(small, 1)).reshape(dp_count, 2, small_rows, width)
+        small_got = shift(pick(small, 1 - me, 1), "expert", 1)
+        small_keep = pick(small, me, 1)
+    first_z = z_sent(add_arrays([after(first_keep, early_sum), first_got], dp_count, us=0))
     if expert_axis == 2:
         x_send, x_keep = whole_call(
-            pair_add_kernel, [(cross[1:], BF16)] * 2, [place], [after(y_keep, first_z[0]), y_got], us=0
+            pair_add_kernel,
+            [((dp_count, shard_rows + small_rows, width), BF16)] * 2,
+            [place],
+            [after(y_keep, first_z[0]), y_got, small_keep, small_got],
+            us=0,
         )
         x_got = rep_swap(x_send, 2)
         token = x_keep
     else:
         x_part = add_pair(pick(part, high, 0), rep_swap(pick(part, 1 - high, 0), 2))
         token = x_part
-    made_own, made_got = back(made_a, after(made_b, token))
     half_rows, half_columns = second_z.shape[1:]
     (second_sum,) = whole_call(
         second_sum_kernel,
@@ -787,18 +791,19 @@
     second_pieces = spread(second_sum)
     if expert_axis == 2:
         (x_sum,) = whole_call(
-            plain_add_kernel, [(cross[1:], BF16)], [], [after(x_keep, second_sum), x_got], us=0
+            plain_add_kernel, [(x_keep.shape, BF16)], [], [after(x_keep, second_sum), x_got], us=0
         )
         attn_z = lax.all_to_all(x_sum, "dp", split_axis=0, concat_axis=0, tiled=True)
         token = x_sum
+    made_own, made_got = back(made_a, after(made_b, token))
     (grad_w_out,) = whole_call(
         second_shared_kernel, [((1, inner // dp_count, width), F32)], [place], second_pieces
     )
-    first_sum = add_arrays([after(first_z[0], token, made_got)] + first_z[1:], us=0)
+    first_sum = add_arrays([after(first_z[0], token)] + first_z[1:], us=0)
     first_pieces = spread(first_sum)
     if expert_axis == 2:
         (attn_sum,) = whole_call(
-            sum_kernel, [(cross[2:], BF16)], [], [after(attn_z, first_sum)], us=0
+            sum_kernel, [(x_keep.shape[1:], BF16)], [], [after(attn_z, first_sum)], us=0
         )
         attn_pieces = spread(attn_sum[:shard_rows])
         small = attn_sum[shard_rows:].astype(F32)

time: 241 us -> 237 us (0.983)
  the two profiles are of different devices: /device:TPU:0 before, /device:TPU:15 now
where the time goes in v2:
time: 237 us; the launch traced here: 233 us
  Pallas kernels  70.3 us (30%)
  waiting for transfers between devices  61.1 us (26%)
  starting transfers between devices  57.3 us (24%)
  local copies, waits for them, and re-layouts  27.9 us (12%)
  other arithmetic  7.63 us (3%)
  matrix products  7.44 us (3%)
    pallas_call x21, Pallas kernels, whole_call(): pl.pallas_call(kernel, out_shape=[jax.ShapeDtypeStruct(s, d) for s, d in...  56.7 us
    ppermute x20, waiting for transfers between devices, shift(): lax.ppermute(values, axis, [(i, (i + step) % count) for i in range(count)])  35 us
    ppermute x23, starting transfers between devices, rep_swap(): return lax.ppermute(values, 'rep', [(i, i ^ bit) for i in range(count)])  32.9 us
    ppermute x23, waiting for transfers between devices, rep_swap(): return lax.ppermute(values, 'rep', [(i, i ^ bit) for i in range(count)])  26.1 us
    unnamed x99, local copies, waits for them, and re-layouts  24.8 us
    ppermute x20, starting transfers between devices, shift(): lax.ppermute(values, axis, [(i, (i + step) % count) for i in range(count)])  17.4 us
    pallas_call x2, Pallas kernels, run_expert(): pl.pallas_call(functools.partial(expert_kernel, experts), out_shape=[jax....  13.6 us
    dot_general x1, matrix products, mm_nt(): return lax.dot_general(one, two, NT, preferred_element_type=F32)  7.13 us
  transfers between devices with their start and end apart: 45, of which 15 were waited for; matrix products, arithmetic and copies ran while one was open for 7% of the time, Pallas kernels for 25%

profile of v2, /device:TPU:15, one launch (start us, length us, event | category | flops | bytes accessed | tf_op | source)
XLA Modules:
  0.0 233.3 jit_solution(12467018687608814737)
XLA Ops:
  3.9 4.1 %collective-permute-start.1 = (bf16[112,384]{1,0:T(8,128)(2,1)S(1)}, bf16[112,384]{1,0:T(8,128)(2,1)S(1)}, u32[]{:S(2)}, u32[]{:S(2)}) collective-permute-start(bf16[112,384]{1,0:T(8,128)(2,1)S(1)} %get-tuple-element.183), channel_id=1, source_target_pairs={{0,4},{2,6},{4,0},{6,2},{1,5},{3,7},{5,1},{7,3},{8,12},{10,14},{12... | collective-permute-start | bytes 258056 | tf_op jit(solution)/shard_map/ppermute | solution.py:42
  13.7 1.6 copy-done.46
  17.0 2.3 collective-permute-done.9
  19.7 4.4 %collective-permute-done.3.got_ref = bf16[4,112,384]{2,1,0:T(8,128)(2,1)S(1)} collective-permute-done((bf16[4,112,384]{2,1,0:T(8,128)(2,1)S(1)}, bf16[4,112,384]{2,1,0:T(8,128)(2,1)S(1)}, u32[]{:S(2)}, u32[]{:S(2)}) %collective-permute-start.3) | collective-permute-done | bytes 344096 | tf_op jit(solution)/shard_map/ppermute | solution.py:42
  25.8 4.5 %collective-permute-done.10.got_ref = bf16[4,96,384]{2,1,0:T(8,128)(2,1)S(1)} collective-permute-done((bf16[4,96,384]{2,1,0:T(8,128)(2,1)S(1)}, bf16[4,96,384]{2,1,0:T(8,128)(2,1)S(1)}, u32[]{:S(2)}, u32[]{:S(2)}) %collective-permute-start.10) | collective-permute-done | bytes 294944 | tf_op jit(solution)/shard_map/ppermute | solution.py:42
  31.2 3.3 %collective-permute-start.4 = (bf16[768,384]{1,0:T(8,128)(2,1)S(1)}, bf16[768,384]{1,0:T(8,128)(2,1)}, u32[]{:S(2)}, u32[]{:S(2)}) collective-permute-start(bf16[768,384]{1,0:T(8,128)(2,1)S(1)} %get-tuple-element.94.refs_0_), channel_id=1, source_target_pairs={{0,8},{8,0},{16,24},{24,16},{1,9},{9,1},{17,25},{25,17},{2,10},{10... | collective-permute-start | bytes 1769480 | tf_op jit(solution)/shard_map/ppermute | solution.py:37
  35.0 8.6 %collective-permute-start.6 = (bf16[768,384]{1,0:T(8,128)(2,1)}, bf16[768,384]{1,0:T(8,128)(2,1)S(1)}, u32[]{:S(2)}, u32[]{:S(2)}) collective-permute-start(bf16[768,384]{1,0:T(8,128)(2,1)} %collective-permute-done.5.refs_2_), channel_id=1, source_target_pairs={{0,8},{8,0},{16,24},{24,16},{1,9},{9,1},{17,25},{25,17},{2,10},{10... | collective-permute-start | bytes 1769480 | tf_op jit(solution)/shard_map/ppermute | solution.py:37
  43.7 7.1 %fusion.2.back_ref = bf16[512,3072]{1,0:T(8,128)(2,1)} fusion(bf16[1,3072,768]{2,1,0:T(8,128)(2,1)} %second_ref.3, bf16[256,768]{1,0:T(8,128)(2,1)S(1)} %collective-permute-done.13.cot_ref, bf16[256,768]{1,0:T(8,128)(2,1)S(1)} %get-tuple-element.178.cot_ref), kind=kOutput, calls=%fused_computation.2 | convolution fusion | flops 2419064832 | bytes 8650752 | tf_op jit(solution)/shard_map/dot_general | solution.py:70
  50.9 4.0 %shard_map.231 = (bf16[256,768]{1,0:T(8,128)(2,1)S(1)}, bf16[256,768]{1,0:T(8,128)(2,1)S(1)}, bf16[256,768]{1,0:T(8,128)(2,1)S(1)}, bf16[12,256,256]{2,1,0:T(8,128)(2,1)S(1)}) custom-call(s32[4]{0:T(128)S(1)} %pad_add_fusion.place_ref, bf16[256,768]{1,0:T(8,128)(2,1)S(1)} %copy-done.40, f32[1,768]{1,0:T(1,128)S(1)} %reshape.97.gain_ref, ...), custom_call_target="tpu_custom_call" | custom-call | flops 4000000000 | bytes 4000001 | tf_op jit(solution)/shard_map/pallas_call | solution.py:83
  58.0 1.4 collective-permute-done.14.refs_3_.refs_7_
  63.4 3.7 %shard_map.233 = (bf16[256,768]{1,0:T(8,128)(2,1)S(1)}, bf16[256,768]{1,0:T(8,128)(2,1)S(1)}, f32[256,768]{1,0:T(8,128)S(1)}, bf16[256,768]{1,0:T(8,128)(2,1)S(1)}, f32[256,1]{1,0:T(8,128)S(1)}) custom-call(s32[4]{0:T(128)S(1)} %pad_add_fusion.place_ref, bf16[256,768]{1,0:T(8,128)(2,1)S(1)} %copy-done.41, bf16[256,768]{1,0:T(8,128)(2,1)S(1)} %copy-done.14, ...), custom_call_target="tpu_custom_call" | custom-call | flops 4000000000 | bytes 4000001 | tf_op jit(solution)/shard_map/pallas_call | solution.py:83
  67.8 2.3 copy-done.31
  70.1 2.3 %copy-done.33 = bf16[1,3072,768]{2,1,0:T(8,128)(2,1)S(1)} copy-done((bf16[1,3072,768]{2,1,0:T(8,128)(2,1)S(1)}, bf16[1,3072,768]{2,1,0:T(8,128)(2,1)}, u32[]{:S(2)}) %copy-start.33) | copy-done | bytes 4718616
  72.4 6.7 %shard_map.234 = (bf16[256,3072]{1,0:T(8,128)(2,1)S(1)}, bf16[256,3072]{1,0:T(8,128)(2,1)S(1)}, bf16[256,768]{1,0:T(8,128)(2,1)S(1)}, bf16[256,768]{1,0:T(8,128)...) custom-call(s32[1]{0:T(128)} %bitcast.3.me_ref, ...), custom_call_target="tpu_custom_call" | custom-call | flops 9000000512 | bytes 9000001 | tf_op jit(solution)/shard_map/pallas_call | solution.py:260
  79.9 2.3 %copy-done.32 = bf16[1,768,3072]{2,1,0:T(8,128)(2,1)S(1)} copy-done((bf16[1,768,3072]{2,1,0:T(8,128)(2,1)S(1)}, bf16[1,768,3072]{2,1,0:T(8,128)(2,1)}, u32[]{:S(2)}) %copy-start.32) | copy-done | bytes 4718616
  82.3 2.3 %copy-done.34 = bf16[1,3072,768]{2,1,0:T(8,128)(2,1)S(1)} copy-done((bf16[1,3072,768]{2,1,0:T(8,128)(2,1)S(1)}, bf16[1,3072,768]{2,1,0:T(8,128)(2,1)}, u32[]{:S(2)}) %copy-start.34) | copy-done | bytes 4718616
  84.6 6.9 %shard_map.235 = (bf16[256,3072]{1,0:T(8,128)(2,1)S(1)}, bf16[256,3072]{1,0:T(8,128)(2,1)S(1)}, bf16[256,768]{1,0:T(8,128)(2,1)S(1)}, bf16[256,768]{1,0:T(8,128)...) custom-call(s32[1]{0:T(128)} %bitcast.3.me_ref, ...), custom_call_target="tpu_custom_call" | custom-call | flops 9000000512 | bytes 9000001 | tf_op jit(solution)/shard_map/pallas_call | solution.py:260
  91.5 1.5 collective-permute-start.16
  93.1 6.5 %shard_map.237 = (bf16[4,768,384]{2,1,0:T(8,128)(2,1)S(1)}, bf16[4,768,384]{2,1,0:T(8,128)(2,1)S(1)}, bf16[2,768,768]{2,1,0:T(8,128)(2,1)S(1)}, bf16[2,768,768]{2,1,0:T(8,128)(2,1)S(1)}) custom-call(s32[4]{0:T(128)S(1)} %pad_add_fusion.place_ref, bf16[768,256]{1,0:T(8,128)(2,1)S(1)} %get-tuple-element.112.refs_0_, ...), custom_call_target="tpu_custom_call" | custom-call | flops 30000001024 | bytes 30000000 | tf_op jit(solution)/shard_map/pallas_call | solution.py:83
  99.6 2.3 %collective-permute-done.16.got_ref = bf16[256,768]{1,0:T(8,128)(2,1)S(1)} collective-permute-done((bf16[256,768]{1,0:T(8,128)(2,1)S(1)}, bf16[256,768]{1,0:T(8,128)(2,1)S(1)}, u32[]{:S(2)}, u32[]{:S(2)}) %collective-permute-start.16) | collective-permute-done | bytes 393248 | tf_op jit(solution)/shard_map/ppermute | solution.py:42
  103.2 9.7 %shard_map.236 = (bf16[2,768,768]{2,1,0:T(8,128)(2,1)S(1)}, bf16[12,256,256]{2,1,0:T(8,128)(2,1)S(1)}, bf16[768,256]{1,0:T(8,128)(2,1)S(1)}, bf16[768,256]{1,0:T...) custom-call(s32[4]{0:T(128)S(1)} %pad_add_fusion.place_ref, ...), custom_call_target="tpu_custom_call" | custom-call | flops 1 | bytes 1 | tf_op jit(solution)/shard_map/pallas_call | solution.py:83
  113.6 2.8 %shard_map.238 = (bf16[2,192,384]{2,1,0:T(8,128)(2,1)S(1)}, bf16[2,192,384]{2,1,0:T(8,128)(2,1)}, bf16[2,192,384]{2,1,0:T(8,128)(2,1)}, bf16[2,192,384]{2,1,0:T(...) custom-call(s32[4]{0:T(128)S(1)} %pad_add_fusion.place_ref, ...), custom_call_target="tpu_custom_call" | custom-call | flops 1 | bytes 1 | tf_op jit(solution)/shard_map/pallas_call | solution.py:83
  117.7 2.2 shard_map.239
  120.9 1.5 collective-permute-start.25
  123.6 3.0 %collective-permute-start.22 = (bf16[2,192,384]{2,1,0:T(8,128)(2,1)}, bf16[2,192,384]{2,1,0:T(8,128)(2,1)}, u32[]{:S(2)}, u32[]{:S(2)}) collective-permute-start(bf16[2,192,384]{2,1,0:T(8,128)(2,1)} %get-tuple-element.148), channel_id=1, source_target_pairs={{0,4},{2,6},{4,0},{6,2},{1,5},{3,7},{5,1},{7,3},{8,12},{10,14},{12... | collective-permute-start | bytes 884744 | tf_op jit(solution)/shard_map/ppermute | solution.py:42
  126.6 4.9 %collective-permute-done.20.two = bf16[4,192,384]{2,1,0:T(8,128)(2,1)S(1)} collective-permute-done((bf16[4,192,384]{2,1,0:T(8,128)(2,1)S(1)}, bf16[4,192,384]{2,1,0:T(8,128)(2,1)S(1)}, u32[]{:S(2)}, u32[]{:S(2)}) %collective-permute-start.20) | collective-permute-done | bytes 589856 | tf_op jit(solution)/shard_map/ppermute | solution.py:37
  133.6 8.9 %shard_map.240 = (f32[256,768]{1,0:T(8,128)}, f32[16,768]{1,0:T(8,128)S(1)}) custom-call(s32[4]{0:T(128)S(1)} %pad_add_fusion.place_ref, bf16[256,768]{1,0:T(8,128)(2,1)S(1)} %copy-done.42, f32[1,768]{1,0:T(1,128)S(1)} %reshape.97.gain_ref, bf16[768,384]{1,0:T(8,128)(2,1)S(1)} %copy-done.37, bf16[768,384]{1,0:T(8,128)(2,1)} %collective-permute-done.4.refs_1_, ...), custom_call_target="tpu_custom_call" | custom-call | flops 30000001024 | bytes 30000000 | tf_op jit(solution)/shard_map/pallas_call | solution.py:83
  146.1 2.5 %collective-permute-done.22.refs_2_ = bf16[2,192,384]{2,1,0:T(8,128)(2,1)} collective-permute-done((bf16[2,192,384]{2,1,0:T(8,128)(2,1)}, bf16[2,192,384]{2,1,0:T(8,128)(2,1)}, u32[]{:S(2)}, u32[]{:S(2)}) %collective-permute-start.22) | collective-permute-done | bytes 294944 | tf_op jit(solution)/shard_map/ppermute | solution.py:42
  148.6 3.0 %collective-permute-done.23.refs_3_ = bf16[2,192,384]{2,1,0:T(8,128)(2,1)} collective-permute-done((bf16[2,192,384]{2,1,0:T(8,128)(2,1)}, bf16[2,192,384]{2,1,0:T(8,128)(2,1)}, u32[]{:S(2)}, u32[]{:S(2)}) %collective-permute-start.23) | collective-permute-done | bytes 294944 | tf_op jit(solution)/shard_map/ppermute | solution.py:42
  153.8 1.5 collective-permute-start.26
  155.2 3.5 %all-to-all-start = ((bf16[4,192,384]{2,1,0:T(8,128)(2,1)}), bf16[4,192,384]{2,1,0:T(8,128)(2,1)S(1)}, u32[]{:S(2)}, u32[]{:S(2)}) async-start(bf16[4,192,384]{2,1,0:T(8,128)(2,1)} %shard_map.241), calls=%async_computation | async-start | bytes 1179648 | tf_op jit(solution)/shard_map/all_to_all | solution.py:755
  159.9 2.2 shard_map.243
  162.2 2.1 collective-permute-done.27.small_got_ref
  164.3 2.4 %shard_map.244 = (bf16[4,112,768]{2,1,0:T(8,128)(2,1)}, bf16[4,112,768]{2,1,0:T(8,128)(2,1)S(1)}) custom-call(s32[4]{0:T(128)S(1)} %pad_add_fusion.place_ref, bf16[2,4,96,768]{3,2,1,0:T(8,128)(2,1)S(1)} %copy-done.4, bf16[2,4,96,768]{3,2,1,0:T(8,128)(2,1)} %collective-permute-done.25.got_ref, bf16[4,16,768]{2,1,0:T(8,128)(2,1)S(1)} %get-tuple-element.181.small_keep_ref, ...), custom_call_target="tpu_custom_call" | custom-call | flops 1 | bytes 1 | tf_op jit(solution)/shard_map/pallas_call | solution.py:83
  168.2 1.7 collective-permute-start.32
  170.4 15.9 %collective-permute-done.28.early_got = bf16[192,384]{1,0:T(8,128)(2,1)S(1)} collective-permute-done((bf16[192,384]{1,0:T(8,128)(2,1)S(1)}, bf16[192,384]{1,0:T(8,128)(2,1)S(1)}, u32[]{:S(2)}, u32[]{:S(2)}) %collective-permute-start.28) | collective-permute-done | bytes 147488 | tf_op jit(solution)/shard_map/ppermute | solution.py:37
  189.3 3.5 %all-to-all-start.1 = ((bf16[4,112,768]{2,1,0:T(8,128)(2,1)}), bf16[4,112,768]{2,1,0:T(8,128)(2,1)S(1)}, u32[]{:S(2)}, u32[]{:S(2)}) async-start(bf16[4,112,768]{2,1,0:T(8,128)(2,1)} %shard_map.246), calls=%async_computation.1 | async-start | bytes 1376256 | tf_op jit(solution)/shard_map/all_to_all | solution.py:796
  192.8 11.8 %collective-permute-done.32.refs_2_ = bf16[192,768]{1,0:T(8,128)(2,1)} collective-permute-done((bf16[192,768]{1,0:T(8,128)(2,1)}, bf16[192,768]{1,0:T(8,128)(2,1)}, u32[]{:S(2)}, u32[]{:S(2)}) %collective-permute-start.32) | collective-permute-done | bytes 294944 | tf_op jit(solution)/shard_map/ppermute | solution.py:42
  207.2 2.8 %collective-permute-start.40 = (bf16[384,384]{1,0:T(8,128)(2,1)}, bf16[384,384]{1,0:T(8,128)(2,1)S(1)}, u32[]{:S(2)}, u32[]{:S(2)}) collective-permute-start(bf16[384,384]{1,0:T(8,128)(2,1)} %shard_map.245.refs_0_), channel_id=1, source_target_pairs={{0,8},{8,0},{16,24},{24,16},{1,9},{9,1},{17,25},{25,17},{2,10},{10... | collective-permute-start | bytes 884744 | tf_op jit(solution)/shard_map/ppermute | solution.py:37
  210.6 2.0 collective-permute-done.38.refs_2_
  212.6 2.8 %collective-permute-start.39 = (bf16[192,768]{1,0:T(8,128)(2,1)S(1)}, bf16[192,768]{1,0:T(8,128)(2,1)S(1)}, u32[]{:S(2)}, u32[]{:S(2)}) collective-permute-start(bf16[192,768]{1,0:T(8,128)(2,1)S(1)} %collective-permute-done.38.refs_2_), channel_id=1, source_target_pairs={{0,8},{8,0},{16,24},{24,16},{1,9},{9,1},{17,25},{25,17},{2,10},{10... | collective-permute-start | bytes 884744 | tf_op jit(solution)/shard_map/ppermute | solution.py:37
  215.5 2.8 %shard_map.251 = f32[1,768,768]{2,1,0:T(8,128)} custom-call(s32[4]{0:T(128)S(1)} %pad_add_fusion.place_ref, bf16[384,384]{1,0:T(8,128)(2,1)} %shard_map.245.refs_0_, bf16[384,384]{1,0:T(8,128)(2,1)S(1)} %collective-permute-done.40.refs_1_, bf16[384,384]{1,0:T(8,128)(2,1)} %collective-permute-done.41.refs_2_, bf16[384,384]{1,0:T(8,128)(2,1)S(1)} %collective-permute-done.42.refs_3_), custom_call_target="tpu_custom_call" | custom-call | flops 2000000000 | bytes 2000001 | tf_op jit(solution)/shard_map/pallas_call | solution.py:83
  218.2 2.1 collective-permute-done.30
  221.3 2.3 shard_map.250
  223.8 1.5 collective-permute-start.34
  226.4 1.3 collective-permute-done.35.refs_2_
  227.8 2.5 %collective-permute-start.36 = (bf16[96,768]{1,0:T(8,128)(2,1)S(1)}, bf16[96,768]{1,0:T(8,128)(2,1)S(1)}, u32[]{:S(2)}, u32[]{:S(2)}) collective-permute-start(bf16[96,768]{1,0:T(8,128)(2,1)S(1)} %collective-permute-done.35.refs_2_), channel_id=1, source_target_pairs={{0,8},{8,0},{16,24},{24,16},{1,9},{9,1},{17,25},{25,17},{2,10},{10... | collective-permute-start | bytes 442376 | tf_op jit(solution)/shard_map/ppermute | solution.py:37
  231.3 1.6 shard_map.249
  (204 shorter events, 48.4 us)
Async XLA Ops:
  2.4 13.0 %collective-permute-start.2 = (bf16[112,384]{1,0:T(8,128)(2,1)S(1)}, bf16[112,384]{1,0:T(8,128)(2,1)S(1)}, u32[]{:S(2)}, u32[]{:S(2)}) collective-permute-start(bf16[112,384]{1,0:T(8,128)(2,1)S(1)} %get-tuple-element.183), channel_id=1, source_target_pairs={{0,6},{2,0},{4,2},{6,4},{1,7},{3,1},{5,3},{7,5},{8,14},{10,8},{12,... | collective-permute-start | bytes 258056 | tf_op jit(solution)/shard_map/ppermute | solution.py:42
  2.6 13.8 %collective-permute-start = (bf16[112,384]{1,0:T(8,128)(2,1)S(1)}, bf16[112,384]{1,0:T(8,128)(2,1)S(1)}, u32[]{:S(2)}, u32[]{:S(2)}) collective-permute-start(bf16[112,384]{1,0:T(8,128)(2,1)S(1)} %get-tuple-element.183), channel_id=1, source_target_pairs={{0,2},{2,4},{4,6},{6,0},{1,3},{3,5},{5,7},{7,1},{8,10},{10,12},{12... | collective-permute-start | bytes 258056 | tf_op jit(solution)/shard_map/ppermute | solution.py:42
  3.9 12.5 %collective-permute-start.1 = (bf16[112,384]{1,0:T(8,128)(2,1)S(1)}, bf16[112,384]{1,0:T(8,128)(2,1)S(1)}, u32[]{:S(2)}, u32[]{:S(2)}) collective-permute-start(bf16[112,384]{1,0:T(8,128)(2,1)S(1)} %get-tuple-element.183), channel_id=1, source_target_pairs={{0,4},{2,6},{4,0},{6,2},{1,5},{3,7},{5,1},{7,3},{8,12},{10,14},{12... | collective-permute-start | bytes 258056 | tf_op jit(solution)/shard_map/ppermute | solution.py:42
  8.9 8.1 %collective-permute-start.7 = (bf16[96,384]{1,0:T(8,128)(2,1)S(1)}, bf16[96,384]{1,0:T(8,128)(2,1)S(1)}, u32[]{:S(2)}, u32[]{:S(2)}) collective-permute-start(bf16[96,384]{1,0:T(8,128)(2,1)S(1)} %dynamic-slice_select_fusion), channel_id=1, source_target_pairs={{0,2},{2,4},{4,6},{6,0},{1,3},{3,5},{5,7},{7,1},{8,10},{10,12},{12... | collective-permute-start | bytes 221192 | tf_op jit(solution)/shard_map/ppermute | solution.py:42
  9.0 8.0 %collective-permute-start.8 = (bf16[96,384]{1,0:T(8,128)(2,1)S(1)}, bf16[96,384]{1,0:T(8,128)(2,1)S(1)}, u32[]{:S(2)}, u32[]{:S(2)}) collective-permute-start(bf16[96,384]{1,0:T(8,128)(2,1)S(1)} %dynamic-slice_select_fusion), channel_id=1, source_target_pairs={{0,4},{2,6},{4,0},{6,2},{1,5},{3,7},{5,1},{7,3},{8,12},{10,14},{12... | collective-permute-start | bytes 221192 | tf_op jit(solution)/shard_map/ppermute | solution.py:42
  15.4 3.9 %collective-permute-start.9 = (bf16[96,384]{1,0:T(8,128)(2,1)S(1)}, bf16[96,384]{1,0:T(8,128)(2,1)S(1)}, u32[]{:S(2)}, u32[]{:S(2)}) collective-permute-start(bf16[96,384]{1,0:T(8,128)(2,1)S(1)} %dynamic-slice_select_fusion), channel_id=1, source_target_pairs={{0,6},{2,0},{4,2},{6,4},{1,7},{3,1},{5,3},{7,5},{8,14},{10,8},{12,... | collective-permute-start | bytes 221192 | tf_op jit(solution)/shard_map/ppermute | solution.py:42
  16.5 7.5 %collective-permute-start.3 = (bf16[4,112,384]{2,1,0:T(8,128)(2,1)S(1)}, bf16[4,112,384]{2,1,0:T(8,128)(2,1)S(1)}, u32[]{:S(2)}, u32[]{:S(2)}) collective-permute-start(bf16[4,112,384]{2,1,0:T(8,128)(2,1)S(1)} %pad_maximum_fusion.own_ref), channel_id=1, source_target_pairs={{0,1},{1,0},{2,3},{3,2},{4,5},{5,4},{6,7},{7,6},{8,9},{9,8},{10,11... | collective-permute-start | bytes 1032200 | tf_op jit(solution)/shard_map/ppermute | solution.py:42
  19.4 11.0 %collective-permute-start.10 = (bf16[4,96,384]{2,1,0:T(8,128)(2,1)S(1)}, bf16[4,96,384]{2,1,0:T(8,128)(2,1)S(1)}, u32[]{:S(2)}, u32[]{:S(2)}) collective-permute-start(bf16[4,96,384]{2,1,0:T(8,128)(2,1)S(1)} %pad_maximum_fusion.1.own_ref), channel_id=1, source_target_pairs={{0,1},{1,0},{2,3},{3,2},{4,5},{5,4},{6,7},{7,6},{8,9},{9,8},{10,11... | collective-permute-start | bytes 884744 | tf_op jit(solution)/shard_map/ppermute | solution.py:42
  24.6 10.0 %collective-permute-start.5 = (bf16[768,384]{1,0:T(8,128)(2,1)S(1)}, bf16[768,384]{1,0:T(8,128)(2,1)}, u32[]{:S(2)}, u32[]{:S(2)}) collective-permute-start(bf16[768,384]{1,0:T(8,128)(2,1)S(1)} %get-tuple-element.94.refs_0_), channel_id=1, source_target_pairs={{0,16},{8,24},{16,0},{24,8},{1,17},{9,25},{17,1},{25,9},{2,18},{10... | collective-permute-start | bytes 1769480 | tf_op jit(solution)/shard_map/ppermute | solution.py:37
  25.8 25.0 %copy-start.20 = (bf16[256,768]{1,0:T(8,128)(2,1)}, bf16[256,768]{1,0:T(8,128)(2,1)S(1)}, u32[]{:S(2)}) copy-start(bf16[256,768]{1,0:T(8,128)(2,1)S(1)} %get-tuple-element.178.cot_ref) | copy-start | bytes 1179652
  30.3 13.3 %collective-permute-start.13 = (bf16[256,768]{1,0:T(8,128)(2,1)}, bf16[256,768]{1,0:T(8,128)(2,1)S(1)}, u32[]{:S(2)}, u32[]{:S(2)}) collective-permute-start(bf16[256,768]{1,0:T(8,128)(2,1)} %get-tuple-element.97), channel_id=1, source_target_pairs={{0,1},{1,0},{2,3},{3,2},{4,5},{5,4},{6,7},{7,6},{8,9},{9,8},{10,11... | collective-permute-start | bytes 1179656 | tf_op jit(solution)/shard_map/ppermute | solution.py:42
  31.2 19.6 %collective-permute-start.4 = (bf16[768,384]{1,0:T(8,128)(2,1)S(1)}, bf16[768,384]{1,0:T(8,128)(2,1)}, u32[]{:S(2)}, u32[]{:S(2)}) collective-permute-start(bf16[768,384]{1,0:T(8,128)(2,1)S(1)} %get-tuple-element.94.refs_0_), channel_id=1, source_target_pairs={{0,8},{8,0},{16,24},{24,16},{1,9},{9,1},{17,25},{25,17},{2,10},{10... | collective-permute-start | bytes 1769480 | tf_op jit(solution)/shard_map/ppermute | solution.py:37
  34.7 22.5 %collective-permute-start.12 = (bf16[768,384]{1,0:T(8,128)(2,1)S(1)}, bf16[768,384]{1,0:T(8,128)(2,1)S(1)}, u32[]{:S(2)}, u32[]{:S(2)}) collective-permute-start(bf16[768,384]{1,0:T(8,128)(2,1)S(1)} %shard_map.232.refs_0_.refs_4_), channel_id=1, source_target_pairs={{0,16},{8,24},{16,0},{24,8},{1,17},{9,25},{17,1},{25,9},{2,18},{10... | collective-permute-start | bytes 1769480 | tf_op jit(solution)/shard_map/ppermute | solution.py:37
  35.0 15.8 %collective-permute-start.6 = (bf16[768,384]{1,0:T(8,128)(2,1)}, bf16[768,384]{1,0:T(8,128)(2,1)S(1)}, u32[]{:S(2)}, u32[]{:S(2)}) collective-permute-start(bf16[768,384]{1,0:T(8,128)(2,1)} %collective-permute-done.5.refs_2_), channel_id=1, source_target_pairs={{0,8},{8,0},{16,24},{24,16},{1,9},{9,1},{17,25},{25,17},{2,10},{10... | collective-permute-start | bytes 1769480 | tf_op jit(solution)/shard_map/ppermute | solution.py:37
  50.8 7.2 %collective-permute-start.11 = (bf16[768,384]{1,0:T(8,128)(2,1)S(1)}, bf16[768,384]{1,0:T(8,128)(2,1)}, u32[]{:S(2)}, u32[]{:S(2)}) collective-permute-start(bf16[768,384]{1,0:T(8,128)(2,1)S(1)} %shard_map.232.refs_0_.refs_4_), channel_id=1, source_target_pairs={{0,8},{8,0},{16,24},{24,16},{1,9},{9,1},{17,25},{25,17},{2,10},{10... | collective-permute-start | bytes 1769480 | tf_op jit(solution)/shard_map/ppermute | solution.py:37
  57.2 2.2 collective-permute-start.14
  67.7 12.2 %collective-permute-start.15 = (bf16[256,768]{1,0:T(8,128)(2,1)S(1)}, bf16[256,768]{1,0:T(8,128)(2,1)S(1)}, u32[]{:S(2)}, u32[]{:S(2)}) collective-permute-start(bf16[256,768]{1,0:T(8,128)(2,1)S(1)} %get-tuple-element.102.rows_ref), channel_id=1, source_target_pairs={{0,1},{1,0},{2,3},{3,2},{4,5},{5,4},{6,7},{7,6},{8,9},{9,8},{10,11... | collective-permute-start | bytes 1179656 | tf_op jit(solution)/shard_map/ppermute | solution.py:42
  91.5 10.4 %collective-permute-start.16 = (bf16[256,768]{1,0:T(8,128)(2,1)S(1)}, bf16[256,768]{1,0:T(8,128)(2,1)S(1)}, u32[]{:S(2)}, u32[]{:S(2)}) collective-permute-start(bf16[256,768]{1,0:T(8,128)(2,1)S(1)} %get-tuple-element.106), channel_id=1, source_target_pairs={{0,1},{1,0},{2,3},{3,2},{4,5},{5,4},{6,7},{7,6},{8,9},{9,8},{10,11... | collective-permute-start | bytes 1179656 | tf_op jit(solution)/shard_map/ppermute | solution.py:42
  101.9 11.7 %collective-permute-start.18 = (bf16[2,768,768]{2,1,0:T(8,128)(2,1)S(1)}, bf16[2,768,768]{2,1,0:T(8,128)(2,1)S(1)}, u32[]{:S(2)}, u32[]{:S(2)}) collective-permute-start(bf16[2,768,768]{2,1,0:T(8,128)(2,1)S(1)} %get-tuple-element.127), channel_id=1, source_target_pairs={{0,8},{8,0},{16,24},{24,16},{1,9},{9,1},{17,25},{25,17},{2,10},{10... | collective-permute-start | bytes 7077896 | tf_op jit(solution)/shard_map/ppermute | solution.py:37
  103.1 10.5 %collective-permute-start.17 = (bf16[4,768,384]{2,1,0:T(8,128)(2,1)S(1)}, bf16[4,768,384]{2,1,0:T(8,128)(2,1)S(1)}, u32[]{:S(2)}, u32[]{:S(2)}) collective-permute-start(bf16[4,768,384]{2,1,0:T(8,128)(2,1)S(1)} %get-tuple-element.124), channel_id=1, source_target_pairs={{0,8},{8,0},{16,24},{24,16},{1,9},{9,1},{17,25},{25,17},{2,10},{10... | collective-permute-start | bytes 7077896 | tf_op jit(solution)/shard_map/ppermute | solution.py:37
  112.9 4.8 %collective-permute-start.19 = (bf16[2,768,768]{2,1,0:T(8,128)(2,1)S(1)}, bf16[2,768,768]{2,1,0:T(8,128)(2,1)S(1)}, u32[]{:S(2)}, u32[]{:S(2)}) collective-permute-start(bf16[2,768,768]{2,1,0:T(8,128)(2,1)S(1)} %get-tuple-element.130), channel_id=1, source_target_pairs={{0,8},{8,0},{16,24},{24,16},{1,9},{9,1},{17,25},{25,17},{2,10},{10... | collective-permute-start | bytes 7077896 | tf_op jit(solution)/shard_map/ppermute | solution.py:37
  116.4 17.2 %copy-start.42 = (bf16[256,768]{1,0:T(8,128)(2,1)S(1)}, bf16[256,768]{1,0:T(8,128)(2,1)}, u32[]{:S(2)}) copy-start(bf16[256,768]{1,0:T(8,128)(2,1)} %tokens_ref.5) | copy-start | bytes 1179652
  116.4 15.1 %collective-permute-start.20 = (bf16[4,192,384]{2,1,0:T(8,128)(2,1)S(1)}, bf16[4,192,384]{2,1,0:T(8,128)(2,1)S(1)}, u32[]{:S(2)}, u32[]{:S(2)}) collective-permute-start(bf16[4,192,384]{2,1,0:T(8,128)(2,1)S(1)} %get-tuple-element.145), channel_id=1, source_target_pairs={{0,16},{8,24},{16,0},{24,8},{1,17},{9,25},{17,1},{25,9},{2,18},{10... | collective-permute-start | bytes 1769480 | tf_op jit(solution)/shard_map/ppermute | solution.py:37
  120.9 43.4 %collective-permute-start.25 = (bf16[2,4,96,768]{3,2,1,0:T(8,128)(2,1)}, bf16[2,4,96,768]{3,2,1,0:T(8,128)(2,1)}, u32[]{:S(2)}, u32[]{:S(2)}) collective-permute-start(bf16[2,4,96,768]{3,2,1,0:T(8,128)(2,1)} %get-tuple-element.138), channel_id=1, source_target_pairs={{0,1},{1,0},{2,3},{3,2},{4,5},{5,4},{6,7},{7,6},{8,9},{9,8},{10,11... | collective-permute-start | bytes 3538952 | tf_op jit(solution)/shard_map/ppermute | solution.py:42
  122.4 23.1 %collective-permute-start.21 = (bf16[2,192,384]{2,1,0:T(8,128)(2,1)}, bf16[2,192,384]{2,1,0:T(8,128)(2,1)S(1)}, u32[]{:S(2)}, u32[]{:S(2)}) collective-permute-start(bf16[2,192,384]{2,1,0:T(8,128)(2,1)} %get-tuple-element.147), channel_id=1, source_target_pairs={{0,2},{2,4},{4,6},{6,0},{1,3},{3,5},{5,7},{7,1},{8,10},{10,12},{12... | collective-permute-start | bytes 884744 | tf_op jit(solution)/shard_map/ppermute | solution.py:42
  123.6 25.1 %collective-permute-start.22 = (bf16[2,192,384]{2,1,0:T(8,128)(2,1)}, bf16[2,192,384]{2,1,0:T(8,128)(2,1)}, u32[]{:S(2)}, u32[]{:S(2)}) collective-permute-start(bf16[2,192,384]{2,1,0:T(8,128)(2,1)} %get-tuple-element.148), channel_id=1, source_target_pairs={{0,4},{2,6},{4,0},{6,2},{1,5},{3,7},{5,1},{7,3},{8,12},{10,14},{12... | collective-permute-start | bytes 884744 | tf_op jit(solution)/shard_map/ppermute | solution.py:42
  126.6 25.0 %collective-permute-start.23 = (bf16[2,192,384]{2,1,0:T(8,128)(2,1)}, bf16[2,192,384]{2,1,0:T(8,128)(2,1)}, u32[]{:S(2)}, u32[]{:S(2)}) collective-permute-start(bf16[2,192,384]{2,1,0:T(8,128)(2,1)} %get-tuple-element.149), channel_id=1, source_target_pairs={{0,6},{2,0},{4,2},{6,4},{1,7},{3,1},{5,3},{7,5},{8,14},{10,8},{12,... | collective-permute-start | bytes 884744 | tf_op jit(solution)/shard_map/ppermute | solution.py:42
  132.4 27.5 %collective-permute-start.24 = (bf16[4,192,768]{2,1,0:T(8,128)(2,1)}, bf16[4,192,768]{2,1,0:T(8,128)(2,1)}, u32[]{:S(2)}, u32[]{:S(2)}) collective-permute-start(bf16[4,192,768]{2,1,0:T(8,128)(2,1)} %get-tuple-element.152), channel_id=1, source_target_pairs={{0,16},{8,24},{16,0},{24,8},{1,17},{9,25},{17,1},{25,9},{2,18},{10... | collective-permute-start | bytes 3538952 | tf_op jit(solution)/shard_map/ppermute | solution.py:37
  153.8 5.0 %collective-permute-start.26 = (bf16[8,16,768]{2,1,0:T(8,128)(2,1)}, bf16[8,16,768]{2,1,0:T(8,128)(2,1)S(1)}, u32[]{:S(2)}, u32[]{:S(2)}) collective-permute-start(bf16[8,16,768]{2,1,0:T(8,128)(2,1)} %fusion.9), channel_id=1, source_target_pairs={{0,8},{8,0},{16,24},{24,16},{1,9},{9,1},{17,25},{25,17},{2,10},{10... | collective-permute-start | bytes 589832 | tf_op jit(solution)/shard_map/ppermute | solution.py:37
  155.2 31.1 %all-to-all-start = ((bf16[4,192,384]{2,1,0:T(8,128)(2,1)}), bf16[4,192,384]{2,1,0:T(8,128)(2,1)S(1)}, u32[]{:S(2)}, u32[]{:S(2)}) async-start(bf16[4,192,384]{2,1,0:T(8,128)(2,1)} %shard_map.241), calls=%async_computation | async-start | bytes 1179648 | tf_op jit(solution)/shard_map/all_to_all | solution.py:755
  159.8 4.5 %collective-permute-start.27 = (bf16[4,16,768]{2,1,0:T(8,128)(2,1)S(1)}, bf16[4,16,768]{2,1,0:T(8,128)(2,1)S(1)}, u32[]{:S(2)}, u32[]{:S(2)}) collective-permute-start(bf16[4,16,768]{2,1,0:T(8,128)(2,1)S(1)} %get-tuple-element.180), channel_id=1, source_target_pairs={{0,1},{1,0},{2,3},{3,2},{4,5},{5,4},{6,7},{7,6},{8,9},{9,8},{10,11... | collective-permute-start | bytes 294920 | tf_op jit(solution)/shard_map/ppermute | solution.py:42
  166.6 21.7 %collective-permute-start.29 = (bf16[4,112,768]{2,1,0:T(8,128)(2,1)}, bf16[4,112,768]{2,1,0:T(8,128)(2,1)S(1)}, u32[]{:S(2)}, u32[]{:S(2)}) collective-permute-start(bf16[4,112,768]{2,1,0:T(8,128)(2,1)} %get-tuple-element.161), channel_id=1, source_target_pairs={{0,16},{8,24},{16,0},{24,8},{1,17},{9,25},{17,1},{25,9},{2,18},{10... | collective-permute-start | bytes 2064392 | tf_op jit(solution)/shard_map/ppermute | solution.py:37
  167.8 18.5 %collective-permute-start.28 = (bf16[192,384]{1,0:T(8,128)(2,1)S(1)}, bf16[192,384]{1,0:T(8,128)(2,1)S(1)}, u32[]{:S(2)}, u32[]{:S(2)}) collective-permute-start(bf16[192,384]{1,0:T(8,128)(2,1)S(1)} %slice_bitcast_fusion), channel_id=1, source_target_pairs={{0,16},{8,24},{16,0},{24,8},{1,17},{9,25},{17,1},{25,9},{2,18},{10... | collective-permute-start | bytes 442376 | tf_op jit(solution)/shard_map/ppermute | solution.py:37
  168.2 24.6 %collective-permute-start.31 = (bf16[192,768]{1,0:T(8,128)(2,1)}, bf16[192,768]{1,0:T(8,128)(2,1)}, u32[]{:S(2)}, u32[]{:S(2)}) collective-permute-start(bf16[192,768]{1,0:T(8,128)(2,1)} %get-tuple-element.164), channel_id=1, source_target_pairs={{0,2},{2,4},{4,6},{6,0},{1,3},{3,5},{5,7},{7,1},{8,10},{10,12},{12... | collective-permute-start | bytes 884744 | tf_op jit(solution)/shard_map/ppermute | solution.py:42
  168.2 36.5 %collective-permute-start.32 = (bf16[192,768]{1,0:T(8,128)(2,1)}, bf16[192,768]{1,0:T(8,128)(2,1)}, u32[]{:S(2)}, u32[]{:S(2)}) collective-permute-start(bf16[192,768]{1,0:T(8,128)(2,1)} %get-tuple-element.165), channel_id=1, source_target_pairs={{0,4},{2,6},{4,0},{6,2},{1,5},{3,7},{5,1},{7,3},{8,12},{10,14},{12... | collective-permute-start | bytes 884744 | tf_op jit(solution)/shard_map/ppermute | solution.py:42
  169.9 34.8 %collective-permute-start.33 = (bf16[192,768]{1,0:T(8,128)(2,1)}, bf16[192,768]{1,0:T(8,128)(2,1)}, u32[]{:S(2)}, u32[]{:S(2)}) collective-permute-start(bf16[192,768]{1,0:T(8,128)(2,1)} %get-tuple-element.166), channel_id=1, source_target_pairs={{0,6},{2,0},{4,2},{6,4},{1,7},{3,1},{5,3},{7,5},{8,14},{10,8},{12,... | collective-permute-start | bytes 884744 | tf_op jit(solution)/shard_map/ppermute | solution.py:42
  187.2 22.8 %copy-start.29 = (f32[256,1]{1,0:T(8,128)S(1)}, f32[256,1]{1,0:T(8,128)}, u32[]{:S(2)}) copy-start(f32[256,1]{1,0:T(8,128)} %copy-done.28) | copy-start | bytes 3076
  187.2 22.7 %collective-permute-start.41 = (bf16[384,384]{1,0:T(8,128)(2,1)}, bf16[384,384]{1,0:T(8,128)(2,1)}, u32[]{:S(2)}, u32[]{:S(2)}) collective-permute-start(bf16[384,384]{1,0:T(8,128)(2,1)} %shard_map.245.refs_0_), channel_id=1, source_target_pairs={{0,16},{8,24},{16,0},{24,8},{1,17},{9,25},{17,1},{25,9},{2,18},{10... | collective-permute-start | bytes 884744 | tf_op jit(solution)/shard_map/ppermute | solution.py:37
  189.3 34.3 %all-to-all-start.1 = ((bf16[4,112,768]{2,1,0:T(8,128)(2,1)}), bf16[4,112,768]{2,1,0:T(8,128)(2,1)S(1)}, u32[]{:S(2)}, u32[]{:S(2)}) async-start(bf16[4,112,768]{2,1,0:T(8,128)(2,1)} %shard_map.246), calls=%async_computation.1 | async-start | bytes 1376256 | tf_op jit(solution)/shard_map/all_to_all | solution.py:796
  206.0 6.7 %collective-permute-start.38 = (bf16[192,768]{1,0:T(8,128)(2,1)S(1)}, bf16[192,768]{1,0:T(8,128)(2,1)S(1)}, u32[]{:S(2)}, u32[]{:S(2)}) collective-permute-start(bf16[192,768]{1,0:T(8,128)(2,1)S(1)} %shard_map.247.refs_0_), channel_id=1, source_target_pairs={{0,16},{8,24},{16,0},{24,8},{1,17},{9,25},{17,1},{25,9},{2,18},{10... | collective-permute-start | bytes 884744 | tf_op jit(solution)/shard_map/ppermute | solution.py:37
  207.2 8.3 %collective-permute-start.40 = (bf16[384,384]{1,0:T(8,128)(2,1)}, bf16[384,384]{1,0:T(8,128)(2,1)S(1)}, u32[]{:S(2)}, u32[]{:S(2)}) collective-permute-start(bf16[384,384]{1,0:T(8,128)(2,1)} %shard_map.245.refs_0_), channel_id=1, source_target_pairs={{0,8},{8,0},{16,24},{24,16},{1,9},{9,1},{17,25},{25,17},{2,10},{10... | collective-permute-start | bytes 884744 | tf_op jit(solution)/shard_map/ppermute | solution.py:37
  209.9 5.5 %collective-permute-start.42 = (bf16[384,384]{1,0:T(8,128)(2,1)}, bf16[384,384]{1,0:T(8,128)(2,1)S(1)}, u32[]{:S(2)}, u32[]{:S(2)}) collective-permute-start(bf16[384,384]{1,0:T(8,128)(2,1)} %collective-permute-done.41.refs_2_), channel_id=1, source_target_pairs={{0,8},{8,0},{16,24},{24,16},{1,9},{9,1},{17,25},{25,17},{2,10},{10... | collective-permute-start | bytes 884744 | tf_op jit(solution)/shard_map/ppermute | solution.py:37
  209.9 10.4 %collective-permute-start.30 = (bf16[256,768]{1,0:T(8,128)(2,1)}, bf16[256,768]{1,0:T(8,128)(2,1)S(1)}, u32[]{:S(2)}, u32[]{:S(2)}) collective-permute-start(bf16[256,768]{1,0:T(8,128)(2,1)} %copy-done.43), channel_id=1, source_target_pairs={{0,1},{1,0},{2,3},{3,2},{4,5},{5,4},{6,7},{7,6},{8,9},{9,8},{10,11... | collective-permute-start | bytes 1179656 | tf_op jit(solution)/shard_map/ppermute | solution.py:42
  210.1 11.2 %collective-permute-start.37 = (bf16[192,768]{1,0:T(8,128)(2,1)S(1)}, bf16[192,768]{1,0:T(8,128)(2,1)S(1)}, u32[]{:S(2)}, u32[]{:S(2)}) collective-permute-start(bf16[192,768]{1,0:T(8,128)(2,1)S(1)} %shard_map.247.refs_0_), channel_id=1, source_target_pairs={{0,8},{8,0},{16,24},{24,16},{1,9},{9,1},{17,25},{25,17},{2,10},{10... | collective-permute-start | bytes 884744 | tf_op jit(solution)/shard_map/ppermute | solution.py:37
  212.6 8.7 %collective-permute-start.39 = (bf16[192,768]{1,0:T(8,128)(2,1)S(1)}, bf16[192,768]{1,0:T(8,128)(2,1)S(1)}, u32[]{:S(2)}, u32[]{:S(2)}) collective-permute-start(bf16[192,768]{1,0:T(8,128)(2,1)S(1)} %collective-permute-done.38.refs_2_), channel_id=1, source_target_pairs={{0,8},{8,0},{16,24},{24,16},{1,9},{9,1},{17,25},{25,17},{2,10},{10... | collective-permute-start | bytes 884744 | tf_op jit(solution)/shard_map/ppermute | solution.py:37
  223.7 4.1 %collective-permute-start.35 = (bf16[96,768]{1,0:T(8,128)(2,1)S(1)}, bf16[96,768]{1,0:T(8,128)(2,1)S(1)}, u32[]{:S(2)}, u32[]{:S(2)}) collective-permute-start(bf16[96,768]{1,0:T(8,128)(2,1)S(1)} %slice.72.refs_0_), channel_id=1, source_target_pairs={{0,16},{8,24},{16,0},{24,8},{1,17},{9,25},{17,1},{25,9},{2,18},{10... | collective-permute-start | bytes 442376 | tf_op jit(solution)/shard_map/ppermute | solution.py:37
  223.8 7.1 %collective-permute-start.34 = (bf16[96,768]{1,0:T(8,128)(2,1)S(1)}, bf16[96,768]{1,0:T(8,128)(2,1)S(1)}, u32[]{:S(2)}, u32[]{:S(2)}) collective-permute-start(bf16[96,768]{1,0:T(8,128)(2,1)S(1)} %slice.72.refs_0_), channel_id=1, source_target_pairs={{0,8},{8,0},{16,24},{24,16},{1,9},{9,1},{17,25},{25,17},{2,10},{10... | collective-permute-start | bytes 442376 | tf_op jit(solution)/shard_map/ppermute | solution.py:37
  227.8 3.5 %collective-permute-start.36 = (bf16[96,768]{1,0:T(8,128)(2,1)S(1)}, bf16[96,768]{1,0:T(8,128)(2,1)S(1)}, u32[]{:S(2)}, u32[]{:S(2)}) collective-permute-start(bf16[96,768]{1,0:T(8,128)(2,1)S(1)} %collective-permute-done.35.refs_2_), channel_id=1, source_target_pairs={{0,8},{8,0},{16,24},{24,16},{1,9},{9,1},{17,25},{25,17},{2,10},{10... | collective-permute-start | bytes 442376 | tf_op jit(solution)/shard_map/ppermute | solution.py:37
  (46 other events, 220.7 us)
